TPU v7x, 256 devices: a whole 4x4x8 slice. The times are simulated.
256 devices in a mesh: row: 16 (over z, core), col: 16 (over x, y).
Axes of the slice: x: 4, y: 4, z: 8, core: 2. Of those that a mesh axis runs over, the one named last changes fastest.
Arguments:
- observed: float32 [2, 4096, 4096], P(None, 'row', 'col'), may hold values from -6 to 6
- coherence_class: int32 [4096, 4096], P('row', 'col'), may hold values from 0 to 7
- class_weight: float32 [8], replicated, may hold values from 0.0002 to 0.003
- class_stiffness: float32 [8], replicated, may hold values from 0.5 to 4
Outputs:
- solution: float32 [2, 4096, 4096], P(None, 'row', 'col')
All inputs are finite; a program needn't handle non-finite values.
Results may differ from a plain program's by a relative error of at most 0.0003.
Values sent between devices are 32-bit elements; how exact they have to be, the bound alone decides.
No kernel may reach another device: no remote copies, remote signals or barrier semaphores. Data moves between devices by JAX's collectives and lax.ppermute only.
A program may use at most 320 MiB of HBM per device.

v0:
```python
import jax
import jax.numpy as jnp
from jax import lax
from jax.sharding import PartitionSpec as P

LEVELS = 5
CG_ITERS = 12


def extended(shard, sides, width):
    for axis, dim in sides:
        count, length = (lax.axis_size(axis), shard.shape[dim])
        up = [(i, (i + 1) % count) for i in range(count - 1)]
        down = [(j, i) for i, j in up]
        last = lax.slice_in_dim(shard, length - width, length, axis=dim)
        leading = lax.slice_in_dim(shard, 0, width, axis=dim)
        before = lax.ppermute(last, axis, up)
        after = lax.ppermute(leading, axis, down)
        shard = jnp.concatenate([before, shard, after], axis=dim)
    return shard


def lookup(classes, table):
    result = jnp.zeros(classes.shape, jnp.float32)
    for entry in range(table.shape[0]):
        result = jnp.where(classes == entry, table[entry], result)
    return result


def edge_terms(padded):
    centre = padded[1:-1, 1:-1]

    def single(other):
        return jnp.where(other > 0.0, 0.5 * (centre + other), 0.0)

    return (
        single(padded[:-2, 1:-1]),
        single(padded[2:, 1:-1]),
        single(padded[1:-1, :-2]),
        single(padded[1:-1, 2:]),
    )


def with_diag(weight, edges):
    return (edges, weight + edges[0] + edges[1] + edges[2] + edges[3])


def stiffness_padded(stiff):
    return extended(stiff, (("row", 0), ("col", 1)), 1)


def field_padded(field):
    return extended(field, (("row", 1), ("col", 2)), 1)


def local_padded(field):
    return jnp.pad(field, ((0, 0), (1, 1), (1, 1)))


def pull(padded, edges):
    north, south, west, east = edges
    total = north * padded[:, :-2, 1:-1] + south * padded[:, 2:, 1:-1]
    return total + west * padded[:, 1:-1, :-2] + east * padded[:, 1:-1, 2:]


def colour_mask(rows, cols):
    first = lax.broadcasted_iota(jnp.int32, (rows, cols), 0)
    second = lax.broadcasted_iota(jnp.int32, (rows, cols), 1)
    return (first + second) % 2 == 0


def relax(field, rhs, edges, diag, chosen, padder):
    fresh = (rhs + pull(padder(field), edges)) / diag
    return jnp.where(chosen, fresh, field)


def coarsen(field):
    shape = field.shape
    parts = field.reshape(shape[:-2] + (shape[-2] // 2, 2, shape[-1] // 2, 2))
    return jnp.sum(parts, axis=(-3, -1))


def level_down(rhs, weight, stiff, stiff_padder, padder, saved):
    edges, diag = with_diag(weight, edge_terms(stiff_padder(stiff)))
    red = colour_mask(weight.shape[0], weight.shape[1])
    field = jnp.where(red, rhs / diag, 0.0)
    field = relax(field, rhs, edges, diag, jnp.logical_not(red), padder)
    resid = rhs - (diag * field - pull(padder(field), edges))
    saved.append((field, rhs, edges, diag, red))
    return (coarsen(resid), coarsen(weight), 0.5 * coarsen(stiff))


def level_up(correction, entry, padder):
    field, rhs, edges, diag, red = entry
    field = field + jnp.repeat(jnp.repeat(correction, 2, axis=1), 2, axis=2)
    field = relax(field, rhs, edges, diag, red, padder)
    return relax(field, rhs, edges, diag, jnp.logical_not(red), padder)


def conjugate(rhs, edges, diag, padder, curvature_sum, norm_sum):
    solved = jnp.zeros_like(rhs)
    resid = rhs
    direction = rhs
    norm_now = norm_sum(jnp.sum(resid * resid, axis=(1, 2)))
    for step in range(CG_ITERS):
        image = diag * direction - pull(padder(direction), edges)
        alpha = norm_now / curvature_sum(jnp.sum(direction * image, axis=(1, 2)))
        solved = solved + alpha[:, None, None] * direction
        resid = resid - alpha[:, None, None] * image
        norm_next = norm_sum(jnp.sum(resid * resid, axis=(1, 2)))
        direction = resid + (norm_next / norm_now)[:, None, None] * direction
        norm_now = norm_next
    return solved


def same_value(value):
    return value


def own_share(whole, fields, rows, cols):
    row_start = lax.axis_index("row") * rows
    col_start = lax.axis_index("col") * cols
    return lax.dynamic_slice(whole, (jnp.int32(0), row_start, col_start), (fields, rows, cols))


def local(observed, coherence_class, class_weight, class_stiffness):
    weight = lookup(coherence_class, class_weight)
    stiff = lookup(coherence_class, class_stiffness)
    rhs = observed
    saved = []
    top = LEVELS
    for level in range(top):
        rhs, weight, stiff = level_down(rhs, weight, stiff, stiffness_padded, field_padded, saved)
    fields = rhs.shape[0]
    rows = rhs.shape[1]
    cols = rhs.shape[2]
    packed = jnp.concatenate([rhs, weight[None], stiff[None]], axis=0)
    packed = lax.all_gather(packed, "col", axis=2, tiled=True)
    packed = lax.all_gather(packed, "row", axis=1, tiled=True)
    whole_rhs = packed[:fields]
    whole_weight = packed[fields]
    whole_stiff = packed[fields + 1]
    edges, diag = with_diag(whole_weight, edge_terms(jnp.pad(whole_stiff, 1)))
    whole = conjugate(whole_rhs, edges, diag, local_padded, same_value, same_value)
    correction = own_share(whole, fields, rows, cols)
    for level in range(top - 1, -1, -1):
        correction = level_up(correction, saved[level], field_padded)
    return correction


def solution(mesh):
    in_specs = (P(None, "row", "col"), P("row", "col"), P(), P())
    out_specs = P(None, "row", "col")
    return jax.shard_map(local, mesh=mesh, in_specs=in_specs, out_specs=out_specs, check_vma=False)
```

profile of v0, /device:TPU:130, one launch (start us, length us, event | category | flops | bytes accessed | tf_op | source)
XLA Modules:
  0.0 688.3 jit_solution(5800917019795827602)
XLA Ops:
  1.6 6.9 select_select_fusion.1
  10.4 4.9 collective-permute-start.1
  15.3 18.1 %reshape.234 = f32[128,2,128,2]{3,2,1,0:T(8,128)} reshape(f32[256,256]{1,0:T(8,128)S(1)} %get-tuple-element.77) | data formatting | bytes 524288 | tf_op jit(solution)/shard_map/reshape | solution.py:79
  33.4 8.0 %reduce_sum.352 = f32[128,128]{1,0:T(8,128)S(1)} reduce(f32[128,2,128,2]{3,2,1,0:T(8,128)} %reshape.234, f32[]{:T(128)} %constant.49.clone.1), dimensions={1,3}, to_apply=%region_1.2 | reduce | flops 49152 | bytes 327684 | tf_op jit(solution)/shard_map/reduce_sum | solution.py:80
  43.9 4.9 collective-permute-start.13
  48.8 5.6 mul.627
  70.8 4.5 collective-permute-start.3
  77.8 6.5 add_add_fusion
  93.9 4.9 collective-permute-start.25
  101.4 6.2 collective-permute-start.7
  115.5 5.4 divide_select_fusion.2
  128.2 18.1 %reshape.235 = f32[128,2,128,2]{3,2,1,0:T(8,128)} reshape(f32[256,256]{1,0:T(8,128)S(1)} %get-tuple-element.73) | data formatting | bytes 524288 | tf_op jit(solution)/shard_map/reshape | solution.py:79
  146.2 8.0 %reduce_sum.353 = f32[128,128]{1,0:T(8,128)S(1)} reduce(f32[128,2,128,2]{3,2,1,0:T(8,128)} %reshape.235, f32[]{:T(128)} %constant.49.clone.1), dimensions={1,3}, to_apply=%region_2.3 | reduce | flops 49152 | bytes 327684 | tf_op jit(solution)/shard_map/reduce_sum | solution.py:80
  156.3 6.0 collective-permute-start.15
  172.4 4.6 fusion.19
  177.2 34.8 %reshape.233 = f32[2,128,2,128,2]{4,3,2,1,0:T(8,128)} reshape(f32[2,256,256]{2,1,0:T(8,128)S(1)} %copy.164) | data formatting | bytes 1048576 | tf_op jit(solution)/shard_map/reshape | solution.py:79
  212.1 13.4 %reduce_sum.351 = f32[2,128,128]{2,1,0:T(8,128)S(1)} reduce(f32[2,128,2,128,2]{4,3,2,1,0:T(8,128)} %reshape.233, f32[]{:T(128)} %constant.49.clone.1), dimensions={2,4}, to_apply=%region_0.1 | reduce | flops 98304 | bytes 655364 | tf_op jit(solution)/shard_map/reduce_sum | solution.py:80
  230.8 4.8 collective-permute-start.37
  244.6 5.4 collective-permute-done.18
  255.9 5.5 reshape.237
  266.2 6.0 collective-permute-start.27
  283.8 9.8 %reshape.236 = f32[2,64,2,64,2]{4,3,2,1,0:T(8,128)} reshape(f32[2,128,128]{2,1,0:T(8,128)S(1)} %fusion.166) | data formatting | bytes 262144 | tf_op jit(solution)/shard_map/reshape | solution.py:79
  293.6 4.5 reduce_sum.354
  303.2 4.9 collective-permute-start.49
  314.7 5.6 collective-permute-done.30
  328.1 6.0 collective-permute-start.39
  429.9 22.2 %all_gather.6 = f32[4,8,128]{1,0,2:T(4,128)S(1)} all-gather(f32[4,8,8]{1,0,2:T(4,128)S(1)} %copy.165), channel_id=1, replica_groups=mesh['row'=16,'col'=16] {'col'}, dimensions={2}, use_global_device_ids=true | all-gather | bytes 17408 | tf_op jit(solution)/shard_map/all_gather | solution.py:138
  452.1 15.1 %all_gather.7 = f32[4,128,128]{2,0,1:T(4,128)S(1)} all-gather(f32[4,8,128]{2,0,1:T(4,128)S(1)} %copy.166), channel_id=1, replica_groups=mesh['row'=16,'col'=16] {'row'}, dimensions={1}, use_global_device_ids=true | all-gather | bytes 278528 | tf_op jit(solution)/shard_map/all_gather | solution.py:139
  490.8 5.9 collective-permute-done.62
  642.3 5.0 collective-permute-done.92
  657.0 5.2 divide_select_fusion.1
  668.3 5.0 collective-permute-done.96
  (531 shorter events, 413.8 us)
Async XLA Ops:
  8.5 58.6 %collective-permute-start = (f32[1,256]{1,0:T(1,128)S(1)}, f32[1,256]{1,0:T(1,128)S(1)}, u32[]{:S(2)}, u32[]{:S(2)}) collective-permute-start(f32[1,256]{1,0:T(1,128)S(1)} %get-tuple-element.107), channel_id=1, source_target_pairs={{0,16},{16,32},{32,48},{48,64},{64,80},{80,96},{96,112},{112,128},... | collective-permute-start | bytes 3080 | tf_op jit(solution)/shard_map/ppermute | solution.py:17
  10.4 56.7 %collective-permute-start.1 = (f32[1,256]{1,0:T(1,128)S(1)}, f32[1,256]{1,0:T(1,128)S(1)}, u32[]{:S(2)}, u32[]{:S(2)}) collective-permute-start(f32[1,256]{1,0:T(1,128)S(1)} %get-tuple-element.106), channel_id=1, source_target_pairs={{16,0},{32,16},{48,32},{64,48},{80,64},{96,80},{112,96},{128,112},... | collective-permute-start | bytes 3080 | tf_op jit(solution)/shard_map/ppermute | solution.py:18
  42.0 59.4 %collective-permute-start.12 = (f32[1,128]{1,0:T(1,128)}, f32[1,128]{1,0:T(1,128)}, u32[]{:S(2)}, u32[]{:S(2)}) collective-permute-start(f32[1,128]{1,0:T(1,128)} %get-tuple-element.147), channel_id=1, source_target_pairs={{0,16},{16,32},{32,48},{48,64},{64,80},{80,96},{96,112},{112,128},... | collective-permute-start | bytes 1544 | tf_op jit(solution)/shard_map/ppermute | solution.py:17
  43.9 63.7 %collective-permute-start.13 = (f32[1,128]{1,0:T(1,128)}, f32[1,128]{1,0:T(1,128)}, u32[]{:S(2)}, u32[]{:S(2)}) collective-permute-start(f32[1,128]{1,0:T(1,128)} %get-tuple-element.146), channel_id=1, source_target_pairs={{16,0},{32,16},{48,32},{64,48},{80,64},{96,80},{112,96},{128,112},... | collective-permute-start | bytes 1544 | tf_op jit(solution)/shard_map/ppermute | solution.py:18
  57.7 180.0 %collective-permute-start.24 = (f32[1,64]{1,0:T(1,128)}, f32[1,64]{1,0:T(1,128)}, u32[]{:S(2)}, u32[]{:S(2)}) collective-permute-start(f32[1,64]{1,0:T(1,128)} %get-tuple-element.167), channel_id=1, source_target_pairs={{0,16},{16,32},{32,48},{48,64},{64,80},{80,96},{96,112},{112,128},... | collective-permute-start | bytes 776 | tf_op jit(solution)/shard_map/ppermute | solution.py:17
  67.3 9.0 %collective-permute-start.2 = (f32[258,1]{1,0:T(8,128)S(1)}, f32[258,1]{1,0:T(8,128)S(1)}, u32[]{:S(2)}, u32[]{:S(2)}) collective-permute-start(f32[258,1]{1,0:T(8,128)S(1)} %get-tuple-element.103), channel_id=1, source_target_pairs={{0,1},{1,2},{2,3},{3,4},{4,5},{5,6},{6,7},{7,8},{8,9},{9,10},{10,1... | collective-permute-start | bytes 3104 | tf_op jit(solution)/shard_map/ppermute | solution.py:17
  89.7 9.1 %collective-permute-start.4 = (f32[2,1,256]{1,0,2:T(2,128)}, f32[2,1,256]{1,0,2:T(2,128)S(1)}, u32[]{:S(2)}, u32[]{:S(2)}) collective-permute-start(f32[2,1,256]{1,0,2:T(2,128)} %get-tuple-element.100), channel_id=1, source_target_pairs={{0,16},{16,32},{32,48},{48,64},{64,80},{80,96},{96,112},{112,128},... | collective-permute-start | bytes 6152 | tf_op jit(solution)/shard_map/ppermute | solution.py:17
  93.9 147.1 %collective-permute-start.25 = (f32[1,64]{1,0:T(1,128)}, f32[1,64]{1,0:T(1,128)}, u32[]{:S(2)}, u32[]{:S(2)}) collective-permute-start(f32[1,64]{1,0:T(1,128)} %get-tuple-element.166), channel_id=1, source_target_pairs={{16,0},{32,16},{48,32},{64,48},{80,64},{96,80},{112,96},{128,112},... | collective-permute-start | bytes 776 | tf_op jit(solution)/shard_map/ppermute | solution.py:18
  98.8 213.1 %collective-permute-start.36 = (f32[1,32]{1,0:T(1,128)}, f32[1,32]{1,0:T(1,128)}, u32[]{:S(2)}, u32[]{:S(2)}) collective-permute-start(f32[1,32]{1,0:T(1,128)} %get-tuple-element.187), channel_id=1, source_target_pairs={{0,16},{16,32},{32,48},{48,64},{64,80},{80,96},{96,112},{112,128},... | collective-permute-start | bytes 392 | tf_op jit(solution)/shard_map/ppermute | solution.py:17
  101.4 9.9 %collective-permute-start.7 = (f32[2,258,1]{1,0,2:T(2,128)}, f32[2,258,1]{1,0,2:T(2,128)S(1)}, u32[]{:S(2)}, u32[]{:S(2)}) collective-permute-start(f32[2,258,1]{1,0,2:T(2,128)} %get-tuple-element.93), channel_id=1, source_target_pairs={{1,0},{2,1},{3,2},{4,3},{5,4},{6,5},{7,6},{8,7},{9,8},{10,9},{11,1... | collective-permute-start | bytes 6200 | tf_op jit(solution)/shard_map/ppermute | solution.py:18
  122.1 32.2 %collective-permute-start.9 = (f32[2,1,256]{1,0,2:T(2,128)}, f32[2,1,256]{1,0,2:T(2,128)S(1)}, u32[]{:S(2)}, u32[]{:S(2)}) collective-permute-start(f32[2,1,256]{1,0,2:T(2,128)} %get-tuple-element.99), channel_id=1, source_target_pairs={{16,0},{32,16},{48,32},{64,48},{80,64},{96,80},{112,96},{128,112},... | collective-permute-start | bytes 6152 | tf_op jit(solution)/shard_map/ppermute | solution.py:18
  125.5 30.7 %collective-permute-start.8 = (f32[2,1,256]{1,0,2:T(2,128)}, f32[2,1,256]{1,0,2:T(2,128)S(1)}, u32[]{:S(2)}, u32[]{:S(2)}) collective-permute-start(f32[2,1,256]{1,0,2:T(2,128)} %get-tuple-element.98), channel_id=1, source_target_pairs={{0,16},{16,32},{32,48},{48,64},{64,80},{80,96},{96,112},{112,128},... | collective-permute-start | bytes 6152 | tf_op jit(solution)/shard_map/ppermute | solution.py:17
  154.3 8.5 %collective-permute-start.14 = (f32[130,1]{1,0:T(8,128)}, f32[130,1]{1,0:T(8,128)S(1)}, u32[]{:S(2)}, u32[]{:S(2)}) collective-permute-start(f32[130,1]{1,0:T(8,128)} %get-tuple-element.137), channel_id=1, source_target_pairs={{0,1},{1,2},{2,3},{3,4},{4,5},{5,6},{6,7},{7,8},{8,9},{9,10},{10,1... | collective-permute-start | bytes 1568 | tf_op jit(solution)/shard_map/ppermute | solution.py:17
  156.3 8.5 %collective-permute-start.15 = (f32[130,1]{1,0:T(8,128)S(1)}, f32[130,1]{1,0:T(8,128)S(1)}, u32[]{:S(2)}, u32[]{:S(2)}) collective-permute-start(f32[130,1]{1,0:T(8,128)S(1)} %copy-done.53), channel_id=1, source_target_pairs={{1,0},{2,1},{3,2},{4,3},{5,4},{6,5},{7,6},{8,7},{9,8},{10,9},{11,1... | collective-permute-start | bytes 1568 | tf_op jit(solution)/shard_map/ppermute | solution.py:18
  230.8 83.2 %collective-permute-start.37 = (f32[1,32]{1,0:T(1,128)S(1)}, f32[1,32]{1,0:T(1,128)S(1)}, u32[]{:S(2)}, u32[]{:S(2)}) collective-permute-start(f32[1,32]{1,0:T(1,128)S(1)} %copy-done.56), channel_id=1, source_target_pairs={{16,0},{32,16},{48,32},{64,48},{80,64},{96,80},{112,96},{128,112},... | collective-permute-start | bytes 392 | tf_op jit(solution)/shard_map/ppermute | solution.py:18
  235.6 119.1 %collective-permute-start.48 = (f32[1,16]{1,0:T(1,128)}, f32[1,16]{1,0:T(1,128)}, u32[]{:S(2)}, u32[]{:S(2)}) collective-permute-start(f32[1,16]{1,0:T(1,128)} %get-tuple-element.191), channel_id=1, source_target_pairs={{0,16},{16,32},{32,48},{48,64},{64,80},{80,96},{96,112},{112,128},... | collective-permute-start | bytes 200 | tf_op jit(solution)/shard_map/ppermute | solution.py:17
  241.0 9.1 %collective-permute-start.18 = (f32[2,130,1]{2,1,0:T(8,128)S(1)}, f32[2,130,1]{2,1,0:T(8,128)S(1)}, u32[]{:S(2)}, u32[]{:S(2)}) collective-permute-start(f32[2,130,1]{2,1,0:T(8,128)S(1)} %get-tuple-element.114), channel_id=1, source_target_pairs={{0,1},{1,2},{2,3},{3,4},{4,5},{5,6},{6,7},{7,8},{8,9},{9,10},{10,1... | collective-permute-start | bytes 3128 | tf_op jit(solution)/shard_map/ppermute | solution.py:17
  250.3 14.0 %collective-permute-start.21 = (f32[2,1,128]{2,1,0:T(1,128)S(1)}, f32[2,1,128]{2,1,0:T(1,128)S(1)}, u32[]{:S(2)}, u32[]{:S(2)}) collective-permute-start(f32[2,1,128]{2,1,0:T(1,128)S(1)} %get-tuple-element.125), channel_id=1, source_target_pairs={{16,0},{32,16},{48,32},{64,48},{80,64},{96,80},{112,96},{128,112},... | collective-permute-start | bytes 3080 | tf_op jit(solution)/shard_map/ppermute | solution.py:18
  253.8 12.5 %collective-permute-start.20 = (f32[2,1,128]{2,1,0:T(1,128)S(1)}, f32[2,1,128]{2,1,0:T(1,128)S(1)}, u32[]{:S(2)}, u32[]{:S(2)}) collective-permute-start(f32[2,1,128]{2,1,0:T(1,128)S(1)} %get-tuple-element.124), channel_id=1, source_target_pairs={{0,16},{16,32},{32,48},{48,64},{64,80},{80,96},{96,112},{112,128},... | collective-permute-start | bytes 3080 | tf_op jit(solution)/shard_map/ppermute | solution.py:17
  274.3 9.3 %collective-permute-start.22 = (f32[2,130,1]{2,1,0:T(8,128)S(1)}, f32[2,130,1]{2,1,0:T(8,128)S(1)}, u32[]{:S(2)}, u32[]{:S(2)}) collective-permute-start(f32[2,130,1]{2,1,0:T(8,128)S(1)} %get-tuple-element.112), channel_id=1, source_target_pairs={{0,1},{1,2},{2,3},{3,4},{4,5},{5,6},{6,7},{7,8},{8,9},{9,10},{10,1... | collective-permute-start | bytes 3128 | tf_op jit(solution)/shard_map/ppermute | solution.py:17
  303.2 51.6 %collective-permute-start.49 = (f32[1,16]{1,0:T(1,128)}, f32[1,16]{1,0:T(1,128)}, u32[]{:S(2)}, u32[]{:S(2)}) collective-permute-start(f32[1,16]{1,0:T(1,128)} %get-tuple-element.190), channel_id=1, source_target_pairs={{16,0},{32,16},{48,32},{64,48},{80,64},{96,80},{112,96},{128,112},... | collective-permute-start | bytes 200 | tf_op jit(solution)/shard_map/ppermute | solution.py:18
  311.9 8.4 %collective-permute-start.30 = (f32[2,66,1]{2,1,0:T(8,128)S(1)}, f32[2,66,1]{2,1,0:T(8,128)S(1)}, u32[]{:S(2)}, u32[]{:S(2)}) collective-permute-start(f32[2,66,1]{2,1,0:T(8,128)S(1)} %get-tuple-element.134), channel_id=1, source_target_pairs={{0,1},{1,2},{2,3},{3,4},{4,5},{5,6},{6,7},{7,8},{8,9},{9,10},{10,1... | collective-permute-start | bytes 1592 | tf_op jit(solution)/shard_map/ppermute | solution.py:17
  322.4 11.8 %collective-permute-start.32 = (f32[2,1,64]{2,1,0:T(1,128)S(1)}, f32[2,1,64]{2,1,0:T(1,128)S(1)}, u32[]{:S(2)}, u32[]{:S(2)}) collective-permute-start(f32[2,1,64]{2,1,0:T(1,128)S(1)} %get-tuple-element.142), channel_id=1, source_target_pairs={{0,16},{16,32},{32,48},{48,64},{64,80},{80,96},{96,112},{112,128},... | collective-permute-start | bytes 1544 | tf_op jit(solution)/shard_map/ppermute | solution.py:17
  324.9 11.3 %collective-permute-start.38 = (f32[34,1]{1,0:T(8,128)S(1)}, f32[34,1]{1,0:T(8,128)S(1)}, u32[]{:S(2)}, u32[]{:S(2)}) collective-permute-start(f32[34,1]{1,0:T(8,128)S(1)} %get-tuple-element.177), channel_id=1, source_target_pairs={{0,1},{1,2},{2,3},{3,4},{4,5},{5,6},{6,7},{7,8},{8,9},{9,10},{10,1... | collective-permute-start | bytes 416 | tf_op jit(solution)/shard_map/ppermute | solution.py:17
  328.1 12.0 %collective-permute-start.39 = (f32[34,1]{1,0:T(8,128)S(1)}, f32[34,1]{1,0:T(8,128)S(1)}, u32[]{:S(2)}, u32[]{:S(2)}) collective-permute-start(f32[34,1]{1,0:T(8,128)S(1)} %get-tuple-element.176), channel_id=1, source_target_pairs={{1,0},{2,1},{3,2},{4,3},{5,4},{6,5},{7,6},{8,7},{9,8},{10,9},{11,1... | collective-permute-start | bytes 416 | tf_op jit(solution)/shard_map/ppermute | solution.py:18
  364.9 20.2 %collective-permute-start.50 = (f32[18,1]{1,0:T(8,128)S(1)}, f32[18,1]{1,0:T(8,128)S(1)}, u32[]{:S(2)}, u32[]{:S(2)}) collective-permute-start(f32[18,1]{1,0:T(8,128)S(1)} %get-tuple-element.189), channel_id=1, source_target_pairs={{0,1},{1,2},{2,3},{3,4},{4,5},{5,6},{6,7},{7,8},{8,9},{9,10},{10,1... | collective-permute-start | bytes 224 | tf_op jit(solution)/shard_map/ppermute | solution.py:17
  369.9 9.2 %collective-permute-start.45 = (f32[2,1,32]{2,1,0:T(1,128)S(1)}, f32[2,1,32]{2,1,0:T(1,128)S(1)}, u32[]{:S(2)}, u32[]{:S(2)}) collective-permute-start(f32[2,1,32]{2,1,0:T(1,128)S(1)} %get-tuple-element.163), channel_id=1, source_target_pairs={{16,0},{32,16},{48,32},{64,48},{80,64},{96,80},{112,96},{128,112},... | collective-permute-start | bytes 776 | tf_op jit(solution)/shard_map/ppermute | solution.py:18
  374.3 10.9 %collective-permute-start.51 = (f32[18,1]{1,0:T(8,128)S(1)}, f32[18,1]{1,0:T(8,128)S(1)}, u32[]{:S(2)}, u32[]{:S(2)}) collective-permute-start(f32[18,1]{1,0:T(8,128)S(1)} %get-tuple-element.188), channel_id=1, source_target_pairs={{1,0},{2,1},{3,2},{4,3},{5,4},{6,5},{7,6},{8,7},{9,8},{10,9},{11,1... | collective-permute-start | bytes 224 | tf_op jit(solution)/shard_map/ppermute | solution.py:18
  605.6 9.1 %collective-permute-start.86 = (f32[2,130,1]{2,1,0:T(8,128)S(1)}, f32[2,130,1]{2,1,0:T(8,128)S(1)}, u32[]{:S(2)}, u32[]{:S(2)}) collective-permute-start(f32[2,130,1]{2,1,0:T(8,128)S(1)} %get-tuple-element.110), channel_id=1, source_target_pairs={{0,1},{1,2},{2,3},{3,4},{4,5},{5,6},{6,7},{7,8},{8,9},{9,10},{10,1... | collective-permute-start | bytes 3128 | tf_op jit(solution)/shard_map/ppermute | solution.py:17
  625.7 9.1 %collective-permute-start.90 = (f32[2,130,1]{2,1,0:T(8,128)S(1)}, f32[2,130,1]{2,1,0:T(8,128)S(1)}, u32[]{:S(2)}, u32[]{:S(2)}) collective-permute-start(f32[2,130,1]{2,1,0:T(8,128)S(1)} %get-tuple-element.108), channel_id=1, source_target_pairs={{0,1},{1,2},{2,3},{3,4},{4,5},{5,6},{6,7},{7,8},{8,9},{9,10},{10,1... | collective-permute-start | bytes 3128 | tf_op jit(solution)/shard_map/ppermute | solution.py:17
  638.4 8.9 %collective-permute-start.92 = (f32[2,1,256]{1,0,2:T(2,128)S(1)}, f32[2,1,256]{1,0,2:T(2,128)S(1)}, u32[]{:S(2)}, u32[]{:S(2)}) collective-permute-start(f32[2,1,256]{1,0,2:T(2,128)S(1)} %get-tuple-element.96), channel_id=1, source_target_pairs={{0,16},{16,32},{32,48},{48,64},{64,80},{80,96},{96,112},{112,128},... | collective-permute-start | bytes 6152 | tf_op jit(solution)/shard_map/ppermute | solution.py:17
  664.4 8.9 %collective-permute-start.96 = (f32[2,1,256]{1,0,2:T(2,128)S(1)}, f32[2,1,256]{1,0,2:T(2,128)S(1)}, u32[]{:S(2)}, u32[]{:S(2)}) collective-permute-start(f32[2,1,256]{1,0,2:T(2,128)S(1)} %get-tuple-element.94), channel_id=1, source_target_pairs={{0,16},{16,32},{32,48},{48,64},{64,80},{80,96},{96,112},{112,128},... | collective-permute-start | bytes 6152 | tf_op jit(solution)/shard_map/ppermute | solution.py:17
  (125 other events, 4379.9 us)
where the time goes:
time: 700 us; the launch traced here: 688 us
  starting transfers between devices  284 us (41%)
  waiting for transfers between devices  139 us (20%)
  local copies, waits for them, and re-layouts  114 us (16%)
  other arithmetic  111 us (16%)
  blocking collectives  37.3 us (5%)
    ppermute x50, starting transfers between devices, extended(): after = lax.ppermute(leading, axis, down)  147 us
    ppermute x50, starting transfers between devices, extended(): before = lax.ppermute(last, axis, up)  136 us
    ppermute x50, waiting for transfers between devices, extended(): before = lax.ppermute(last, axis, up)  131 us
    reshape x11, local copies, waits for them, and re-layouts, coarsen(): parts = field.reshape(shape[:-2] + (shape[-2] // 2, 2, shape[-1] // 2, 2))  91.8 us
    reduce_sum x15, other arithmetic, coarsen(): return jnp.sum(parts, axis=(-3, -1))  41.6 us
    select_n x15, other arithmetic, relax(): return jnp.where(chosen, fresh, field)  24 us
    all_gather x1, blocking collectives, local(): packed = lax.all_gather(packed, 'col', axis=2, tiled=True)  22.2 us
    all_gather x1, blocking collectives, local(): packed = lax.all_gather(packed, 'row', axis=1, tiled=True)  15.1 us
  transfers between devices with their start and end apart: 100, of which 44 were waited for; matrix products, arithmetic and copies ran while one was open for 27% of the time, Pallas kernels for 0%

commit v1 on v0

v1 whole, which is shorter than its diff:
```python
import jax
import jax.numpy as jnp
from jax import lax
from jax.experimental import pallas as pl
from jax.experimental.pallas import tpu as pltpu
from jax.sharding import PartitionSpec as P

LEVELS = 5
CG_ITERS = 12
FAR = -1.0e4


def roll(x, shift, axis):
    return pltpu.roll(x, shift % x.shape[axis], axis)


def lane_bit(shape, level):
    lane = lax.broadcasted_iota(jnp.int32, shape, len(shape) - 1)
    return (lane >> level) % 2 == 0


def ends(ref, index, count):
    ref[index + (0,)] = roll(ref[index + (count,)], 1, 0)
    ref[index + (count + 1,)] = roll(ref[index + (1,)], -1, 0)


def loop(count, body, unroll):
    if count <= unroll:
        for i in range(count):
            body(i)
        return

    def step(i, carry):
        for j in range(unroll):
            body(i * unroll + j)
        return carry

    lax.fori_loop(0, count // unroll, step, 0)


def edges_at(a, level, gr, gb, even):
    step = 1 << level
    r, b = gr[a + 1], gb[a + 1]
    same = jnp.maximum(r + b, 0.0)
    red_other = jnp.maximum(r + jnp.where(even, gb[a], gb[a + 2]), 0.0)
    red_east = jnp.maximum(r + roll(b, -step, 1), 0.0)
    red_west = jnp.maximum(r + roll(b, step, 1), 0.0)
    black_other = jnp.maximum(b + jnp.where(even, gr[a + 2], gr[a]), 0.0)
    black_east = jnp.maximum(b + roll(r, -step, 1), 0.0)
    black_west = jnp.maximum(b + roll(r, step, 1), 0.0)
    return same, red_other, red_east, red_west, black_other, black_east, black_west


def make_edges(level, count, gr, gb, wr, wb, ke, inv, width, unroll):
    even = lane_bit((8, width), level)

    def body(a):
        k = edges_at(a, level, gr, gb, even)
        for i in range(7):
            ke[i, a] = k[i]
        inv[0, a] = 1.0 / jnp.maximum(wr[a] + k[0] + k[1] + k[2] + k[3], 1e-20)
        inv[1, a] = 1.0 / jnp.maximum(wb[a] + k[0] + k[4] + k[5] + k[6], 1e-20)

    loop(count, body, unroll)


def pull_red(a, level, f, black, ke, even):
    step = 1 << level
    b = black[f, a + 1]
    total = ke[0, a] * b + ke[1, a] * jnp.where(even, black[f, a], black[f, a + 2])
    return total + ke[2, a] * roll(b, -step, 1) + ke[3, a] * roll(b, step, 1)


def pull_black(a, level, f, red, ke, even):
    step = 1 << level
    r = red[f, a + 1]
    total = ke[0, a] * r + ke[4, a] * jnp.where(even, red[f, a + 2], red[f, a])
    return total + ke[5, a] * roll(r, -step, 1) + ke[6, a] * roll(r, step, 1)


def pair_sum(x, level, even):
    step = 1 << level
    return x + jnp.where(even, roll(x, -step, 1), roll(x, step, 1))


def lookup(table, index):
    parts = []
    for c in range(index.shape[1] // 128):
        parts.append(jnp.take_along_axis(table, index[:, c * 128 : (c + 1) * 128], axis=1))
    return jnp.concatenate(parts, axis=1)


def down_kernel(own, north, south, west, east, tables, *rest):
    rhs_s, blk_s, g_s, w_s = (rest[i * LEVELS : (i + 1) * LEVELS] for i in range(4))
    message = rest[4 * LEVELS]
    full, red, ke, inv, frame, arrived = rest[4 * LEVELS + 1 :]
    width = 512
    tab_g = jnp.broadcast_to(tables[0:1, :], (8, 128))
    tab_w = jnp.broadcast_to(tables[1:2, :], (8, 128))
    tiles = 64

    copies = []
    for source, at in ((north, 0), (own, 128), (south, 384)):
        for half in range(2):
            copies.append((source.at[:, :, pl.ds(half * 128, 128)], frame.at[:, 1 + half, pl.ds(at, source.shape[1]), :]))
    copies += [(west, frame.at[:, 0]), (east, frame.at[:, 3])]
    copies = [pltpu.make_async_copy(a, b, arrived.at[i]) for i, (a, b) in enumerate(copies)]
    for copy in copies:
        copy.start()
    for copy in copies:
        copy.wait()

    def frame_tile(f, a):
        return jnp.concatenate([frame[f, c, pl.ds(a, 8, stride=tiles), :] for c in range(4)], axis=1)

    for level in range(LEVELS):
        count = tiles // 2
        even = lane_bit((8, width), level)
        rhs, blk, g, w = rhs_s[level], blk_s[level], g_s[level], w_s[level]
        gr, gb = g.at[0], g.at[1]
        unroll = 2 if level == 0 else 4

        def pack(a, level=level, even=even, rhs=rhs, g=g, w=w):
            for f in range(2):
                if level == 0:
                    x, y = frame_tile(f, 2 * a), frame_tile(f, 2 * a + 1)
                else:
                    x, y = full[f, 2 * a], full[f, 2 * a + 1]
                rhs[f, a] = jnp.where(even, x, y)
                rhs[2 + f, a] = jnp.where(even, y, x)
            if level == 0:
                i, j = (frame_tile(2, 2 * a + k).astype(jnp.int32) for k in range(2))
                gx, gy, wx, wy = lookup(tab_g, i), lookup(tab_g, j), lookup(tab_w, i), lookup(tab_w, j)
            else:
                gx, gy, wx, wy = full[2, 2 * a], full[2, 2 * a + 1], full[3, 2 * a], full[3, 2 * a + 1]
            g[0, a + 1] = jnp.where(even, gx, gy)
            g[1, a + 1] = jnp.where(even, gy, gx)
            w[0, a] = jnp.where(even, wx, wy)
            w[1, a] = jnp.where(even, wy, wx)

        loop(count, pack, unroll)
        ends(g, (0,), count)
        ends(g, (1,), count)
        make_edges(level, count, gr, gb, w.at[0], w.at[1], ke, inv, width, unroll)

        def first_red(a, rhs=rhs):
            for f in range(2):
                red[f, a + 1] = rhs[f, a] * inv[0, a]

        loop(count, first_red, unroll)
        for f in range(2):
            ends(red, (f,), count)

        def first_black(a, level=level, even=even, rhs=rhs, blk=blk):
            for f in range(2):
                blk[f, a + 1] = (rhs[2 + f, a] + pull_black(a, level, f, red, ke, even)) * inv[1, a]

        loop(count, first_black, unroll)
        for f in range(2):
            ends(blk, (f,), count)

        def restrict(a, level=level, even=even, blk=blk, g=g, w=w):
            for f in range(2):
                full[f, a] = pair_sum(pull_red(a, level, f, blk, ke, even), level, even)
            full[2, a] = 0.5 * pair_sum(g[0, a + 1] + g[1, a + 1], level, even)
            full[3, a] = pair_sum(w[0, a] + w[1, a], level, even)

        loop(count, restrict, unroll)
        tiles = count

    lane = lax.broadcasted_iota(jnp.int32, (width, 128), 0)
    out = lax.broadcasted_iota(jnp.int32, (width, 128), 1)
    pick = jnp.where(lane == (4 + out % 8) * 32, 1.0, 0.0)
    place = lax.broadcasted_iota(jnp.int32, (8, 128), 1)
    sub = lax.broadcasted_iota(jnp.int32, (8, 128), 0)
    parts = [0.0, 0.0]
    for which in range(4):
        for a in range(2):
            spread = jnp.dot(full[which, a], pick, precision=lax.Precision.HIGHEST, preferred_element_type=jnp.float32)
            mine = (place // 8) == (which % 2) * 8 + (a + 2 * sub - 4)
            mine = jnp.logical_and(mine, jnp.logical_and(a + 2 * sub >= 4, a + 2 * sub < 12))
            parts[which // 2] += jnp.sum(jnp.where(mine, spread, 0.0), axis=0, keepdims=True)
    both = jnp.concatenate(parts * 4, axis=0)

    def send(i, carry):
        message[pl.ds(i * 8, 8), :] = both
        return carry

    lax.fori_loop(0, message.shape[0] // 8, send, 0)


def cg(gathered, kc, e, r, d, q):
    lane = lax.broadcasted_iota(jnp.int32, (8, 128), 1)
    sub = lax.broadcasted_iota(jnp.int32, (8, 128), 0)
    group = lane // 8
    arrays = [[None] * 16 for _ in range(4)]
    for hi in range(2):
        for pair in range(2):
            v = [gathered[pl.ds((hi * 128 + c) * 2 + pair, 8, stride=32), :] for c in range(16)]
            for k in (1, 2, 4, 8):
                low = (group // k) % 2 == 0
                for c in range(16):
                    if not c & k:
                        x, y = v[c], v[c | k]
                        v[c] = jnp.where(low, x, roll(y, 8 * k, 1))
                        v[c | k] = jnp.where(low, roll(x, -8 * k, 1), y)
            for i in range(16):
                arrays[2 * pair + i // 8][hi * 8 + i % 8] = v[i]

    def north(tile, t):
        if t % 8:
            return tile(t - 1)
        turned = roll(tile(t + 7), 1, 0)
        return turned if t == 0 else jnp.where(sub == 0, roll(tile(7), 1, 0), turned)

    def south(tile, t):
        if t % 8 != 7:
            return tile(t + 1)
        turned = roll(tile(t - 7), -1, 0)
        return turned if t == 15 else jnp.where(sub == 7, roll(tile(8), -1, 0), turned)

    g = arrays[2]
    for t in range(16):
        up = jnp.maximum(g[t] + north(lambda i: g[i], t), 0.0)
        down = jnp.maximum(g[t] + south(lambda i: g[i], t), 0.0)
        if t == 0:
            up = jnp.where(sub == 0, 0.0, up)
        if t == 15:
            down = jnp.where(sub == 7, 0.0, down)
        left = jnp.where(lane == 0, 0.0, jnp.maximum(g[t] + roll(g[t], 1, 1), 0.0))
        right = jnp.where(lane == 127, 0.0, jnp.maximum(g[t] + roll(g[t], -1, 1), 0.0))
        kc[0, t] = up
        kc[1, t] = down
        kc[2, t] = left
        kc[3, t] = right
        kc[4, t] = arrays[3][t] + up + down + left + right

    norm = []
    for f in range(2):
        total = 0.0
        for t in range(16):
            x = arrays[f][t]
            e[f, t] = jnp.zeros_like(x)
            r[f, t] = x
            d[f, t] = x
            total += x * x
        norm.append(jnp.sum(total, axis=(0, 1), keepdims=True))

    def iterate(_, norm):
        alpha = []
        for f in range(2):
            tile = lambda i, f=f: d[f, i]
            total = 0.0
            for t in range(16):
                x = d[f, t]
                image = kc[4, t] * x - (
                    kc[0, t] * north(tile, t)
                    + kc[1, t] * south(tile, t)
                    + kc[2, t] * roll(x, 1, 1)
                    + kc[3, t] * roll(x, -1, 1)
                )
                q[f, t] = image
                total += x * image
            alpha.append(norm[f] / jnp.sum(total, axis=(0, 1), keepdims=True))
        fresh = []
        for f in range(2):
            total = 0.0
            for t in range(16):
                e[f, t] = e[f, t] + alpha[f] * d[f, t]
                x = r[f, t] - alpha[f] * q[f, t]
                r[f, t] = x
                total += x * x
            fresh.append(jnp.sum(total, axis=(0, 1), keepdims=True))
        for f in range(2):
            beta = fresh[f] / norm[f]
            for t in range(16):
                d[f, t] = r[f, t] + beta * d[f, t]
        return tuple(fresh)

    lax.fori_loop(0, CG_ITERS, iterate, tuple(norm))


def up_kernel(place, gathered, *rest):
    rhs_s, blk_s, g_s, w_s = (rest[i * LEVELS : (i + 1) * LEVELS] for i in range(4))
    out = rest[4 * LEVELS]
    full, red, blk, ke, inv, kc, e, r, d, q, result, sent = rest[4 * LEVELS + 1 :]
    width = 512
    cg(gathered, kc, e, r, d, q)
    row0 = place[0] * 8 - 4
    col0 = place[1] * 8 - 4
    o = lax.broadcasted_iota(jnp.int32, (16, 128), 0)
    n = lax.broadcasted_iota(jnp.int32, (16, 128), 1)
    row = (n // 64) * 64 + (n % 8) * 8 + (n // 8) % 8
    rows = jnp.where(row == row0 + o // 8 + 2 * (o % 8), 1.0, 0.0)
    j = lax.broadcasted_iota(jnp.int32, (128, width), 0)
    lane = lax.broadcasted_iota(jnp.int32, (128, width), 1)
    cols = jnp.where(j == col0 + lane // 32, 1.0, 0.0)
    for f in range(2):
        whole = jnp.concatenate([e[f, t] for t in range(16)], axis=0)
        part = jnp.dot(rows, whole, precision=lax.Precision.HIGHEST, preferred_element_type=jnp.float32)
        part = jnp.dot(part, cols, precision=lax.Precision.HIGHEST, preferred_element_type=jnp.float32)
        full[f, 0] = part[0:8]
        full[f, 1] = part[8:16]

    for level in range(LEVELS - 1, -1, -1):
        count = 32 >> level
        even = lane_bit((8, width), level)
        rhs, old, g, w = rhs_s[level], blk_s[level], g_s[level], w_s[level]
        unroll = 2 if level == 0 else 4
        make_edges(level, count, g.at[0], g.at[1], w.at[0], w.at[1], ke, inv, width, unroll)

        def correct(a, old=old):
            for f in range(2):
                blk[f, a + 1] = old[f, a + 1] + full[f, a]

        loop(count, correct, unroll)
        for f in range(2):
            ends(blk, (f,), count)

        def second_red(a, level=level, even=even, rhs=rhs):
            for f in range(2):
                red[f, a + 1] = (rhs[f, a] + pull_red(a, level, f, blk, ke, even)) * inv[0, a]

        loop(count, second_red, unroll)
        for f in range(2):
            ends(red, (f,), count)

        def second_black(a, level=level, even=even, rhs=rhs):
            for f in range(2):
                x = red[f, a + 1]
                y = (rhs[2 + f, a] + pull_black(a, level, f, red, ke, even)) * inv[1, a]
                first, second = jnp.where(even, x, y), jnp.where(even, y, x)
                if level:
                    full[f, 2 * a] = first
                    full[f, 2 * a + 1] = second
                else:
                    for half in range(2):
                        lanes = slice(128 + 128 * half, 256 + 128 * half)
                        result[f, half, pl.ds(2 * a, 4, stride=64), :] = first[2:6, lanes]
                        result[f, half, pl.ds(2 * a + 1, 4, stride=64), :] = second[2:6, lanes]

        loop(count, second_black, unroll)

    copies = [pltpu.make_async_copy(result.at[:, i], out.at[:, :, pl.ds(i * 128, 128)], sent.at[i]) for i in range(2)]
    for copy in copies:
        copy.start()
    for copy in copies:
        copy.wait()


def level_shapes():
    shapes = []
    for build in (
        lambda n: (4, n, 8, 512),
        lambda n: (2, n + 2, 8, 512),
        lambda n: (2, n + 2, 8, 512),
        lambda n: (2, n, 8, 512),
    ):
        shapes += [build(32 >> level) for level in range(LEVELS)]
    return shapes


def send(x, axis, step):
    count = lax.axis_size(axis)
    return lax.ppermute(x, axis, [(i, i + step) for i in range(count) if 0 <= i + step < count])


def make_tables(class_weight, class_stiffness):
    pad = lambda x, first: jnp.pad(jnp.concatenate([jnp.full((1,), first, jnp.float32), x]), (0, 119))
    return jnp.stack([pad(0.5 * class_stiffness, FAR), pad(class_weight, 0.0)])


VMEM = pl.BlockSpec(memory_space=pltpu.VMEM)
ANY = pl.BlockSpec(memory_space=pl.ANY)
PARAMS = pltpu.CompilerParams(vmem_limit_bytes=56 * 1024 * 1024)


def down(own, north, south, west, east, tables):
    return pl.pallas_call(
        down_kernel,
        out_shape=[jax.ShapeDtypeStruct(s, jnp.float32) for s in level_shapes() + [(512, 128)]],
        in_specs=[ANY] * 5 + [VMEM],
        out_specs=[VMEM] * (4 * LEVELS + 1),
        scratch_shapes=[
            pltpu.VMEM((4, 32, 8, 512), jnp.float32),
            pltpu.VMEM((2, 34, 8, 512), jnp.float32),
            pltpu.VMEM((7, 32, 8, 512), jnp.float32),
            pltpu.VMEM((2, 32, 8, 512), jnp.float32),
            pltpu.VMEM((3, 4, 512, 128), jnp.float32),
            pltpu.SemaphoreType.DMA((8,)),
        ],
        compiler_params=PARAMS,
        name="down",
    )(own, north, south, west, east, tables)


def up(place, gathered, saved):
    grid = pltpu.VMEM((2, 16, 8, 128), jnp.float32)
    return pl.pallas_call(
        up_kernel,
        out_shape=jax.ShapeDtypeStruct((2, 256, 256), jnp.float32),
        in_specs=[pl.BlockSpec(memory_space=pltpu.SMEM)] + [VMEM] * (4 * LEVELS + 1),
        out_specs=ANY,
        scratch_shapes=[
            pltpu.VMEM((2, 32, 8, 512), jnp.float32),
            pltpu.VMEM((2, 34, 8, 512), jnp.float32),
            pltpu.VMEM((2, 34, 8, 512), jnp.float32),
            pltpu.VMEM((7, 32, 8, 512), jnp.float32),
            pltpu.VMEM((2, 32, 8, 512), jnp.float32),
            pltpu.VMEM((5, 16, 8, 128), jnp.float32),
            grid,
            grid,
            grid,
            grid,
            pltpu.VMEM((2, 2, 256, 128), jnp.float32),
            pltpu.SemaphoreType.DMA((2,)),
        ],
        compiler_params=PARAMS,
        name="up",
    )(place, gathered, *saved)


def local(observed, coherence_class, class_weight, class_stiffness):
    own = jnp.concatenate([observed, (coherence_class + 1).astype(jnp.float32)[None]], axis=0)
    north = send(own[:, 128:], "row", 1)
    south = send(own[:, :128], "row", -1)
    right = jnp.concatenate([north[:, :, 128:], own[:, :, 128:], south[:, :, 128:]], axis=1)
    left = jnp.concatenate([north[:, :, :128], own[:, :, :128], south[:, :, :128]], axis=1)
    west = send(right, "col", 1)
    east = send(left, "col", -1)
    results = down(own, north, south, west, east, make_tables(class_weight, class_stiffness))
    message = results[-1].reshape(256, 2, 128)
    gathered = lax.all_to_all(message, ("row", "col"), 0, 0).reshape(512, 128)
    place = jnp.stack([lax.axis_index("row"), lax.axis_index("col")]).astype(jnp.int32)
    return up(place, gathered, results[:-1])


def solution(mesh):
    in_specs = (P(None, "row", "col"), P("row", "col"), P(), P())
    out_specs = P(None, "row", "col")
    return jax.shard_map(local, mesh=mesh, in_specs=in_specs, out_specs=out_specs, check_vma=False)
```

time: 700 us -> 117 us (0.17)
  the two profiles are of different devices: /device:TPU:130 before, /device:TPU:1 now
where the time goes in v1:
time: 117 us
  Pallas kernels  43.1 us (37%)
  starting transfers between devices  33.6 us (29%)
  waiting for transfers between devices  33.1 us (28%)
  other arithmetic  4.49 us (4%)
  local copies, waits for them, and re-layouts  2.28 us (2%)
    pallas_call x1, Pallas kernels, down(): pl.pallas_call(down_kernel, out_shape=[jax.ShapeDtypeStruct(s, jnp.float3...  23.3 us
    all_to_all x1, starting transfers between devices, local(): gathered = lax.all_to_all(message, ('row', 'col'), 0, 0).reshape(512, 128)  21.3 us
    pallas_call x1, Pallas kernels, up(): pl.pallas_call(up_kernel, out_shape=jax.ShapeDtypeStruct((2, 256, 256), j...  19.8 us
    ppermute x4, waiting for transfers between devices, send(): lax.ppermute(x, axis, [(i, i + step) for i in range(count) if 0 <= i + st...  18 us
    all_to_all x1, waiting for transfers between devices, local(): gathered = lax.all_to_all(message, ('row', 'col'), 0, 0).reshape(512, 128)  15.1 us
    ppermute x4, starting transfers between devices, send(): lax.ppermute(x, axis, [(i, i + step) for i in range(count) if 0 <= i + st...  12.3 us
  transfers between devices with their start and end apart: 5, of which 5 were waited for; matrix products, arithmetic and copies ran while one was open for 2% of the time, Pallas kernels for 0%

profile of v1, /device:TPU:1, one launch (start us, length us, event | category | flops | bytes accessed | tf_op | source)
XLA Modules:
  0.0 116.7 jit_solution(17977944461117232349)
XLA Ops:
  0.0 0.0 copy-start
  0.0 1.0 convert_bitcast_fusion
  1.0 1.1 fusion.1
  2.1 4.9 %collective-permute-start = (f32[3,128,256]{2,1,0:T(8,128)S(1)}, f32[3,128,256]{2,1,0:T(8,128)S(1)}, u32[]{:S(2)}, u32[]{:S(2)}) collective-permute-start(f32[3,128,256]{2,1,0:T(8,128)S(1)} %get-tuple-element.50), channel_id=1, source_target_pairs={{0,16},{16,32},{32,48},{48,64},{64,80},{80,96},{96,112},{112,128},... | collective-permute-start | bytes 1179656 | tf_op jit(solution)/shard_map/ppermute | solution.py:365
  7.1 1.9 %collective-permute-start.1 = (f32[3,128,256]{2,1,0:T(8,128)S(1)}, f32[3,128,256]{2,1,0:T(8,128)S(1)}, u32[]{:S(2)}, u32[]{:S(2)}) collective-permute-start(f32[3,128,256]{2,1,0:T(8,128)S(1)} %get-tuple-element.49), channel_id=1, source_target_pairs={{16,0},{32,16},{48,32},{64,48},{80,64},{96,80},{112,96},{128,112},... | collective-permute-start | bytes 1179656 | tf_op jit(solution)/shard_map/ppermute | solution.py:365
  9.0 0.0 copy-done
  9.0 0.1 fusion.3
  9.1 2.7 %collective-permute-done.north = f32[3,128,256]{2,1,0:T(8,128)S(1)} collective-permute-done((f32[3,128,256]{2,1,0:T(8,128)S(1)}, f32[3,128,256]{2,1,0:T(8,128)S(1)}, u32[]{:S(2)}, u32[]{:S(2)}) %collective-permute-start) | collective-permute-done | bytes 393248 | tf_op jit(solution)/shard_map/ppermute | solution.py:365
  11.8 0.0 copy-start.1
  11.8 4.4 %collective-permute-done.1.south = f32[3,128,256]{2,1,0:T(8,128)S(1)} collective-permute-done((f32[3,128,256]{2,1,0:T(8,128)S(1)}, f32[3,128,256]{2,1,0:T(8,128)S(1)}, u32[]{:S(2)}, u32[]{:S(2)}) %collective-permute-start.1) | collective-permute-done | bytes 393248 | tf_op jit(solution)/shard_map/ppermute | solution.py:365
  16.2 0.0 copy-start.2
  16.2 0.1 pad_maximum_fusion.2
  16.3 0.0 copy-done.1
  16.3 0.6 copy-done.2
  16.9 1.4 %collective-permute-start.3 = (f32[3,512,128]{2,1,0:T(8,128)S(1)}, f32[3,512,128]{2,1,0:T(8,128)S(1)}, u32[]{:S(2)}, u32[]{:S(2)}) collective-permute-start(f32[3,512,128]{2,1,0:T(8,128)S(1)} %pad_maximum_fusion.2), channel_id=1, source_target_pairs={{1,0},{2,1},{3,2},{4,3},{5,4},{6,5},{7,6},{8,7},{9,8},{10,9},{11,1... | collective-permute-start | bytes 2359304 | tf_op jit(solution)/shard_map/ppermute | solution.py:365
  18.4 0.1 pad_maximum_fusion.1
  18.4 4.0 %collective-permute-start.2 = (f32[3,512,128]{2,1,0:T(8,128)S(1)}, f32[3,512,128]{2,1,0:T(8,128)S(1)}, u32[]{:S(2)}, u32[]{:S(2)}) collective-permute-start(f32[3,512,128]{2,1,0:T(8,128)S(1)} %pad_maximum_fusion.1), channel_id=1, source_target_pairs={{0,1},{1,2},{2,3},{3,4},{4,5},{5,6},{6,7},{7,8},{8,9},{9,10},{10,1... | collective-permute-start | bytes 2359304 | tf_op jit(solution)/shard_map/ppermute | solution.py:365
  22.5 0.0 copy-done.7
  22.5 0.0 copy-done.6
  22.5 0.1 fusion.4
  22.6 0.6 pad_maximum_fusion.3.tables
  23.2 0.9 pad_maximum_fusion.own
  24.1 9.1 %collective-permute-done.3.east = f32[3,512,128]{2,1,0:T(8,128)S(1)} collective-permute-done((f32[3,512,128]{2,1,0:T(8,128)S(1)}, f32[3,512,128]{2,1,0:T(8,128)S(1)}, u32[]{:S(2)}, u32[]{:S(2)}) %collective-permute-start.3) | collective-permute-done | bytes 786464 | tf_op jit(solution)/shard_map/ppermute | solution.py:365
  33.2 1.8 %collective-permute-done.2.west = f32[3,512,128]{2,1,0:T(8,128)S(1)} collective-permute-done((f32[3,512,128]{2,1,0:T(8,128)S(1)}, f32[3,512,128]{2,1,0:T(8,128)S(1)}, u32[]{:S(2)}, u32[]{:S(2)}) %collective-permute-start.2) | collective-permute-done | bytes 786464 | tf_op jit(solution)/shard_map/ppermute | solution.py:365
  35.0 0.0 copy-done.4
  35.0 0.9 copy-done.5
  35.9 23.3 %down.1 = (f32[4,32,8,512]{3,2,1,0:T(8,128)}, f32[4,16,8,512]{3,2,1,0:T(8,128)}, f32[4,8,8,512]{3,2,1,0:T(8,128)}, f32[4,4,8,512]{3,2,1,0:T(8,128)}, f32[4,2,8,5...) custom-call(f32[3,256,256]{2,1,0:T(8,128)} %pad_maximum_fusion.own, ...), custom_call_target="tpu_custom_call" | custom-call | tf_op jit(solution)/shard_map/down/pallas_call | solution.py:379
  59.2 21.3 %all-to-all-start = ((f32[256,2,128]{2,1,0:T(2,128)}), f32[256,2,128]{2,1,0:T(2,128)S(1)}, u32[]{:S(2)}, u32[]{:S(2)}) async-start(f32[256,2,128]{2,1,0:T(2,128)} %bitcast.11), calls=%async_computation | async-start | bytes 524288 | tf_op jit(solution)/shard_map/all_to_all | solution.py:433
  80.6 0.6 pad_add_fusion.place
  81.2 15.1 %all-to-all-done = f32[256,2,128]{2,1,0:T(2,128)S(1)} async-done(((f32[256,2,128]{2,1,0:T(2,128)}), f32[256,2,128]{2,1,0:T(2,128)S(1)}, u32[]{:S(2)}, u32[]{:S(2)}) %all-to-all-start) | async-done | bytes 262176 | tf_op jit(solution)/shard_map/all_to_all | solution.py:433
  96.3 0.7 copy-done.3
  97.0 19.8 %up.1 = f32[2,256,256]{2,1,0:T(8,128)} custom-call(s32[2]{0:T(128)} %pad_add_fusion.place, f32[512,128]{1,0:T(8,128)} %bitcast.10, f32[4,32,8,512]{3,2,1,0:T(8,128)} %get-tuple-element.27.rest_0_, f32[4,16,8,512]{3,2,1,0:T(8,128)} %get-tuple-element.28.rest_1_, f32[4,8,8,512]{3,2,1,0:T(8,128)} %get-tuple-element.29.rest_2_, ...), custom_call_target="tpu_custom_call" | custom-call | tf_op jit(solution)/shard_map/up/pallas_call | solution.py:399
  (8 shorter events, 0.1 us)
Async XLA Ops:
  0.0 9.0 %copy-start = (f32[2,256,256]{2,1,0:T(8,128)S(1)}, f32[2,256,256]{2,1,0:T(8,128)}, u32[]{:S(2)}) copy-start(f32[2,256,256]{2,1,0:T(8,128)} %param.4) | copy-start | bytes 1572868
  2.1 9.6 %collective-permute-start = (f32[3,128,256]{2,1,0:T(8,128)S(1)}, f32[3,128,256]{2,1,0:T(8,128)S(1)}, u32[]{:S(2)}, u32[]{:S(2)}) collective-permute-start(f32[3,128,256]{2,1,0:T(8,128)S(1)} %get-tuple-element.50), channel_id=1, source_target_pairs={{0,16},{16,32},{32,48},{48,64},{64,80},{80,96},{96,112},{112,128},... | collective-permute-start | bytes 1179656 | tf_op jit(solution)/shard_map/ppermute | solution.py:365
  7.1 9.1 %collective-permute-start.1 = (f32[3,128,256]{2,1,0:T(8,128)S(1)}, f32[3,128,256]{2,1,0:T(8,128)S(1)}, u32[]{:S(2)}, u32[]{:S(2)}) collective-permute-start(f32[3,128,256]{2,1,0:T(8,128)S(1)} %get-tuple-element.49), channel_id=1, source_target_pairs={{16,0},{32,16},{48,32},{64,48},{80,64},{96,80},{112,96},{128,112},... | collective-permute-start | bytes 1179656 | tf_op jit(solution)/shard_map/ppermute | solution.py:365
  11.8 4.5 %copy-start.1 = (f32[3,128,256]{2,1,0:T(8,128)}, f32[3,128,256]{2,1,0:T(8,128)S(1)}, u32[]{:S(2)}) copy-start(f32[3,128,256]{2,1,0:T(8,128)S(1)} %collective-permute-done.north) | copy-start | bytes 1179652
  16.2 0.7 copy-start.2
  16.9 5.5 %copy-start.7 = (f32[8]{0:T(128)S(1)}, f32[8]{0:T(128)}, u32[]{:S(2)}) copy-start(f32[8]{0:T(128)} %param.7) | copy-start | bytes 100
  16.9 5.5 %copy-start.6 = (f32[8]{0:T(128)S(1)}, f32[8]{0:T(128)}, u32[]{:S(2)}) copy-start(f32[8]{0:T(128)} %param.6) | copy-start | bytes 100
  16.9 16.3 %collective-permute-start.3 = (f32[3,512,128]{2,1,0:T(8,128)S(1)}, f32[3,512,128]{2,1,0:T(8,128)S(1)}, u32[]{:S(2)}, u32[]{:S(2)}) collective-permute-start(f32[3,512,128]{2,1,0:T(8,128)S(1)} %pad_maximum_fusion.2), channel_id=1, source_target_pairs={{1,0},{2,1},{3,2},{4,3},{5,4},{6,5},{7,6},{8,7},{9,8},{10,9},{11,1... | collective-permute-start | bytes 2359304 | tf_op jit(solution)/shard_map/ppermute | solution.py:365
  18.4 16.6 %collective-permute-start.2 = (f32[3,512,128]{2,1,0:T(8,128)S(1)}, f32[3,512,128]{2,1,0:T(8,128)S(1)}, u32[]{:S(2)}, u32[]{:S(2)}) collective-permute-start(f32[3,512,128]{2,1,0:T(8,128)S(1)} %pad_maximum_fusion.1), channel_id=1, source_target_pairs={{0,1},{1,2},{2,3},{3,4},{4,5},{5,6},{6,7},{7,8},{8,9},{9,10},{10,1... | collective-permute-start | bytes 2359304 | tf_op jit(solution)/shard_map/ppermute | solution.py:365
  33.2 1.8 %copy-start.4 = (f32[3,512,128]{2,1,0:T(8,128)}, f32[3,512,128]{2,1,0:T(8,128)S(1)}, u32[]{:S(2)}) copy-start(f32[3,512,128]{2,1,0:T(8,128)S(1)} %collective-permute-done.3.east) | copy-start | bytes 2359300
  35.0 0.9 copy-start.5
  59.2 37.1 %all-to-all-start = ((f32[256,2,128]{2,1,0:T(2,128)}), f32[256,2,128]{2,1,0:T(2,128)S(1)}, u32[]{:S(2)}, u32[]{:S(2)}) async-start(f32[256,2,128]{2,1,0:T(2,128)} %bitcast.11), calls=%async_computation | async-start | bytes 524288 | tf_op jit(solution)/shard_map/all_to_all | solution.py:433
  96.3 0.7 copy-start.3

commit v2 on v1

v2 whole, which is shorter than its diff:
```python
import jax
import jax.numpy as jnp
from jax import lax
from jax.experimental import pallas as pl
from jax.experimental.pallas import tpu as pltpu
from jax.sharding import PartitionSpec as P

CG_ITERS = 12
FAR = -1.0e4
TILES = (48, 24, 12, 6, 3)
LANES = (384, 256, 128, 128, 128)
F32 = jnp.float32
BF16 = jnp.bfloat16
BLACK, EDGE, INV, STATE = 4, 6, 11, 13


def iota(shape, axis):
    return lax.broadcasted_iota(jnp.int32, shape, axis)


def roll(x, shift, axis):
    return pltpu.roll(x, shift % x.shape[axis], axis)


def dot(a, b):
    return jnp.dot(a, b, preferred_element_type=F32)


def split(x):
    high = x.astype(BF16)
    return high, (x - high.astype(F32)).astype(BF16)


def times(x, pattern):
    high, low = split(x)
    return dot(high, pattern) + dot(low, pattern)


def pick(pattern, x):
    high, low = split(x)
    return dot(pattern, high) + dot(pattern, low)


def onehot(condition):
    return jnp.where(condition, 1.0, 0.0).astype(BF16)


def even_lanes(shape):
    return iota(shape, len(shape) - 1) % 2 == 0


def signed_lane(level, lane):
    width = LANES[level]
    own = 256 >> level
    return jnp.where(lane < (own + width) // 2, lane, lane - width)


def coarse_lane(level, lane):
    c = signed_lane(level, lane) >> 1
    return jnp.where(c < 0, c + LANES[level + 1], c)


def side_lane(field, lane3):
    c = (signed_lane(3, lane3) >> 1) + 64 * field
    return jnp.where(c < 0, c + 128, c)


def ends(ref, index, count):
    ref[index, 0] = roll(ref[index, count], 1, 0)
    ref[index, count + 1] = roll(ref[index, 1], -1, 0)


def loop(count, body, unroll):
    if count <= unroll:
        for i in range(count):
            body(i)
        return

    def step(i, carry):
        for j in range(unroll):
            body(i * unroll + j)
        return carry

    lax.fori_loop(0, count // unroll, step, 0)


def pull_red(a, black, f, state, even):
    b = black[f, a + 1]
    total = state[EDGE, a + 1] * b + state[EDGE + 1, a + 1] * jnp.where(even, black[f, a], black[f, a + 2])
    return total + state[EDGE + 3, a + 1] * roll(b, -1, 1) + roll(state[EDGE + 4, a + 1] * b, 1, 1)


def pull_black(a, red, f, state, even):
    r = red[f, a + 1]
    total = state[EDGE, a + 1] * r + state[EDGE + 2, a + 1] * jnp.where(even, red[f, a + 2], red[f, a])
    return total + state[EDGE + 4, a + 1] * roll(r, -1, 1) + roll(state[EDGE + 3, a + 1] * r, 1, 1)


def lookup(table, index):
    parts = []
    for c in range(index.shape[1] // 128):
        parts.append(jnp.take_along_axis(table, index[:, c * 128 : (c + 1) * 128], axis=1))
    return jnp.concatenate(parts, axis=1)


def edges4(g, w):
    k = [jnp.maximum(g + roll(g, s, x), 0.0) for s, x in ((1, 0), (-1, 0), (1, 1), (-1, 1))]
    return k, 1.0 / jnp.maximum(w + k[0] + k[1] + k[2] + k[3], 1e-20)


def pull4(k, v):
    return k[0] * roll(v, 1, 0) + k[1] * roll(v, -1, 0) + k[2] * roll(v, 1, 1) + k[3] * roll(v, -1, 1)


def red4():
    return (iota((24, 128), 0) + iota((24, 128), 1)) % 2 == 0


def rows_kernel(observed, classes, own, top, bottom):
    x = (classes[...] + 1).astype(F32)
    own[...] = x
    top[2] = x[:64]
    bottom[2] = x[192:]
    for f in range(2):
        top[f] = observed[f, 0:64]
        bottom[f] = observed[f, 192:256]


def cols_kernel(observed, classes, north, south, left, right):
    low = iota((192, 128), 1) < 64
    for f in range(3):
        own = observed.at[f] if f < 2 else classes
        sides = []
        for c in (0, 128):
            lanes = slice(c, c + 128)
            b = jnp.concatenate([own[192:256, lanes], south[f, :, lanes], north[f, :, lanes]], axis=0)
            sides.append((own[0:192, lanes], b))
        left[f] = jnp.where(low, sides[0][0], roll(sides[0][1], 64, 1))
        right[f] = jnp.where(low, roll(sides[1][1], 64, 1), sides[1][0])


def message_row(x, pattern, mine):
    return jnp.sum(jnp.where(mine, times(x, pattern), 0.0), axis=0, keepdims=True)


def down_kernel(place, observed, classes, north, south, west, east, tables, *rest):
    saved = rest[:4]
    saved4, message = rest[4:6]
    states = rest[6:10]
    gw, red, full, sums, frame, strip, nat, arrived, sent = rest[10:]

    pieces = []
    for f in range(3):
        own = observed.at[f] if f < 2 else classes
        for half in range(2):
            lanes = pl.ds(half * 128, 128)
            pieces.append((own.at[:, lanes], frame.at[f, half, pl.ds(0, 256), :]))
            pieces.append((south.at[f, :, lanes], frame.at[f, half, pl.ds(256, 64), :]))
            pieces.append((north.at[f, :, lanes], frame.at[f, half, pl.ds(320, 64), :]))
    pieces += [(west, strip.at[0]), (east, strip.at[1])]
    copies = [pltpu.make_async_copy(a, b, arrived.at[i]) for i, (a, b) in enumerate(pieces)]
    for copy in copies:
        copy.start()
    for copy in copies:
        copy.wait()
    low = iota((192, 128), 1) < 64
    for f in range(3):
        w, e = strip[0, f], strip[1, f]
        frame[f, 2, 0:192, :] = jnp.where(low, e, w)
        frame[f, 2, 192:384, :] = roll(jnp.where(low, w, e), 64, 1)

    tab_g = jnp.broadcast_to(tables[0:1, :], (8, 128))
    tab_w = jnp.broadcast_to(tables[1:2, :], (8, 128))

    def frame_tile(f, a):
        return jnp.concatenate([frame[f, c, pl.ds(a, 8, stride=48), :] for c in range(3)], axis=1)

    outgoing = []
    for level in range(4):
        count, width = TILES[level] // 2, LANES[level]
        even = even_lanes((8, width))
        state = states[level]
        unroll = (4, 4, 6, 3)[level]
        here = pl.ds(0, width)

        def pack(a, level=level, even=even, state=state, here=here):
            for f in range(2):
                if level == 0:
                    x, y = frame_tile(f, 2 * a), frame_tile(f, 2 * a + 1)
                else:
                    x, y = full[f, 2 * a, :, here], full[f, 2 * a + 1, :, here]
                state[f, a + 1] = jnp.where(even, x, y)
                state[2 + f, a + 1] = jnp.where(even, y, x)
            if level == 0:
                i, j = (frame_tile(2, 2 * a + k).astype(jnp.int32) for k in range(2))
                pairs = ((lookup(tab_g, i), lookup(tab_g, j)), (lookup(tab_w, i), lookup(tab_w, j)))
            else:
                pairs = tuple((full[q, 2 * a, :, here], full[q, 2 * a + 1, :, here]) for q in (2, 3))
            for q, (x, y) in enumerate(pairs):
                gw[2 * q, a + 1, :, here] = jnp.where(even, x, y)
                gw[2 * q + 1, a + 1, :, here] = jnp.where(even, y, x)

        loop(count, pack, unroll)
        for q in range(2):
            gw[q, 0, :, here] = roll(gw[q, count, :, here], 1, 0)
            gw[q, count + 1, :, here] = roll(gw[q, 1, :, here], -1, 0)

        def edges(a, even=even, state=state, here=here):
            r, b = gw[0, a + 1, :, here], gw[1, a + 1, :, here]
            same = jnp.maximum(r + b, 0.0)
            r_other = jnp.maximum(r + jnp.where(even, gw[1, a, :, here], gw[1, a + 2, :, here]), 0.0)
            b_other = jnp.maximum(b + jnp.where(even, gw[0, a + 2, :, here], gw[0, a, :, here]), 0.0)
            r_east = jnp.maximum(r + roll(b, -1, 1), 0.0)
            b_east = jnp.maximum(b + roll(r, -1, 1), 0.0)
            r_inv = 1.0 / jnp.maximum(gw[2, a + 1, :, here] + same + r_other + r_east + roll(b_east, 1, 1), 1e-20)
            b_inv = 1.0 / jnp.maximum(gw[3, a + 1, :, here] + same + b_other + b_east + roll(r_east, 1, 1), 1e-20)
            for i, x in enumerate((same, r_other, b_other, r_east, b_east, r_inv, b_inv)):
                state[EDGE + i, a + 1] = x
            for f in range(2):
                red[f, a + 1, :, here] = state[f, a + 1] * r_inv
            sums[2, a, :, here] = 0.5 * (r + b)
            sums[3, a, :, here] = gw[2, a + 1, :, here] + gw[3, a + 1, :, here]

        loop(count, edges, unroll)
        for f in range(2):
            red[f, 0, :, here] = roll(red[f, count, :, here], 1, 0)
            red[f, count + 1, :, here] = roll(red[f, 1, :, here], -1, 0)

        def first_black(a, even=even, state=state, here=here):
            view = red.at[:, :, :, here]
            for f in range(2):
                state[BLACK + f, a + 1] = (state[2 + f, a + 1] + pull_black(a, view, f, state, even)) * state[INV + 1, a + 1]

        loop(count, first_black, unroll)
        for f in range(2):
            ends(state, BLACK + f, count)
        outgoing.append(pltpu.make_async_copy(state, saved[level], sent.at[level]))
        outgoing[-1].start()

        def restrict(a, even=even, state=state, here=here):
            for f in range(2):
                sums[f, a, :, here] = pull_red(a, state.at[BLACK : BLACK + 2], f, state, even)

        loop(count, restrict, unroll)
        fine = iota((width, LANES[level + 1]), 0)
        lane = iota((width, LANES[level + 1]), 1)
        if level < 3:
            pattern = onehot(coarse_lane(level, fine) == lane)
            for q in range(4):
                x = sums[q, 0:count, :, here].reshape(count * 8, width)
                full[q, 0:count, :, pl.ds(0, LANES[level + 1])] = times(x, pattern).reshape(count, 8, LANES[level + 1])
        else:
            first, second = (onehot(side_lane(f, fine) == lane) for f in range(2))
            x = [sums[q, 0:3, :, here].reshape(24, 128) for q in range(4)]
            results = [times(x[0], first) + times(x[1], second)] + [times(x[q], first + second) for q in (2, 3)]
            for q in range(3):
                for a in range(3):
                    nat[q, pl.ds(a, 8, stride=3), :] = results[q][a * 8 : a * 8 + 8]

    rhs, g, w = nat[0], nat[1], nat[2]
    is_red = red4()
    k, inv = edges4(g, w)
    v = jnp.where(is_red, rhs * inv, 0.0)
    v = jnp.where(is_red, v, (rhs + pull4(k, v)) * inv)
    merged = jnp.where(is_red, rhs, v)
    saved4[0] = merged
    saved4[1] = rhs
    saved4[2] = g
    saved4[3] = w
    nat[3] = jnp.where(is_red, pull4(k, v), 0.0)
    nat[4] = jnp.where(iota((24, 128), 1) < 64, 0.5 * g, w)

    lane = iota((128, 128), 0)
    l = iota((128, 128), 1)
    sub, at = iota((8, 128), 0), iota((8, 128), 1)
    pattern = onehot(jnp.logical_and(lane // 64 == l // 64, (lane % 64) // 2 == l % 8))
    mine = sub == (at // 8) % 8
    common = []
    for q in (3, 4):
        x = nat[q, pl.ds(0, 8, stride=2), :] + nat[q, pl.ds(1, 8, stride=2), :]
        common.append(message_row(x, pattern, mine))
    pattern = onehot(jnp.logical_and(lane // 64 == l // 64, lane % 64 == l % 16))
    top = message_row(merged[0:8], pattern, sub == (at // 16) % 4)
    bottom = message_row(merged[8:16], pattern, sub == (at // 16) % 4 + 4)
    mine = iota((16, 128), 0) == (iota((16, 128), 1) // 4) % 16
    pattern = onehot(jnp.logical_and(lane // 64 == l // 64, lane % 64 == l % 4))
    left = message_row(merged[0:16], pattern, mine)
    pattern = onehot(jnp.logical_and(lane // 64 == l // 64, lane % 64 == l % 4 + 12))
    right = message_row(merged[0:16], pattern, mine)

    block = jnp.concatenate((common + [jnp.zeros((1, 128), F32)]) * 8, axis=0)

    def send(i, carry):
        message[pl.ds(pl.multiple_of(i * 24, 8), 24), :] = block
        return carry

    lax.fori_loop(0, 32, send, 0)
    row, col = place[0], place[1]
    for dr, dc, what in NEIGHBOURS:
        x = {-1: top, 1: bottom}.get(dr, left if dc < 0 else right)
        r, c = row + dr, col + dc

        @pl.when(jnp.logical_and(jnp.logical_and(r >= 0, r < 16), jnp.logical_and(c >= 0, c < 16)))
        def _(r=r, c=c, x=x):
            message[pl.ds((r * 16 + c) * 3 + 2, 1), :] = x

    for copy in outgoing:
        copy.wait()


NEIGHBOURS = [(dr, dc, None) for dr in (-1, 0, 1) for dc in (-1, 0, 1) if dr or dc]


def cg(gathered, kc, e, r, d, q):
    lane = iota((8, 128), 1)
    sub = iota((8, 128), 0)
    group = lane // 8
    arrays = [[None] * 16 for _ in range(4)]
    for hi in range(2):
        for pair in range(2):
            v = [gathered[pl.ds((hi * 128 + c) * 3 + pair, 8, stride=48), :] for c in range(16)]
            for k in (1, 2, 4, 8):
                low = (group // k) % 2 == 0
                for c in range(16):
                    if not c & k:
                        x, y = v[c], v[c | k]
                        v[c] = jnp.where(low, x, roll(y, 8 * k, 1))
                        v[c | k] = jnp.where(low, roll(x, -8 * k, 1), y)
            for i in range(16):
                arrays[2 * pair + i // 8][hi * 8 + i % 8] = v[i]

    def north(tile, t):
        if t % 8:
            return tile(t - 1)
        turned = roll(tile(t + 7), 1, 0)
        return turned if t == 0 else jnp.where(sub == 0, roll(tile(7), 1, 0), turned)

    def south(tile, t):
        if t % 8 != 7:
            return tile(t + 1)
        turned = roll(tile(t - 7), -1, 0)
        return turned if t == 15 else jnp.where(sub == 7, roll(tile(8), -1, 0), turned)

    g = arrays[2]
    for t in range(16):
        up = jnp.maximum(g[t] + north(lambda i: g[i], t), 0.0)
        down = jnp.maximum(g[t] + south(lambda i: g[i], t), 0.0)
        if t == 0:
            up = jnp.where(sub == 0, 0.0, up)
        if t == 15:
            down = jnp.where(sub == 7, 0.0, down)
        left = jnp.where(lane == 0, 0.0, jnp.maximum(g[t] + roll(g[t], 1, 1), 0.0))
        right = jnp.where(lane == 127, 0.0, jnp.maximum(g[t] + roll(g[t], -1, 1), 0.0))
        kc[0, t] = up
        kc[1, t] = down
        kc[2, t] = left
        kc[3, t] = right
        kc[4, t] = arrays[3][t] + up + down + left + right

    norm = []
    for f in range(2):
        total = 0.0
        for t in range(16):
            x = arrays[f][t]
            e[f, t] = jnp.zeros_like(x)
            r[f, t] = x
            d[f, t] = x
            total += x * x
        norm.append(jnp.sum(total, axis=(0, 1), keepdims=True))

    def iterate(_, norm):
        alpha = []
        for f in range(2):
            tile = lambda i, f=f: d[f, i]
            total = 0.0
            for t in range(16):
                x = d[f, t]
                image = kc[4, t] * x - (
                    kc[0, t] * north(tile, t)
                    + kc[1, t] * south(tile, t)
                    + kc[2, t] * roll(x, 1, 1)
                    + kc[3, t] * roll(x, -1, 1)
                )
                q[f, t] = image
                total += x * image
            alpha.append(norm[f] / jnp.sum(total, axis=(0, 1), keepdims=True))
        fresh = []
        for f in range(2):
            total = 0.0
            for t in range(16):
                e[f, t] = e[f, t] + alpha[f] * d[f, t]
                x = r[f, t] - alpha[f] * q[f, t]
                r[f, t] = x
                total += x * x
            fresh.append(jnp.sum(total, axis=(0, 1), keepdims=True))
        for f in range(2):
            beta = fresh[f] / norm[f]
            for t in range(16):
                d[f, t] = r[f, t] + beta * d[f, t]
        return tuple(fresh)

    lax.fori_loop(0, CG_ITERS, iterate, tuple(norm))


def merged_frame(place, gathered, merged):
    row, col = place[0], place[1]
    at = iota((24, 128), 0)
    l = iota((24, 128), 1)
    total = {}
    for dr, dc, _ in NEIGHBOURS:
        r, c = row + dr, col + dc
        there = jnp.logical_and(jnp.logical_and(r >= 0, r < 16), jnp.logical_and(c >= 0, c < 16))
        index = jnp.where(there, (r * 16 + c) * 3 + 2, 0)
        x = gathered[pl.ds(index, 1), :] * jnp.where(there, 1.0, 0.0)
        if dr:
            mine = at == (20 if dr < 0 else 16) + (l // 16) % 4
        else:
            mine = at == (l // 4) % 16
        key = dc if dr else 2 * dc
        total[key] = total.get(key, 0.0) + jnp.where(mine, jnp.broadcast_to(x, (24, 128)), 0.0)
    l = iota((128, 128), 0)
    lane = iota((128, 128), 1)
    base = (l // 64) * 64
    j, c = l % 16, l % 4
    patterns = {
        0: lane == base + j,
        -1: jnp.logical_and(j >= 12, lane == (base + j - 16) % 128),
        1: jnp.logical_and(j < 4, lane == base + 16 + j),
        -2: lane == (base + c - 4) % 128,
        2: lane == base + 16 + c,
    }
    own = jnp.logical_and(at < 16, iota((24, 128), 1) % 64 < 16)
    result = jnp.where(own, merged, 0.0)
    for key, x in total.items():
        result += times(x, onehot(patterns[key]))
    return result


def up_kernel(place, gathered, saved4, *rest):
    saved, out = rest[:4], rest[4]
    states = rest[5:9]
    full, red, blk, kc, e, r, d, q, result, nat, arrived, sent = rest[9:]
    copies = [pltpu.make_async_copy(saved[level], states[level], arrived.at[level]) for level in range(4)]
    for copy in copies[::-1]:
        copy.start()
    cg(gathered, kc, e, r, d, q)

    n = iota((24, 128), 1)
    at = iota((24, 128), 0)
    grid_row = (n // 64) * 64 + (n % 8) * 8 + (n // 8) % 8
    rows = onehot(grid_row == place[0] * 8 + (jnp.where(at < 20, at, at - 24) >> 1))
    j = iota((128, 128), 0)
    lane = iota((128, 128), 1)
    correction = 0.0
    for f in range(2):
        c = (lane + 32) % 128 - 32 - 64 * f
        cols = onehot(jnp.logical_and(jnp.logical_and(c >= -32, c < 32), j == place[1] * 8 + (c >> 1)))
        whole = jnp.concatenate([e[f, t] for t in range(16)], axis=0)
        correction += times(pick(rows, whole), cols)

    is_red = red4()
    merged = merged_frame(place, gathered, saved4[0])
    k, inv = edges4(saved4[2], saved4[3])
    x = jnp.where(is_red, 0.0, merged + correction)
    x = jnp.where(is_red, (merged + pull4(k, x)) * inv, 0.0)
    nat[...] = jnp.where(is_red, x, (saved4[1] + pull4(k, x)) * inv)
    ordered = jnp.concatenate([nat[pl.ds(a, 8, stride=3), :] for a in range(3)], axis=0)

    for level in range(3, -1, -1):
        count, width = TILES[level] // 2, LANES[level]
        even = even_lanes((8, width))
        state = states[level]
        unroll = (4, 4, 6, 3)[level]
        here = pl.ds(0, width)
        if level == 3:
            lane, wide = iota((128, 128), 0), iota((128, 128), 1)
            corrections = [times(ordered, onehot(side_lane(f, wide) == lane)) for f in range(2)]
        else:
            coarse = LANES[level + 1]
            lane, wide = iota((coarse, width), 0), iota((coarse, width), 1)
            pattern = onehot(coarse_lane(level, wide) == lane)
            corrections = [
                times(full[f, 0:count, :, pl.ds(0, coarse)].reshape(count * 8, coarse), pattern) for f in range(2)
            ]
        copies[level].wait()
        for f in range(2):
            blk[f, 1 : count + 1, :, here] = state[BLACK + f, 1 : count + 1] + corrections[f].reshape(count, 8, width)
            blk[f, 0, :, here] = roll(blk[f, count, :, here], 1, 0)
            blk[f, count + 1, :, here] = roll(blk[f, 1, :, here], -1, 0)

        def second_red(a, even=even, state=state, here=here):
            view = blk.at[:, :, :, here]
            for f in range(2):
                red[f, a + 1, :, here] = (state[f, a + 1] + pull_red(a, view, f, state, even)) * state[INV, a + 1]

        loop(count, second_red, unroll)
        for f in range(2):
            red[f, 0, :, here] = roll(red[f, count, :, here], 1, 0)
            red[f, count + 1, :, here] = roll(red[f, 1, :, here], -1, 0)

        def second_black(a, level=level, even=even, state=state, here=here):
            view = red.at[:, :, :, here]
            for f in range(2):
                x = red[f, a + 1, :, here]
                y = (state[2 + f, a + 1] + pull_black(a, view, f, state, even)) * state[INV + 1, a + 1]
                first, second = jnp.where(even, x, y), jnp.where(even, y, x)
                if level:
                    full[f, 2 * a, :, here] = first
                    full[f, 2 * a + 1, :, here] = second
                else:
                    for half in range(2):
                        lanes = slice(128 * half, 128 + 128 * half)
                        result[f, half, pl.ds(2 * a, 8, stride=48), :] = first[:, lanes]
                        result[f, half, pl.ds(2 * a + 1, 8, stride=48), :] = second[:, lanes]

        loop(count, second_black, unroll)

    copies = []
    for f in range(2):
        for half in range(2):
            source = result.at[f, half, pl.ds(0, 256), :]
            copies.append(pltpu.make_async_copy(source, out.at[f, :, pl.ds(half * 128, 128)], sent.at[2 * f + half]))
    for copy in copies:
        copy.start()
    for copy in copies:
        copy.wait()


VMEM = pl.BlockSpec(memory_space=pltpu.VMEM)
ANY = pl.BlockSpec(memory_space=pl.ANY)
SMEM = pl.BlockSpec(memory_space=pltpu.SMEM)
PARAMS = pltpu.CompilerParams(vmem_limit_bytes=48 * 1024 * 1024)


def shaped(*shape):
    return jax.ShapeDtypeStruct(shape, F32)


def scratch(*shape):
    return pltpu.VMEM(shape, F32)


def state_shapes():
    return [(STATE, TILES[level] // 2 + 2, 8, LANES[level]) for level in range(4)]


def row_strips(observed, classes):
    return pl.pallas_call(
        rows_kernel,
        out_shape=[shaped(256, 256), shaped(3, 64, 256), shaped(3, 64, 256)],
        in_specs=[VMEM] * 2,
        out_specs=[VMEM] * 3,
        compiler_params=PARAMS,
        name="rows",
    )(observed, classes)


def col_strips(observed, classes, north, south):
    return pl.pallas_call(
        cols_kernel,
        out_shape=[shaped(3, 192, 128)] * 2,
        in_specs=[VMEM] * 4,
        out_specs=[VMEM] * 2,
        compiler_params=PARAMS,
        name="cols",
    )(observed, classes, north, south)


def down(place, observed, classes, north, south, west, east, tables):
    return pl.pallas_call(
        down_kernel,
        out_shape=[shaped(*s) for s in state_shapes()] + [shaped(4, 24, 128), shaped(768, 128)],
        in_specs=[SMEM] + [ANY] * 6 + [VMEM],
        out_specs=[ANY] * 4 + [VMEM] * 2,
        scratch_shapes=[scratch(*s) for s in state_shapes()]
        + [
            scratch(4, 26, 8, 384),
            scratch(2, 26, 8, 384),
            scratch(4, 24, 8, 256),
            scratch(4, 24, 8, 384),
            scratch(3, 3, 384, 128),
            scratch(2, 3, 192, 128),
            scratch(5, 24, 128),
            pltpu.SemaphoreType.DMA((20,)),
            pltpu.SemaphoreType.DMA((4,)),
        ],
        compiler_params=PARAMS,
        name="down",
    )(place, observed, classes, north, south, west, east, tables)


def up(place, gathered, saved4, saved):
    return pl.pallas_call(
        up_kernel,
        out_shape=shaped(2, 256, 256),
        in_specs=[SMEM] + [VMEM] * 2 + [ANY] * 4,
        out_specs=ANY,
        scratch_shapes=[scratch(*s) for s in state_shapes()]
        + [
            scratch(2, 24, 8, 256),
            scratch(2, 26, 8, 384),
            scratch(2, 26, 8, 384),
            scratch(5, 16, 8, 128),
            scratch(2, 16, 8, 128),
            scratch(2, 16, 8, 128),
            scratch(2, 16, 8, 128),
            scratch(2, 16, 8, 128),
            scratch(2, 2, 384, 128),
            scratch(24, 128),
            pltpu.SemaphoreType.DMA((4,)),
            pltpu.SemaphoreType.DMA((4,)),
        ],
        compiler_params=PARAMS,
        name="up",
    )(place, gathered, saved4, *saved)


def make_tables(class_weight, class_stiffness):
    pad = lambda x, first: jnp.pad(jnp.concatenate([jnp.full((1,), first, F32), x]), (0, 119))
    return jnp.stack([pad(0.5 * class_stiffness, FAR), pad(class_weight, 0.0)])


def send(x, axis, step):
    count = lax.axis_size(axis)
    return lax.ppermute(x, axis, [(i, i + step) for i in range(count) if 0 <= i + step < count])


def local(observed, coherence_class, class_weight, class_stiffness):
    place = jnp.stack([lax.axis_index("row"), lax.axis_index("col")]).astype(jnp.int32)
    classes, top, bottom = row_strips(observed, coherence_class)
    north = send(bottom, "row", 1)
    south = send(top, "row", -1)
    left, right = col_strips(observed, classes, north, south)
    west = send(right, "col", 1)
    east = send(left, "col", -1)
    tables = make_tables(class_weight, class_stiffness)
    *saved, saved4, message = down(place, observed, classes, north, south, west, east, tables)
    gathered = lax.all_to_all(message.reshape(256, 1, 384), ("row", "col"), 0, 0).reshape(768, 128)
    return up(place, gathered, saved4, saved)


def solution(mesh):
    in_specs = (P(None, "row", "col"), P("row", "col"), P(), P())
    out_specs = P(None, "row", "col")
    return jax.shard_map(local, mesh=mesh, in_specs=in_specs, out_specs=out_specs, check_vma=False)
```

time: 117 us -> 83.6 us (0.71)
  blocking collectives: 0 us -> 36.3 us
  waiting for transfers between devices: 33.1 us -> 10 us
  starting transfers between devices: 33.6 us -> 11.4 us
  Pallas kernels: 43.1 us -> 21 us
  other arithmetic: 4.49 us -> 1.48 us
    all_to_all x0 -> x1, blocking collectives: none -> 36.3 us  [local(): lax.all_to_all(message.reshape(256, 1, 384), ('row', 'col'), 0, 0)]
    pallas_call x2 -> x4, Pallas kernels: 43.1 us -> 21 us  [the longest x1 11.6 us: up(): pl.pallas_call(up_kernel, out_shape=shaped(2, 256, 256), in_specs=[SMEM]...]
    all_to_all x1 -> x0, starting transfers between devices: 21.3 us -> none  [local(): gathered = lax.all_to_all(message, ('row', 'col'), 0, 0).reshape(512, 128)]
    all_to_all x1 -> x0, waiting for transfers between devices: 15.1 us -> none  [local(): gathered = lax.all_to_all(message, ('row', 'col'), 0, 0).reshape(512, 128)]
    ppermute x4, waiting for transfers between devices: 18 us -> 10 us  [send(): lax.ppermute(x, axis, [(i, i + step) for i in range(count) if 0 <= i + st...]
    concatenate x5 -> x0, other arithmetic: 2.2 us -> none  [the longest x3 2.09 us: local(): jnp.concatenate([observed, (coherence_class + 1).astype(jnp.float32)[None...]
    unnamed x16 -> x6, local copies, waits for them, and re-layouts: 2.23 us -> 3.03 us
  transfers between devices with their start and end apart: 5 -> 4, of which waited for: 5 -> 3; matrix products, arithmetic and copies ran while one was open for 2% -> 2% of each run, Pallas kernels for 0% -> 0%
where the time goes in v2:
time: 83.6 us; the launch traced here: 83.2 us
  blocking collectives  36.3 us (43%)
  Pallas kernels  21 us (25%)
  starting transfers between devices  11.4 us (14%)
  waiting for transfers between devices  10 us (12%)
  local copies, waits for them, and re-layouts  3.03 us (4%)
  other arithmetic  1.48 us (2%)
    all_to_all x1, blocking collectives, local(): lax.all_to_all(message.reshape(256, 1, 384), ('row', 'col'), 0, 0)  36.3 us
    pallas_call x1, Pallas kernels, up(): pl.pallas_call(up_kernel, out_shape=shaped(2, 256, 256), in_specs=[SMEM]...  11.6 us
    ppermute x4, starting transfers between devices, send(): lax.ppermute(x, axis, [(i, i + step) for i in range(count) if 0 <= i + st...  11.4 us
    ppermute x4, waiting for transfers between devices, send(): lax.ppermute(x, axis, [(i, i + step) for i in range(count) if 0 <= i + st...  10 us
    pallas_call x1, Pallas kernels, down(): pl.pallas_call(down_kernel, out_shape=[shaped(*s) for s in state_shapes()...  9.12 us
    unnamed x6, local copies, waits for them, and re-layouts  3.03 us
  transfers between devices with their start and end apart: 4, of which 3 were waited for; matrix products, arithmetic and copies ran while one was open for 2% of the time, Pallas kernels for 0%

profile of v2, /device:TPU:1, one launch (start us, length us, event | category | flops | bytes accessed | tf_op | source)
XLA Modules:
  0.0 83.2 jit_solution(12655424114709903271)
XLA Ops:
  0.0 0.0 copy-start
  0.0 1.0 %copy-done = f32[2,256,256]{2,1,0:T(8,128)S(1)} copy-done((f32[2,256,256]{2,1,0:T(8,128)S(1)}, f32[2,256,256]{2,1,0:T(8,128)}, u32[]{:S(2)}) %copy-start) | copy-done | bytes 524312
  1.0 0.0 copy-start.2
  1.0 0.9 %copy-done.2 = s32[256,256]{1,0:T(8,128)S(1)} copy-done((s32[256,256]{1,0:T(8,128)S(1)}, s32[256,256]{1,0:T(8,128)}, u32[]{:S(2)}) %copy-start.2) | copy-done | bytes 262168
  2.0 4.9 %collective-permute-start = (f32[3,64,256]{2,1,0:T(8,128)S(1)}, f32[3,64,256]{2,1,0:T(8,128)S(1)}, u32[]{:S(2)}, u32[]{:S(2)}) collective-permute-start(f32[3,64,256]{2,1,0:T(8,128)S(1)} %get-tuple-element.17), channel_id=1, source_target_pairs={{0,16},{16,32},{32,48},{48,64},{64,80},{80,96},{96,112},{112,128},... | collective-permute-start | bytes 589832 | tf_op jit(solution)/shard_map/ppermute | solution.py:625
  7.0 1.9 %collective-permute-start.1 = (f32[3,64,256]{2,1,0:T(8,128)S(1)}, f32[3,64,256]{2,1,0:T(8,128)S(1)}, u32[]{:S(2)}, u32[]{:S(2)}) collective-permute-start(f32[3,64,256]{2,1,0:T(8,128)S(1)} %get-tuple-element.18), channel_id=1, source_target_pairs={{16,0},{32,16},{48,32},{64,48},{80,64},{96,80},{112,96},{128,112},... | collective-permute-start | bytes 589832 | tf_op jit(solution)/shard_map/ppermute | solution.py:625
  8.9 0.7 broadcast_multiply_fusion
  9.6 0.0 collective-permute-done.north
  9.6 4.4 %collective-permute-done.1.south = f32[3,64,256]{2,1,0:T(8,128)S(1)} collective-permute-done((f32[3,64,256]{2,1,0:T(8,128)S(1)}, f32[3,64,256]{2,1,0:T(8,128)S(1)}, u32[]{:S(2)}, u32[]{:S(2)}) %collective-permute-start.1) | collective-permute-done | bytes 196640 | tf_op jit(solution)/shard_map/ppermute | solution.py:625
  14.0 0.0 copy-start.1
  14.0 1.0 %copy-done.1 = f32[2,256,256]{2,1,0:T(8,128)S(1)} copy-done((f32[2,256,256]{2,1,0:T(8,128)S(1)}, f32[2,256,256]{2,1,0:T(8,128)}, u32[]{:S(2)}) %copy-start.1) | copy-done | bytes 524312
  15.0 0.2 cols.1
  15.2 3.2 %collective-permute-start.2 = (f32[3,192,128]{2,1,0:T(8,128)S(1)}, f32[3,192,128]{2,1,0:T(8,128)S(1)}, u32[]{:S(2)}, u32[]{:S(2)}) collective-permute-start(f32[3,192,128]{2,1,0:T(8,128)S(1)} %get-tuple-element.19), channel_id=1, source_target_pairs={{0,1},{1,2},{2,3},{3,4},{4,5},{5,6},{6,7},{7,8},{8,9},{9,10},{10,1... | collective-permute-start | bytes 884744 | tf_op jit(solution)/shard_map/ppermute | solution.py:625
  18.5 1.3 %collective-permute-start.3 = (f32[3,192,128]{2,1,0:T(8,128)S(1)}, f32[3,192,128]{2,1,0:T(8,128)S(1)}, u32[]{:S(2)}, u32[]{:S(2)}) collective-permute-start(f32[3,192,128]{2,1,0:T(8,128)S(1)} %get-tuple-element.20), channel_id=1, source_target_pairs={{1,0},{2,1},{3,2},{4,3},{5,4},{6,5},{7,6},{8,7},{9,8},{10,9},{11,1... | collective-permute-start | bytes 884744 | tf_op jit(solution)/shard_map/ppermute | solution.py:625
  19.8 0.1 pad_add_fusion.place
  19.8 0.7 fusion
  20.6 1.5 %collective-permute-done.2.west = f32[3,192,128]{2,1,0:T(8,128)S(1)} collective-permute-done((f32[3,192,128]{2,1,0:T(8,128)S(1)}, f32[3,192,128]{2,1,0:T(8,128)S(1)}, u32[]{:S(2)}, u32[]{:S(2)}) %collective-permute-start.2) | collective-permute-done | bytes 294944 | tf_op jit(solution)/shard_map/ppermute | solution.py:625
  22.1 4.1 %collective-permute-done.3.east = f32[3,192,128]{2,1,0:T(8,128)S(1)} collective-permute-done((f32[3,192,128]{2,1,0:T(8,128)S(1)}, f32[3,192,128]{2,1,0:T(8,128)S(1)}, u32[]{:S(2)}, u32[]{:S(2)}) %collective-permute-start.3) | collective-permute-done | bytes 294944 | tf_op jit(solution)/shard_map/ppermute | solution.py:625
  26.2 9.1 %down.1 = (f32[13,26,8,384]{3,2,1,0:T(8,128)}, f32[13,14,8,256]{3,2,1,0:T(8,128)S(1)}, f32[13,8,8,128]{3,2,1,0:T(8,128)S(1)}, f32[13,5,8,128]{3,2,1,0:T(8,128)S(...) custom-call(s32[2]{0:T(128)S(1)} %pad_add_fusion.place, f32[2,256,256]{2,1,0:T(8,128)S(1)} %copy-done.1, ...), custom_call_target="tpu_custom_call" | custom-call | tf_op jit(solution)/shard_map/down/pallas_call | solution.py:570
  35.3 36.3 %all_to_all.5 = f32[256,1,384]{2,1,0:T(1,128)S(1)} all-to-all(f32[256,1,384]{2,1,0:T(1,128)S(1)} %bitcast.9), channel_id=1, replica_groups=mesh['row'=16,'col'=16] {'row','col'}, dimensions={0} | all-to-all | bytes 786432 | tf_op jit(solution)/shard_map/all_to_all | solution.py:638
  71.6 11.6 %up.1 = f32[2,256,256]{2,1,0:T(8,128)} custom-call(s32[2]{0:T(128)S(1)} %pad_add_fusion.place, f32[768,128]{1,0:T(8,128)S(1)} %bitcast.8, f32[4,24,128]{2,1,0:T(8,128)S(1)} %get-tuple-element.22.saved4, f32[13,26,8,384]{3,2,1,0:T(8,128)} %get-tuple-element.23.rest_0_, f32[13,14,8,256]{3,2,1,0:T(8,128)S(1)} %get-tuple-element.24.rest_1_, ...), custom_call_target="tpu_custom_call" | custom-call | tf_op jit(solution)/shard_map/up/pallas_call | solution.py:593
  (2 shorter events, 0.1 us)
Async XLA Ops:
  0.0 1.0 %copy-start = (f32[2,256,256]{2,1,0:T(8,128)S(1)}, f32[2,256,256]{2,1,0:T(8,128)}, u32[]{:S(2)}) copy-start(f32[2,256,256]{2,1,0:T(8,128)} %observed.5) | copy-start | bytes 1572868
  1.0 0.9 %copy-start.2 = (s32[256,256]{1,0:T(8,128)S(1)}, s32[256,256]{1,0:T(8,128)}, u32[]{:S(2)}) copy-start(s32[256,256]{1,0:T(8,128)} %classes.1) | copy-start | bytes 786436
  2.0 7.5 %collective-permute-start = (f32[3,64,256]{2,1,0:T(8,128)S(1)}, f32[3,64,256]{2,1,0:T(8,128)S(1)}, u32[]{:S(2)}, u32[]{:S(2)}) collective-permute-start(f32[3,64,256]{2,1,0:T(8,128)S(1)} %get-tuple-element.17), channel_id=1, source_target_pairs={{0,16},{16,32},{32,48},{48,64},{64,80},{80,96},{96,112},{112,128},... | collective-permute-start | bytes 589832 | tf_op jit(solution)/shard_map/ppermute | solution.py:625
  7.0 7.0 %collective-permute-start.1 = (f32[3,64,256]{2,1,0:T(8,128)S(1)}, f32[3,64,256]{2,1,0:T(8,128)S(1)}, u32[]{:S(2)}, u32[]{:S(2)}) collective-permute-start(f32[3,64,256]{2,1,0:T(8,128)S(1)} %get-tuple-element.18), channel_id=1, source_target_pairs={{16,0},{32,16},{48,32},{64,48},{80,64},{96,80},{112,96},{128,112},... | collective-permute-start | bytes 589832 | tf_op jit(solution)/shard_map/ppermute | solution.py:625
  14.0 1.0 %copy-start.1 = (f32[2,256,256]{2,1,0:T(8,128)S(1)}, f32[2,256,256]{2,1,0:T(8,128)}, u32[]{:S(2)}) copy-start(f32[2,256,256]{2,1,0:T(8,128)} %observed.5) | copy-start | bytes 1572868
  15.2 6.9 %collective-permute-start.2 = (f32[3,192,128]{2,1,0:T(8,128)S(1)}, f32[3,192,128]{2,1,0:T(8,128)S(1)}, u32[]{:S(2)}, u32[]{:S(2)}) collective-permute-start(f32[3,192,128]{2,1,0:T(8,128)S(1)} %get-tuple-element.19), channel_id=1, source_target_pairs={{0,1},{1,2},{2,3},{3,4},{4,5},{5,6},{6,7},{7,8},{8,9},{9,10},{10,1... | collective-permute-start | bytes 884744 | tf_op jit(solution)/shard_map/ppermute | solution.py:625
  18.5 7.7 %collective-permute-start.3 = (f32[3,192,128]{2,1,0:T(8,128)S(1)}, f32[3,192,128]{2,1,0:T(8,128)S(1)}, u32[]{:S(2)}, u32[]{:S(2)}) collective-permute-start(f32[3,192,128]{2,1,0:T(8,128)S(1)} %get-tuple-element.20), channel_id=1, source_target_pairs={{1,0},{2,1},{3,2},{4,3},{5,4},{6,5},{7,6},{8,7},{9,8},{10,9},{11,1... | collective-permute-start | bytes 884744 | tf_op jit(solution)/shard_map/ppermute | solution.py:625

commit v3 on v2

--- a/solution.py
+++ b/solution.py
@@ -116,58 +116,79 @@
     return (iota((24, 128), 0) + iota((24, 128), 1)) % 2 == 0
 
 
-def rows_kernel(observed, classes, own, top, bottom):
-    x = (classes[...] + 1).astype(F32)
-    own[...] = x
-    top[2] = x[:64]
-    bottom[2] = x[192:]
-    for f in range(2):
-        top[f] = observed[f, 0:64]
-        bottom[f] = observed[f, 192:256]
-
-
-def cols_kernel(observed, classes, north, south, left, right):
-    low = iota((192, 128), 1) < 64
+def place():
+    return lax.axis_index("row"), lax.axis_index("col")
+
+
+def fold(x, low, swap):
+    half = x.shape[0] // 2
+    first, second = x[:half], x[half:]
+    if swap:
+        return jnp.where(low, roll(second, 64, 1), first)
+    return jnp.where(low, first, roll(second, 64, 1))
+
+
+def sides_kernel(observed, classes, own, row_a, row_b, col_a, col_b):
+    row, col = place()
+    own[0:2] = observed[...]
+    own[2] = classes[...]
+    low = iota((128, 128), 1) < 64
     for f in range(3):
-        own = observed.at[f] if f < 2 else classes
-        sides = []
-        for c in (0, 128):
-            lanes = slice(c, c + 128)
-            b = jnp.concatenate([own[192:256, lanes], south[f, :, lanes], north[f, :, lanes]], axis=0)
-            sides.append((own[0:192, lanes], b))
-        left[f] = jnp.where(low, sides[0][0], roll(sides[0][1], 64, 1))
-        right[f] = jnp.where(low, roll(sides[1][1], 64, 1), sides[1][0])
+        x = own.at[f]
+        top, bottom = x[0:64, :], x[192:256, :]
+        row_a[f] = jnp.where(row % 2 == 0, bottom, top)
+        row_b[f] = jnp.where(row % 2 == 0, top, bottom)
+        left, right = fold(x[:, 0:128], low, False), fold(x[:, 128:256], low, True)
+        col_a[f] = jnp.where(col % 2 == 0, right, left)
+        col_b[f] = jnp.where(col % 2 == 0, left, right)
+
+
+def corners_kernel(row_a, row_b, out_a, out_b):
+    row, col = place()
+    low = iota((64, 128), 1) < 64
+    for f in range(3):
+        a, b = row_a[f], row_b[f]
+        south, north = jnp.where(row % 2 == 0, a, b), jnp.where(row % 2 == 0, b, a)
+        x = jnp.concatenate([south, north], axis=0)
+        left, right = fold(x[:, 0:128], low, False), fold(x[:, 128:256], low, True)
+        out_a[f] = jnp.where(col % 2 == 0, right, left)
+        out_b[f] = jnp.where(col % 2 == 0, left, right)
 
 
 def message_row(x, pattern, mine):
     return jnp.sum(jnp.where(mine, times(x, pattern), 0.0), axis=0, keepdims=True)
 
 
-def down_kernel(place, observed, classes, north, south, west, east, tables, *rest):
+def down_kernel(own, row_a, row_b, col_a, col_b, corner_a, corner_b, tables, *rest):
     saved = rest[:4]
     saved4, message = rest[4:6]
     states = rest[6:10]
-    gw, red, full, sums, frame, strip, nat, arrived, sent = rest[10:]
+    gw, red, full, sums, frame, side, corner, nat, arrived, sent = rest[10:]
+    row, col = place()
+    odd_row, odd_col = row % 2, col % 2
 
     pieces = []
     for f in range(3):
-        own = observed.at[f] if f < 2 else classes
         for half in range(2):
             lanes = pl.ds(half * 128, 128)
-            pieces.append((own.at[:, lanes], frame.at[f, half, pl.ds(0, 256), :]))
-            pieces.append((south.at[f, :, lanes], frame.at[f, half, pl.ds(256, 64), :]))
-            pieces.append((north.at[f, :, lanes], frame.at[f, half, pl.ds(320, 64), :]))
-    pieces += [(west, strip.at[0]), (east, strip.at[1])]
+            pieces.append((own.at[f, :, lanes], frame.at[f, half, pl.ds(0, 256), :]))
+            south = pl.ds(pl.multiple_of(256 + 64 * odd_row, 64), 64)
+            north = pl.ds(pl.multiple_of(320 - 64 * odd_row, 64), 64)
+            pieces.append((row_a.at[f, :, lanes], frame.at[f, half, south, :]))
+            pieces.append((row_b.at[f, :, lanes], frame.at[f, half, north, :]))
+    pieces += [(col_a, side.at[odd_col]), (col_b, side.at[1 - odd_col])]
+    pieces += [(corner_a, corner.at[odd_col]), (corner_b, corner.at[1 - odd_col])]
     copies = [pltpu.make_async_copy(a, b, arrived.at[i]) for i, (a, b) in enumerate(pieces)]
     for copy in copies:
         copy.start()
     for copy in copies:
         copy.wait()
-    low = iota((192, 128), 1) < 64
-    for f in range(3):
-        w, e = strip[0, f], strip[1, f]
-        frame[f, 2, 0:192, :] = jnp.where(low, e, w)
-        frame[f, 2, 192:384, :] = roll(jnp.where(low, w, e), 64, 1)
+    for ref, start, size in ((side, 0, 128), (corner, 256, 64)):
+        low = iota((size, 128), 1) < 64
+        for f in range(3):
+            e, w = ref[0, f], ref[1, f]
+            frame[f, 2, start : start + size, :] = jnp.where(low, e, w)
+            frame[f, 2, start + size : start + 2 * size, :] = roll(jnp.where(low, w, e), 64, 1)
 
     tab_g = jnp.broadcast_to(tables[0:1, :], (8, 128))
     tab_w = jnp.broadcast_to(tables[1:2, :], (8, 128))
@@ -180,7 +201,7 @@
         count, width = TILES[level] // 2, LANES[level]
         even = even_lanes((8, width))
         state = states[level]
-        unroll = (4, 4, 6, 3)[level]
+        unroll = (12, 12, 6, 3)[level]
         here = pl.ds(0, width)
 
         def pack(a, level=level, even=even, state=state, here=here):
@@ -295,7 +316,6 @@
         return carry
 
     lax.fori_loop(0, 32, send, 0)
-    row, col = place[0], place[1]
     for dr, dc, what in NEIGHBOURS:
         x = {-1: top, 1: bottom}.get(dr, left if dc < 0 else right)
         r, c = row + dr, col + dc
@@ -402,8 +422,8 @@
     lax.fori_loop(0, CG_ITERS, iterate, tuple(norm))
 
 
-def merged_frame(place, gathered, merged):
-    row, col = place[0], place[1]
+def merged_frame(gathered, merged):
+    row, col = place()
     at = iota((24, 128), 0)
     l = iota((24, 128), 1)
     total = {}
@@ -436,7 +456,7 @@
     return result
 
 
-def up_kernel(place, gathered, saved4, *rest):
+def up_kernel(gathered, saved4, *rest):
     saved, out = rest[:4], rest[4]
     states = rest[5:9]
     full, red, blk, kc, e, r, d, q, result, nat, arrived, sent = rest[9:]
@@ -445,21 +465,22 @@
         copy.start()
     cg(gathered, kc, e, r, d, q)
 
+    row, col = place()
     n = iota((24, 128), 1)
     at = iota((24, 128), 0)
     grid_row = (n // 64) * 64 + (n % 8) * 8 + (n // 8) % 8
-    rows = onehot(grid_row == place[0] * 8 + (jnp.where(at < 20, at, at - 24) >> 1))
+    rows = onehot(grid_row == row * 8 + (jnp.where(at < 20, at, at - 24) >> 1))
     j = iota((128, 128), 0)
     lane = iota((128, 128), 1)
     correction = 0.0
     for f in range(2):
         c = (lane + 32) % 128 - 32 - 64 * f
-        cols = onehot(jnp.logical_and(jnp.logical_and(c >= -32, c < 32), j == place[1] * 8 + (c >> 1)))
+        cols = onehot(jnp.logical_and(jnp.logical_and(c >= -32, c < 32), j == col * 8 + (c >> 1)))
         whole = jnp.concatenate([e[f, t] for t in range(16)], axis=0)
         correction += times(pick(rows, whole), cols)
 
     is_red = red4()
-    merged = merged_frame(place, gathered, saved4[0])
+    merged = merged_frame(gathered, saved4[0])
     k, inv = edges4(saved4[2], saved4[3])
     x = jnp.where(is_red, 0.0, merged + correction)
     x = jnp.where(is_red, (merged + pull4(k, x)) * inv, 0.0)
@@ -470,7 +491,7 @@
         count, width = TILES[level] // 2, LANES[level]
         even = even_lanes((8, width))
         state = states[level]
-        unroll = (4, 4, 6, 3)[level]
+        unroll = (12, 12, 6, 3)[level]
         here = pl.ds(0, width)
         if level == 3:
             lane, wide = iota((128, 128), 0), iota((128, 128), 1)
@@ -528,7 +549,6 @@
 
 VMEM = pl.BlockSpec(memory_space=pltpu.VMEM)
 ANY = pl.BlockSpec(memory_space=pl.ANY)
-SMEM = pl.BlockSpec(memory_space=pltpu.SMEM)
 PARAMS = pltpu.CompilerParams(vmem_limit_bytes=48 * 1024 * 1024)
 
 
@@ -544,33 +564,33 @@
     return [(STATE, TILES[level] // 2 + 2, 8, LANES[level]) for level in range(4)]
 
 
-def row_strips(observed, classes):
+def side_strips(observed, classes):
     return pl.pallas_call(
-        rows_kernel,
-        out_shape=[shaped(256, 256), shaped(3, 64, 256), shaped(3, 64, 256)],
+        sides_kernel,
+        out_shape=[shaped(3, 256, 256), shaped(3, 64, 256), shaped(3, 64, 256), shaped(3, 128, 128), shaped(3, 128, 128)],
         in_specs=[VMEM] * 2,
-        out_specs=[VMEM] * 3,
+        out_specs=[VMEM] * 5,
         compiler_params=PARAMS,
-        name="rows",
+        name="sides",
     )(observed, classes)
 
 
-def col_strips(observed, classes, north, south):
+def corner_strips(row_a, row_b):
     return pl.pallas_call(
-        cols_kernel,
-        out_shape=[shaped(3, 192, 128)] * 2,
-        in_specs=[VMEM] * 4,
+        corners_kernel,
+        out_shape=[shaped(3, 64, 128)] * 2,
+        in_specs=[VMEM] * 2,
         out_specs=[VMEM] * 2,
         compiler_params=PARAMS,
-        name="cols",
-    )(observed, classes, north, south)
-
-
-def down(place, observed, classes, north, south, west, east, tables):
+        name="corners",
+    )(row_a, row_b)
+
+
+def down(*args):
     return pl.pallas_call(
         down_kernel,
         out_shape=[shaped(*s) for s in state_shapes()] + [shaped(4, 24, 128), shaped(768, 128)],
-        in_specs=[SMEM] + [ANY] * 6 + [VMEM],
+        in_specs=[ANY] * 7 + [VMEM],
         out_specs=[ANY] * 4 + [VMEM] * 2,
         scratch_shapes=[scratch(*s) for s in state_shapes()]
         + [
@@ -579,21 +599,22 @@
             scratch(4, 24, 8, 256),
             scratch(4, 24, 8, 384),
             scratch(3, 3, 384, 128),
-            scratch(2, 3, 192, 128),
+            scratch(2, 3, 128, 128),
+            scratch(2, 3, 64, 128),
             scratch(5, 24, 128),
-            pltpu.SemaphoreType.DMA((20,)),
+            pltpu.SemaphoreType.DMA((22,)),
             pltpu.SemaphoreType.DMA((4,)),
         ],
         compiler_params=PARAMS,
         name="down",
-    )(place, observed, classes, north, south, west, east, tables)
-
-
-def up(place, gathered, saved4, saved):
+    )(*args)
+
+
+def up(gathered, saved4, saved):
     return pl.pallas_call(
         up_kernel,
         out_shape=shaped(2, 256, 256),
-        in_specs=[SMEM] + [VMEM] * 2 + [ANY] * 4,
+        in_specs=[VMEM] * 2 + [ANY] * 4,
         out_specs=ANY,
         scratch_shapes=[scratch(*s) for s in state_shapes()]
         + [
@@ -612,7 +633,7 @@
         ],
         compiler_params=PARAMS,
         name="up",
-    )(place, gathered, saved4, *saved)
+    )(gathered, saved4, *saved)
 
 
 def make_tables(class_weight, class_stiffness):
@@ -620,23 +641,21 @@
     return jnp.stack([pad(0.5 * class_stiffness, FAR), pad(class_weight, 0.0)])
 
 
-def send(x, axis, step):
-    count = lax.axis_size(axis)
-    return lax.ppermute(x, axis, [(i, i + step) for i in range(count) if 0 <= i + step < count])
+def swap(x, axis, first):
+    pairs = [(i, i + 1) for i in range(first, lax.axis_size(axis) - 1, 2)]
+    return lax.ppermute(x, axis, pairs + [(j, i) for i, j in pairs])
 
 
 def local(observed, coherence_class, class_weight, class_stiffness):
-    place = jnp.stack([lax.axis_index("row"), lax.axis_index("col")]).astype(jnp.int32)
-    classes, top, bottom = row_strips(observed, coherence_class)
-    north = send(bottom, "row", 1)
-    south = send(top, "row", -1)
-    left, right = col_strips(observed, classes, north, south)
-    west = send(right, "col", 1)
-    east = send(left, "col", -1)
+    own, row_a, row_b, col_a, col_b = side_strips(observed, (coherence_class + 1).astype(F32))
+    row_a, row_b = swap(row_a, "row", 0), swap(row_b, "row", 1)
+    col_a, col_b = swap(col_a, "col", 0), swap(col_b, "col", 1)
+    corner_a, corner_b = corner_strips(row_a, row_b)
+    corner_a, corner_b = swap(corner_a, "col", 0), swap(corner_b, "col", 1)
     tables = make_tables(class_weight, class_stiffness)
-    *saved, saved4, message = down(place, observed, classes, north, south, west, east, tables)
+    *saved, saved4, message = down(own, row_a, row_b, col_a, col_b, corner_a, corner_b, tables)
     gathered = lax.all_to_all(message.reshape(256, 1, 384), ("row", "col"), 0, 0).reshape(768, 128)
-    return up(place, gathered, saved4, saved)
+    return up(gathered, saved4, saved)
 
 
 def solution(mesh):

time: 83.6 us -> 71.4 us (0.85)
  waiting for transfers between devices: 10 us -> 3.45 us
  Pallas kernels: 21 us -> 17.6 us
  starting transfers between devices: 11.4 us -> 9.26 us
  local copies, waits for them, and re-layouts: 3.03 us -> 1.04 us
  blocking collectives: 36.3 us -> 37.3 us
  other arithmetic: 1.48 us -> 2.37 us
    ppermute x4 -> x6, waiting for transfers between devices: 10 us -> 3.45 us  [swap(): return lax.ppermute(x, axis, pairs + [(j, i) for i, j in pairs])]
    ppermute x4 -> x6, starting transfers between devices: 11.4 us -> 9.26 us  [swap(): return lax.ppermute(x, axis, pairs + [(j, i) for i, j in pairs])]
    unnamed x6 -> x2, local copies, waits for them, and re-layouts: 3.03 us -> 1.04 us
    pallas_call x1, Pallas kernels: 9.12 us -> 7.3 us  [down(): pl.pallas_call(down_kernel, out_shape=[shaped(*s) for s in state_shapes()...]
    pallas_call x3, Pallas kernels: 11.9 us -> 10.3 us  [the longest x1 10 us: up(): pl.pallas_call(up_kernel, out_shape=shaped(2, 256, 256), in_specs=[VMEM]...]
    all_to_all x1, blocking collectives: 36.3 us -> 37.3 us  [local(): lax.all_to_all(message.reshape(256, 1, 384), ('row', 'col'), 0, 0)]
    convert_element_type x0 -> x1, other arithmetic: none -> 0.97 us  [local(): (coherence_class + 1).astype(F32)]
  transfers between devices with their start and end apart: 4 -> 6, of which waited for: 3 -> 2; matrix products, arithmetic and copies ran while one was open for 2% -> 2% of each run, Pallas kernels for 0% -> 0%
where the time goes in v3:
time: 71.4 us; the launch traced here: 71.1 us
  blocking collectives  37.3 us (52%)
  Pallas kernels  17.6 us (25%)
  starting transfers between devices  9.26 us (13%)
  waiting for transfers between devices  3.45 us (5%)
  other arithmetic  2.37 us (3%)
  local copies, waits for them, and re-layouts  1.04 us (1%)
    all_to_all x1, blocking collectives, local(): lax.all_to_all(message.reshape(256, 1, 384), ('row', 'col'), 0, 0)  37.3 us
    pallas_call x1, Pallas kernels, up(): pl.pallas_call(up_kernel, out_shape=shaped(2, 256, 256), in_specs=[VMEM]...  10 us
    ppermute x6, starting transfers between devices, swap(): return lax.ppermute(x, axis, pairs + [(j, i) for i, j in pairs])  9.26 us
    pallas_call x1, Pallas kernels, down(): pl.pallas_call(down_kernel, out_shape=[shaped(*s) for s in state_shapes()...  7.3 us
    ppermute x6, waiting for transfers between devices, swap(): return lax.ppermute(x, axis, pairs + [(j, i) for i, j in pairs])  3.45 us
  transfers between devices with their start and end apart: 6, of which 2 were waited for; matrix products, arithmetic and copies ran while one was open for 2% of the time, Pallas kernels for 0%

profile of v3, /device:TPU:1, one launch (start us, length us, event | category | flops | bytes accessed | tf_op | source)
XLA Modules:
  0.0 71.1 jit_solution(4786533374659968138)
XLA Ops:
  0.0 1.0 %add_convert_fusion.classes = f32[256,256]{1,0:T(8,128)S(1)} fusion(s32[256,256]{1,0:T(8,128)} %param.5), kind=kLoop, calls=%fused_computation | loop fusion | flops 131072 | bytes 524288 | tf_op jit(solution)/shard_map/convert_element_type | solution.py:650
  1.0 0.0 copy-start
  1.0 1.0 %copy-done = f32[2,256,256]{2,1,0:T(8,128)S(1)} copy-done((f32[2,256,256]{2,1,0:T(8,128)S(1)}, f32[2,256,256]{2,1,0:T(8,128)}, u32[]{:S(2)}) %copy-start) | copy-done | bytes 524312
  2.0 0.2 sides.1
  2.2 3.3 %collective-permute-start = (f32[3,64,256]{2,1,0:T(8,128)S(1)}, f32[3,64,256]{2,1,0:T(8,128)S(1)}, u32[]{:S(2)}, u32[]{:S(2)}) collective-permute-start(f32[3,64,256]{2,1,0:T(8,128)S(1)} %get-tuple-element.19), channel_id=1, source_target_pairs={{0,16},{32,48},{64,80},{96,112},{128,144},{160,176},{192,208},{224... | collective-permute-start | bytes 589832 | tf_op jit(solution)/shard_map/ppermute | solution.py:646
  5.5 1.9 %collective-permute-start.1 = (f32[3,64,256]{2,1,0:T(8,128)S(1)}, f32[3,64,256]{2,1,0:T(8,128)S(1)}, u32[]{:S(2)}, u32[]{:S(2)}) collective-permute-start(f32[3,64,256]{2,1,0:T(8,128)S(1)} %get-tuple-element.20), channel_id=1, source_target_pairs={{16,32},{48,64},{80,96},{112,128},{144,160},{176,192},{208,224},{3... | collective-permute-start | bytes 589832 | tf_op jit(solution)/shard_map/ppermute | solution.py:646
  7.4 1.2 %collective-permute-start.2 = (f32[3,128,128]{2,1,0:T(8,128)S(1)}, f32[3,128,128]{2,1,0:T(8,128)S(1)}, u32[]{:S(2)}, u32[]{:S(2)}) collective-permute-start(f32[3,128,128]{2,1,0:T(8,128)S(1)} %get-tuple-element.21), channel_id=1, source_target_pairs={{0,1},{2,3},{4,5},{6,7},{8,9},{10,11},{12,13},{14,15},{1,0},{3,2},... | collective-permute-start | bytes 589832 | tf_op jit(solution)/shard_map/ppermute | solution.py:646
  8.6 0.7 collective-permute-start.3
  9.3 0.7 broadcast_multiply_fusion
  10.0 0.7 %fusion = (f32[1,128]{1,0:T(1,128)S(1)}, f32[1,128]{1,0:T(1,128)S(1)}) fusion(f32[8]{0:T(128)} %param.6, f32[1]{0:T(128)} %constant.10.clone.1, f32[8]{0:T(128)S(1)} %broadcast_multiply_fusion, f32[1]{0:T(128)} %constant.2.clone.1), kind=kLoop, calls=%fused_computation.3 | loop fusion | flops 896 | bytes 1096 | tf_op jit(solution)/shard_map/stack | solution.py:641
  10.7 0.0 collective-permute-done.row_a
  10.7 2.1 %collective-permute-done.1.row_b = f32[3,64,256]{2,1,0:T(8,128)S(1)} collective-permute-done((f32[3,64,256]{2,1,0:T(8,128)S(1)}, f32[3,64,256]{2,1,0:T(8,128)S(1)}, u32[]{:S(2)}, u32[]{:S(2)}) %collective-permute-start.1) | collective-permute-done | bytes 196640 | tf_op jit(solution)/shard_map/ppermute | solution.py:646
  12.8 0.1 corners.1
  12.9 1.5 %collective-permute-start.4 = (f32[3,64,128]{2,1,0:T(8,128)S(1)}, f32[3,64,128]{2,1,0:T(8,128)S(1)}, u32[]{:S(2)}, u32[]{:S(2)}) collective-permute-start(f32[3,64,128]{2,1,0:T(8,128)S(1)} %get-tuple-element.23), channel_id=1, source_target_pairs={{0,1},{2,3},{4,5},{6,7},{8,9},{10,11},{12,13},{14,15},{1,0},{3,2},... | collective-permute-start | bytes 294920 | tf_op jit(solution)/shard_map/ppermute | solution.py:646
  14.5 0.7 collective-permute-start.5
  15.1 0.0 collective-permute-done.2.col_a
  15.1 0.0 collective-permute-done.3.col_b
  15.2 1.3 %collective-permute-done.4.corner_a = f32[3,64,128]{2,1,0:T(8,128)S(1)} collective-permute-done((f32[3,64,128]{2,1,0:T(8,128)S(1)}, f32[3,64,128]{2,1,0:T(8,128)S(1)}, u32[]{:S(2)}, u32[]{:S(2)}) %collective-permute-start.4) | collective-permute-done | bytes 98336 | tf_op jit(solution)/shard_map/ppermute | solution.py:646
  16.5 0.0 collective-permute-done.5.corner_b
  16.5 7.3 %down.1 = (f32[13,26,8,384]{3,2,1,0:T(8,128)}, f32[13,14,8,256]{3,2,1,0:T(8,128)S(1)}, f32[13,8,8,128]{3,2,1,0:T(8,128)S(1)}, f32[13,5,8,128]{3,2,1,0:T(8,128)S(...) custom-call(f32[3,256,256]{2,1,0:T(8,128)S(1)} %get-tuple-element.18.own, ...), custom_call_target="tpu_custom_call" | custom-call | tf_op jit(solution)/shard_map/down/pallas_call | solution.py:590
  23.8 37.3 %all_to_all.5 = f32[256,1,384]{2,1,0:T(1,128)S(1)} all-to-all(f32[256,1,384]{2,1,0:T(1,128)S(1)} %bitcast.7), channel_id=1, replica_groups=mesh['row'=16,'col'=16] {'row','col'}, dimensions={0} | all-to-all | bytes 786432 | tf_op jit(solution)/shard_map/all_to_all | solution.py:657
  61.1 10.0 %up.1 = f32[2,256,256]{2,1,0:T(8,128)} custom-call(f32[768,128]{1,0:T(8,128)S(1)} %bitcast.6, f32[4,24,128]{2,1,0:T(8,128)S(1)} %get-tuple-element.26.saved4, f32[13,26,8,384]{3,2,1,0:T(8,128)} %get-tuple-element.27.rest_0_, f32[13,14,8,256]{3,2,1,0:T(8,128)S(1)} %get-tuple-element.28.rest_1_, f32[13,8,8,128]{3,2,1,0:T(8,128)S(1)} %get-tuple-element.29.rest_2_, ...), custom_call_target="tpu_custom_call" | custom-call | tf_op jit(solution)/shard_map/up/pallas_call | solution.py:614
  (1 shorter events, 0.0 us)
Async XLA Ops:
  1.0 1.0 %copy-start = (f32[2,256,256]{2,1,0:T(8,128)S(1)}, f32[2,256,256]{2,1,0:T(8,128)}, u32[]{:S(2)}) copy-start(f32[2,256,256]{2,1,0:T(8,128)} %observed.1) | copy-start | bytes 1572868
  2.2 8.5 %collective-permute-start = (f32[3,64,256]{2,1,0:T(8,128)S(1)}, f32[3,64,256]{2,1,0:T(8,128)S(1)}, u32[]{:S(2)}, u32[]{:S(2)}) collective-permute-start(f32[3,64,256]{2,1,0:T(8,128)S(1)} %get-tuple-element.19), channel_id=1, source_target_pairs={{0,16},{32,48},{64,80},{96,112},{128,144},{160,176},{192,208},{224... | collective-permute-start | bytes 589832 | tf_op jit(solution)/shard_map/ppermute | solution.py:646
  5.5 7.3 %collective-permute-start.1 = (f32[3,64,256]{2,1,0:T(8,128)S(1)}, f32[3,64,256]{2,1,0:T(8,128)S(1)}, u32[]{:S(2)}, u32[]{:S(2)}) collective-permute-start(f32[3,64,256]{2,1,0:T(8,128)S(1)} %get-tuple-element.20), channel_id=1, source_target_pairs={{16,32},{48,64},{80,96},{112,128},{144,160},{176,192},{208,224},{3... | collective-permute-start | bytes 589832 | tf_op jit(solution)/shard_map/ppermute | solution.py:646
  7.4 7.7 %collective-permute-start.2 = (f32[3,128,128]{2,1,0:T(8,128)S(1)}, f32[3,128,128]{2,1,0:T(8,128)S(1)}, u32[]{:S(2)}, u32[]{:S(2)}) collective-permute-start(f32[3,128,128]{2,1,0:T(8,128)S(1)} %get-tuple-element.21), channel_id=1, source_target_pairs={{0,1},{2,3},{4,5},{6,7},{8,9},{10,11},{12,13},{14,15},{1,0},{3,2},... | collective-permute-start | bytes 589832 | tf_op jit(solution)/shard_map/ppermute | solution.py:646
  8.6 6.5 %collective-permute-start.3 = (f32[3,128,128]{2,1,0:T(8,128)S(1)}, f32[3,128,128]{2,1,0:T(8,128)S(1)}, u32[]{:S(2)}, u32[]{:S(2)}) collective-permute-start(f32[3,128,128]{2,1,0:T(8,128)S(1)} %get-tuple-element.22), channel_id=1, source_target_pairs={{1,2},{3,4},{5,6},{7,8},{9,10},{11,12},{13,14},{2,1},{4,3},{6,5},{... | collective-permute-start | bytes 589832 | tf_op jit(solution)/shard_map/ppermute | solution.py:646
  12.9 3.6 %collective-permute-start.4 = (f32[3,64,128]{2,1,0:T(8,128)S(1)}, f32[3,64,128]{2,1,0:T(8,128)S(1)}, u32[]{:S(2)}, u32[]{:S(2)}) collective-permute-start(f32[3,64,128]{2,1,0:T(8,128)S(1)} %get-tuple-element.23), channel_id=1, source_target_pairs={{0,1},{2,3},{4,5},{6,7},{8,9},{10,11},{12,13},{14,15},{1,0},{3,2},... | collective-permute-start | bytes 294920 | tf_op jit(solution)/shard_map/ppermute | solution.py:646
  14.5 2.0 %collective-permute-start.5 = (f32[3,64,128]{2,1,0:T(8,128)S(1)}, f32[3,64,128]{2,1,0:T(8,128)S(1)}, u32[]{:S(2)}, u32[]{:S(2)}) collective-permute-start(f32[3,64,128]{2,1,0:T(8,128)S(1)} %get-tuple-element.24), channel_id=1, source_target_pairs={{1,2},{3,4},{5,6},{7,8},{9,10},{11,12},{13,14},{2,1},{4,3},{6,5},{... | collective-permute-start | bytes 294920 | tf_op jit(solution)/shard_map/ppermute | solution.py:646

commit v4 on v3

--- a/solution.py
+++ b/solution.py
@@ -159,67 +159,89 @@
     return jnp.sum(jnp.where(mine, times(x, pattern), 0.0), axis=0, keepdims=True)
 
 
-def down_kernel(own, row_a, row_b, col_a, col_b, corner_a, corner_b, tables, *rest):
-    saved = rest[:4]
-    saved4, message = rest[4:6]
-    states = rest[6:10]
-    gw, red, full, sums, frame, side, corner, nat, arrived, sent = rest[10:]
-    row, col = place()
-    odd_row, odd_col = row % 2, col % 2
-
-    pieces = []
+def class_tables(table):
+    lane = iota((8, 128), 1)
+    g, w = jnp.full((8, 128), FAR, F32), jnp.zeros((8, 128), F32)
+    for i in range(8):
+        g = jnp.where(lane == i + 1, 0.5 * table[8 + i], g)
+        w = jnp.where(lane == i + 1, table[i], w)
+    return g, w
+
+
+def interleave(x, y, even):
+    return jnp.where(even, x, y), jnp.where(even, y, x)
+
+
+def middle_kernel(own, row_a, row_b, table, rhs, gw, frame):
+    row, _ = place()
     for f in range(3):
         for half in range(2):
-            lanes = pl.ds(half * 128, 128)
-            pieces.append((own.at[f, :, lanes], frame.at[f, half, pl.ds(0, 256), :]))
-            south = pl.ds(pl.multiple_of(256 + 64 * odd_row, 64), 64)
-            north = pl.ds(pl.multiple_of(320 - 64 * odd_row, 64), 64)
-            pieces.append((row_a.at[f, :, lanes], frame.at[f, half, south, :]))
-            pieces.append((row_b.at[f, :, lanes], frame.at[f, half, north, :]))
-    pieces += [(col_a, side.at[odd_col]), (col_b, side.at[1 - odd_col])]
-    pieces += [(corner_a, corner.at[odd_col]), (corner_b, corner.at[1 - odd_col])]
-    copies = [pltpu.make_async_copy(a, b, arrived.at[i]) for i, (a, b) in enumerate(pieces)]
-    for copy in copies:
-        copy.start()
-    for copy in copies:
-        copy.wait()
-    for ref, start, size in ((side, 0, 128), (corner, 256, 64)):
+            lanes = slice(half * 128, half * 128 + 128)
+            x, y = row_a[f, :, lanes], row_b[f, :, lanes]
+            frame[f, half, 0:256, :] = own[f, :, lanes]
+            frame[f, half, 256:320, :] = jnp.where(row % 2 == 0, x, y)
+            frame[f, half, 320:384, :] = jnp.where(row % 2 == 0, y, x)
+    tables = class_tables(table)
+    even = even_lanes((8, 256))
+
+    def tile(f, a):
+        return jnp.concatenate([frame[f, c, pl.ds(a, 8, stride=48), :] for c in range(2)], axis=1)
+
+    def pack(a):
+        for f in range(2):
+            rhs[f, a], rhs[2 + f, a] = interleave(tile(f, 2 * a), tile(f, 2 * a + 1), even)
+        i, j = (tile(2, 2 * a + k).astype(jnp.int32) for k in range(2))
+        for q in range(2):
+            gw[2 * q, a], gw[2 * q + 1, a] = interleave(lookup(tables[q], i), lookup(tables[q], j), even)
+
+    loop(24, pack, 12)
+
+
+def down_kernel(rhs0, gw0, col_a, col_b, corner_a, corner_b, table, *rest):
+    states = rest[:4]
+    saved4, message = rest[4:6]
+    gw, red, full, sums, frame, nat = rest[6:]
+    row, col = place()
+    even_col = col % 2 == 0
+
+    for a, b, start, size in ((col_a, col_b, 0, 128), (corner_a, corner_b, 256, 64)):
         low = iota((size, 128), 1) < 64
         for f in range(3):
-            e, w = ref[0, f], ref[1, f]
-            frame[f, 2, start : start + size, :] = jnp.where(low, e, w)
-            frame[f, 2, start + size : start + 2 * size, :] = roll(jnp.where(low, w, e), 64, 1)
-
-    tab_g = jnp.broadcast_to(tables[0:1, :], (8, 128))
-    tab_w = jnp.broadcast_to(tables[1:2, :], (8, 128))
-
-    def frame_tile(f, a):
-        return jnp.concatenate([frame[f, c, pl.ds(a, 8, stride=48), :] for c in range(3)], axis=1)
-
-    outgoing = []
+            x, y = a[f], b[f]
+            e, w = jnp.where(even_col, x, y), jnp.where(even_col, y, x)
+            frame[f, start : start + size, :] = jnp.where(low, e, w)
+            frame[f, start + size : start + 2 * size, :] = roll(jnp.where(low, w, e), 64, 1)
+    tables = class_tables(table)
+    narrow = even_lanes((8, 128))
+
+    def side_tile(f, a):
+        return frame[f, pl.ds(a, 8, stride=48), :]
+
     for level in range(4):
         count, width = TILES[level] // 2, LANES[level]
         even = even_lanes((8, width))
         state = states[level]
-        unroll = (12, 12, 6, 3)[level]
+        unroll = (24, 12, 6, 3)[level]
         here = pl.ds(0, width)
 
         def pack(a, level=level, even=even, state=state, here=here):
-            for f in range(2):
-                if level == 0:
-                    x, y = frame_tile(f, 2 * a), frame_tile(f, 2 * a + 1)
-                else:
-                    x, y = full[f, 2 * a, :, here], full[f, 2 * a + 1, :, here]
-                state[f, a + 1] = jnp.where(even, x, y)
-                state[2 + f, a + 1] = jnp.where(even, y, x)
             if level == 0:
-                i, j = (frame_tile(2, 2 * a + k).astype(jnp.int32) for k in range(2))
-                pairs = ((lookup(tab_g, i), lookup(tab_g, j)), (lookup(tab_w, i), lookup(tab_w, j)))
+                for f in range(2):
+                    x = interleave(side_tile(f, 2 * a), side_tile(f, 2 * a + 1), narrow)
+                    for k in range(2):
+                        state[2 * k + f, a + 1] = jnp.concatenate([rhs0[2 * k + f, a], x[k]], axis=1)
+                i, j = (side_tile(2, 2 * a + k).astype(jnp.int32) for k in range(2))
+                for q in range(2):
+                    x = interleave(lookup(tables[q], i), lookup(tables[q], j), narrow)
+                    for k in range(2):
+                        gw[2 * q + k, a + 1] = jnp.concatenate([gw0[2 * q + k, a], x[k]], axis=1)
             else:
-                pairs = tuple((full[q, 2 * a, :, here], full[q, 2 * a + 1, :, here]) for q in (2, 3))
-            for q, (x, y) in enumerate(pairs):
-                gw[2 * q, a + 1, :, here] = jnp.where(even, x, y)
-                gw[2 * q + 1, a + 1, :, here] = jnp.where(even, y, x)
+                for f in range(2):
+                    x = interleave(full[f, 2 * a, :, here], full[f, 2 * a + 1, :, here], even)
+                    state[f, a + 1], state[2 + f, a + 1] = x
+                for q in range(2):
+                    x = interleave(full[2 + q, 2 * a, :, here], full[2 + q, 2 * a + 1, :, here], even)
+                    gw[2 * q, a + 1, :, here], gw[2 * q + 1, a + 1, :, here] = x
 
         loop(count, pack, unroll)
         for q in range(2):
@@ -255,8 +277,6 @@
         loop(count, first_black, unroll)
         for f in range(2):
             ends(state, BLACK + f, count)
-        outgoing.append(pltpu.make_async_copy(state, saved[level], sent.at[level]))
-        outgoing[-1].start()
 
         def restrict(a, even=even, state=state, here=here):
             for f in range(2):
@@ -324,14 +344,11 @@
         def _(r=r, c=c, x=x):
             message[pl.ds((r * 16 + c) * 3 + 2, 1), :] = x
 
-    for copy in outgoing:
-        copy.wait()
-
 
 NEIGHBOURS = [(dr, dc, None) for dr in (-1, 0, 1) for dc in (-1, 0, 1) if dr or dc]
 
 
-def cg(gathered, kc, e, r, d, q):
+def cg(gathered, kc, e, d, s, w, r):
     lane = iota((8, 128), 1)
     sub = iota((8, 128), 0)
     group = lane // 8
@@ -377,49 +394,57 @@
         kc[3, t] = right
         kc[4, t] = arrays[3][t] + up + down + left + right
 
-    norm = []
+    def sums(f):
+        x = [r[f, t] for t in range(16)]
+        tile = lambda i: x[i]
+        total, norm = 0.0, 0.0
+        for t in range(16):
+            image = kc[4, t] * x[t] - (
+                kc[0, t] * north(tile, t)
+                + kc[1, t] * south(tile, t)
+                + kc[2, t] * roll(x[t], 1, 1)
+                + kc[3, t] * roll(x[t], -1, 1)
+            )
+            w[f, t] = image
+            norm += x[t] * x[t]
+            total += x[t] * image
+        return tuple(jnp.sum(y, axis=(0, 1), keepdims=True) for y in (norm, total))
+
+    state = []
     for f in range(2):
-        total = 0.0
         for t in range(16):
             x = arrays[f][t]
             e[f, t] = jnp.zeros_like(x)
+            d[f, t] = jnp.zeros_like(x)
+            s[f, t] = jnp.zeros_like(x)
             r[f, t] = x
-            d[f, t] = x
-            total += x * x
-        norm.append(jnp.sum(total, axis=(0, 1), keepdims=True))
-
-    def iterate(_, norm):
-        alpha = []
+    for f in range(2):
+        norm, total = sums(f)
+        state.append((norm, norm / total, jnp.zeros_like(norm)))
+
+    def iterate(_, state):
         for f in range(2):
-            tile = lambda i, f=f: d[f, i]
-            total = 0.0
+            norm, alpha, beta = state[f]
             for t in range(16):
-                x = d[f, t]
-                image = kc[4, t] * x - (
-                    kc[0, t] * north(tile, t)
-                    + kc[1, t] * south(tile, t)
-                    + kc[2, t] * roll(x, 1, 1)
-                    + kc[3, t] * roll(x, -1, 1)
-                )
-                q[f, t] = image
-                total += x * image
-            alpha.append(norm[f] / jnp.sum(total, axis=(0, 1), keepdims=True))
-        fresh = []
+                x = r[f, t] + beta * d[f, t]
+                y = w[f, t] + beta * s[f, t]
+                d[f, t] = x
+                s[f, t] = y
+                e[f, t] = e[f, t] + alpha * x
+                r[f, t] = r[f, t] - alpha * y
+        result = []
+        fresh = [sums(f) for f in range(2)]
         for f in range(2):
-            total = 0.0
-            for t in range(16):
-                e[f, t] = e[f, t] + alpha[f] * d[f, t]
-                x = r[f, t] - alpha[f] * q[f, t]
-                r[f, t] = x
-                total += x * x
-            fresh.append(jnp.sum(total, axis=(0, 1), keepdims=True))
-        for f in range(2):
-            beta = fresh[f] / norm[f]
-            for t in range(16):
-                d[f, t] = r[f, t] + beta * d[f, t]
-        return tuple(fresh)
-
-    lax.fori_loop(0, CG_ITERS, iterate, tuple(norm))
+            norm, alpha, _ = state[f]
+            beta = fresh[f][0] / norm
+            result.append((fresh[f][0], fresh[f][0] / (fresh[f][1] - beta * fresh[f][0] / alpha), beta))
+        return tuple(result)
+
+    state = lax.fori_loop(0, CG_ITERS - 1, iterate, tuple(state))
+    for f in range(2):
+        _, alpha, beta = state[f]
+        for t in range(16):
+            e[f, t] = e[f, t] + alpha * (r[f, t] + beta * d[f, t])
 
 
 def merged_frame(gathered, merged):
@@ -457,13 +482,9 @@
 
 
 def up_kernel(gathered, saved4, *rest):
-    saved, out = rest[:4], rest[4]
-    states = rest[5:9]
-    full, red, blk, kc, e, r, d, q, result, nat, arrived, sent = rest[9:]
-    copies = [pltpu.make_async_copy(saved[level], states[level], arrived.at[level]) for level in range(4)]
-    for copy in copies[::-1]:
-        copy.start()
-    cg(gathered, kc, e, r, d, q)
+    states, out = rest[:4], rest[4]
+    full, red, blk, kc, e, d, s, w, r, result, nat, sent = rest[5:]
+    cg(gathered, kc, e, d, s, w, r)
 
     row, col = place()
     n = iota((24, 128), 1)
@@ -491,7 +512,7 @@
         count, width = TILES[level] // 2, LANES[level]
         even = even_lanes((8, width))
         state = states[level]
-        unroll = (12, 12, 6, 3)[level]
+        unroll = (24, 12, 6, 3)[level]
         here = pl.ds(0, width)
         if level == 3:
             lane, wide = iota((128, 128), 0), iota((128, 128), 1)
@@ -503,7 +524,6 @@
             corrections = [
                 times(full[f, 0:count, :, pl.ds(0, coarse)].reshape(count * 8, coarse), pattern) for f in range(2)
             ]
-        copies[level].wait()
         for f in range(2):
             blk[f, 1 : count + 1, :, here] = state[BLACK + f, 1 : count + 1] + corrections[f].reshape(count, 8, width)
             blk[f, 0, :, here] = roll(blk[f, count, :, here], 1, 0)
@@ -519,9 +539,9 @@
             red[f, 0, :, here] = roll(red[f, count, :, here], 1, 0)
             red[f, count + 1, :, here] = roll(red[f, 1, :, here], -1, 0)
 
-        def second_black(a, level=level, even=even, state=state, here=here):
+        def second_black(a, fields=(0, 1), level=level, even=even, state=state, here=here):
             view = red.at[:, :, :, here]
-            for f in range(2):
+            for f in fields:
                 x = red[f, a + 1, :, here]
                 y = (state[2 + f, a + 1] + pull_black(a, view, f, state, even)) * state[INV + 1, a + 1]
                 first, second = jnp.where(even, x, y), jnp.where(even, y, x)
@@ -534,22 +554,24 @@
                         result[f, half, pl.ds(2 * a, 8, stride=48), :] = first[:, lanes]
                         result[f, half, pl.ds(2 * a + 1, 8, stride=48), :] = second[:, lanes]
 
-        loop(count, second_black, unroll)
+        if level:
+            loop(count, second_black, unroll)
 
     copies = []
     for f in range(2):
+        loop(24, lambda a, f=f: second_black(a, (f,)), 24)
         for half in range(2):
             source = result.at[f, half, pl.ds(0, 256), :]
             copies.append(pltpu.make_async_copy(source, out.at[f, :, pl.ds(half * 128, 128)], sent.at[2 * f + half]))
-    for copy in copies:
-        copy.start()
+            copies[-1].start()
     for copy in copies:
         copy.wait()
 
 
 VMEM = pl.BlockSpec(memory_space=pltpu.VMEM)
 ANY = pl.BlockSpec(memory_space=pl.ANY)
-PARAMS = pltpu.CompilerParams(vmem_limit_bytes=48 * 1024 * 1024)
+SMEM = pl.BlockSpec(memory_space=pltpu.SMEM)
+PARAMS = pltpu.CompilerParams(vmem_limit_bytes=24 * 1024 * 1024)
 
 
 def shaped(*shape):
@@ -586,24 +608,31 @@
     )(row_a, row_b)
 
 
+def middle(own, row_a, row_b, table):
+    return pl.pallas_call(
+        middle_kernel,
+        out_shape=[shaped(4, 24, 8, 256)] * 2,
+        in_specs=[VMEM] * 3 + [SMEM],
+        out_specs=[VMEM] * 2,
+        scratch_shapes=[scratch(3, 2, 384, 128)],
+        compiler_params=PARAMS,
+        name="middle",
+    )(own, row_a, row_b, table)
+
+
 def down(*args):
     return pl.pallas_call(
         down_kernel,
         out_shape=[shaped(*s) for s in state_shapes()] + [shaped(4, 24, 128), shaped(768, 128)],
-        in_specs=[ANY] * 7 + [VMEM],
-        out_specs=[ANY] * 4 + [VMEM] * 2,
-        scratch_shapes=[scratch(*s) for s in state_shapes()]
-        + [
+        in_specs=[VMEM] * 6 + [SMEM],
+        out_specs=[VMEM] * 6,
+        scratch_shapes=[
             scratch(4, 26, 8, 384),
             scratch(2, 26, 8, 384),
             scratch(4, 24, 8, 256),
             scratch(4, 24, 8, 384),
-            scratch(3, 3, 384, 128),
-            scratch(2, 3, 128, 128),
-            scratch(2, 3, 64, 128),
+            scratch(3, 384, 128),
             scratch(5, 24, 128),
-            pltpu.SemaphoreType.DMA((22,)),
-            pltpu.SemaphoreType.DMA((4,)),
         ],
         compiler_params=PARAMS,
         name="down",
@@ -614,10 +643,9 @@
     return pl.pallas_call(
         up_kernel,
         out_shape=shaped(2, 256, 256),
-        in_specs=[VMEM] * 2 + [ANY] * 4,
+        in_specs=[VMEM] * 6,
         out_specs=ANY,
-        scratch_shapes=[scratch(*s) for s in state_shapes()]
-        + [
+        scratch_shapes=[
             scratch(2, 24, 8, 256),
             scratch(2, 26, 8, 384),
             scratch(2, 26, 8, 384),
@@ -626,9 +654,9 @@
             scratch(2, 16, 8, 128),
             scratch(2, 16, 8, 128),
             scratch(2, 16, 8, 128),
+            scratch(2, 16, 8, 128),
             scratch(2, 2, 384, 128),
             scratch(24, 128),
-            pltpu.SemaphoreType.DMA((4,)),
             pltpu.SemaphoreType.DMA((4,)),
         ],
         compiler_params=PARAMS,
@@ -636,11 +664,6 @@
     )(gathered, saved4, *saved)
 
 
-def make_tables(class_weight, class_stiffness):
-    pad = lambda x, first: jnp.pad(jnp.concatenate([jnp.full((1,), first, F32), x]), (0, 119))
-    return jnp.stack([pad(0.5 * class_stiffness, FAR), pad(class_weight, 0.0)])
-
-
 def swap(x, axis, first):
     pairs = [(i, i + 1) for i in range(first, lax.axis_size(axis) - 1, 2)]
     return lax.ppermute(x, axis, pairs + [(j, i) for i, j in pairs])
@@ -651,9 +674,13 @@
     row_a, row_b = swap(row_a, "row", 0), swap(row_b, "row", 1)
     col_a, col_b = swap(col_a, "col", 0), swap(col_b, "col", 1)
     corner_a, corner_b = corner_strips(row_a, row_b)
+    held = lax.optimization_barrier((corner_a, corner_b, own, row_a, row_b, class_weight, class_stiffness))
+    corner_a, corner_b, own, row_a, row_b, class_weight, class_stiffness = held
     corner_a, corner_b = swap(corner_a, "col", 0), swap(corner_b, "col", 1)
-    tables = make_tables(class_weight, class_stiffness)
-    *saved, saved4, message = down(own, row_a, row_b, col_a, col_b, corner_a, corner_b, tables)
+    table = jnp.concatenate([class_weight, class_stiffness])
+    rhs, gw = middle(own, row_a, row_b, table)
+    results = down(rhs, gw, col_a, col_b, corner_a, corner_b, table)
+    *saved, saved4, message = results
     gathered = lax.all_to_all(message.reshape(256, 1, 384), ("row", "col"), 0, 0).reshape(768, 128)
     return up(gathered, saved4, saved)
 

time: 71.4 us -> 65.7 us (0.920)
  Pallas kernels: 17.6 us -> 13.3 us
  starting transfers between devices: 9.26 us -> 7.88 us
    pallas_call x1, Pallas kernels: 10 us -> 7 us  [up(): pl.pallas_call(up_kernel, out_shape=shaped(2, 256, 256), in_specs=[VMEM]...]
    pallas_call x1, Pallas kernels: 7.3 us -> 4.61 us  [down(): pl.pallas_call(down_kernel, out_shape=[shaped(*s) for s in state_shapes()...]
    ppermute x6, starting transfers between devices: 9.26 us -> 7.88 us  [swap(): return lax.ppermute(x, axis, pairs + [(j, i) for i, j in pairs])]
    pallas_call x0 -> x1, Pallas kernels: none -> 1.37 us  [middle(): pl.pallas_call(middle_kernel, out_shape=[shaped(4, 24, 8, 256)] * 2, in_s...]
    concatenate x0 -> x1, other arithmetic: none -> 0.75 us  [local(): table = jnp.concatenate([class_weight, class_stiffness])]
    another operation x2 -> x0, other arithmetic: 0.74 us -> none  [make_tables(): return jnp.stack([pad(0.5 * class_stiffness, FAR), pad(class_weight, 0.0)])]
  transfers between devices with their start and end apart: 6 -> 6, of which waited for: 2 -> 2; matrix products, arithmetic and copies ran while one was open for 2% -> 1% of each run, Pallas kernels for 0% -> 2%
where the time goes in v4:
time: 65.7 us; the launch traced here: 65.4 us
  blocking collectives  37.3 us (57%)
  Pallas kernels  13.3 us (20%)
  starting transfers between devices  7.88 us (12%)
  waiting for transfers between devices  4.11 us (6%)
  other arithmetic  1.72 us (3%)
  local copies, waits for them, and re-layouts  1.04 us (2%)
    all_to_all x1, blocking collectives, local(): lax.all_to_all(message.reshape(256, 1, 384), ('row', 'col'), 0, 0)  37.3 us
    ppermute x6, starting transfers between devices, swap(): return lax.ppermute(x, axis, pairs + [(j, i) for i, j in pairs])  7.88 us
    pallas_call x1, Pallas kernels, up(): pl.pallas_call(up_kernel, out_shape=shaped(2, 256, 256), in_specs=[VMEM]...  7 us
    pallas_call x1, Pallas kernels, down(): pl.pallas_call(down_kernel, out_shape=[shaped(*s) for s in state_shapes()...  4.61 us
    ppermute x6, waiting for transfers between devices, swap(): return lax.ppermute(x, axis, pairs + [(j, i) for i, j in pairs])  4.11 us
    pallas_call x1, Pallas kernels, middle(): pl.pallas_call(middle_kernel, out_shape=[shaped(4, 24, 8, 256)] * 2, in_s...  1.37 us
  transfers between devices with their start and end apart: 6, of which 2 were waited for; matrix products, arithmetic and copies ran while one was open for 1% of the time, Pallas kernels for 2%

profile of v4, /device:TPU:1, one launch (start us, length us, event | category | flops | bytes accessed | tf_op | source)
XLA Modules:
  0.0 65.4 jit_solution(9271880234120853570)
XLA Ops:
  0.0 1.0 %add_convert_fusion.classes = f32[256,256]{1,0:T(8,128)S(1)} fusion(s32[256,256]{1,0:T(8,128)} %param.5), kind=kLoop, calls=%fused_computation | loop fusion | flops 131072 | bytes 524288 | tf_op jit(solution)/shard_map/convert_element_type | solution.py:673
  1.0 0.0 copy-start
  1.0 1.0 %copy-done = f32[2,256,256]{2,1,0:T(8,128)S(1)} copy-done((f32[2,256,256]{2,1,0:T(8,128)S(1)}, f32[2,256,256]{2,1,0:T(8,128)}, u32[]{:S(2)}) %copy-start) | copy-done | bytes 524312
  2.0 0.2 sides.1
  2.2 3.3 %collective-permute-start = (f32[3,64,256]{2,1,0:T(8,128)S(1)}, f32[3,64,256]{2,1,0:T(8,128)S(1)}, u32[]{:S(2)}, u32[]{:S(2)}) collective-permute-start(f32[3,64,256]{2,1,0:T(8,128)S(1)} %get-tuple-element.27), channel_id=1, source_target_pairs={{0,16},{32,48},{64,80},{96,112},{128,144},{160,176},{192,208},{224... | collective-permute-start | bytes 589832 | tf_op jit(solution)/shard_map/ppermute | solution.py:669
  5.5 1.9 %collective-permute-start.1 = (f32[3,64,256]{2,1,0:T(8,128)S(1)}, f32[3,64,256]{2,1,0:T(8,128)S(1)}, u32[]{:S(2)}, u32[]{:S(2)}) collective-permute-start(f32[3,64,256]{2,1,0:T(8,128)S(1)} %get-tuple-element.28), channel_id=1, source_target_pairs={{16,32},{48,64},{80,96},{112,128},{144,160},{176,192},{208,224},{3... | collective-permute-start | bytes 589832 | tf_op jit(solution)/shard_map/ppermute | solution.py:669
  7.4 1.2 %collective-permute-start.2 = (f32[3,128,128]{2,1,0:T(8,128)S(1)}, f32[3,128,128]{2,1,0:T(8,128)S(1)}, u32[]{:S(2)}, u32[]{:S(2)}) collective-permute-start(f32[3,128,128]{2,1,0:T(8,128)S(1)} %get-tuple-element.39), channel_id=1, source_target_pairs={{0,1},{2,3},{4,5},{6,7},{8,9},{10,11},{12,13},{14,15},{1,0},{3,2},... | collective-permute-start | bytes 589832 | tf_op jit(solution)/shard_map/ppermute | solution.py:669
  8.6 0.7 %collective-permute-start.3 = (f32[3,128,128]{2,1,0:T(8,128)S(1)}, f32[3,128,128]{2,1,0:T(8,128)S(1)}, u32[]{:S(2)}, u32[]{:S(2)}) collective-permute-start(f32[3,128,128]{2,1,0:T(8,128)S(1)} %get-tuple-element.40), channel_id=1, source_target_pairs={{1,2},{3,4},{5,6},{7,8},{9,10},{11,12},{13,14},{2,1},{4,3},{6,5},{... | collective-permute-start | bytes 589832 | tf_op jit(solution)/shard_map/ppermute | solution.py:669
  9.3 0.0 collective-permute-done.row_a
  9.3 3.5 %collective-permute-done.1.row_b = f32[3,64,256]{2,1,0:T(8,128)S(1)} collective-permute-done((f32[3,64,256]{2,1,0:T(8,128)S(1)}, f32[3,64,256]{2,1,0:T(8,128)S(1)}, u32[]{:S(2)}, u32[]{:S(2)}) %collective-permute-start.1) | collective-permute-done | bytes 196640 | tf_op jit(solution)/shard_map/ppermute | solution.py:669
  12.8 0.1 corners.1
  12.9 0.1 collective-permute-start.4
  13.1 0.7 %collective-permute-start.5 = (f32[3,64,128]{2,1,0:T(8,128)S(1)}, f32[3,64,128]{2,1,0:T(8,128)S(1)}, u32[]{:S(2)}, u32[]{:S(2)}) collective-permute-start(f32[3,64,128]{2,1,0:T(8,128)S(1)} %get-tuple-element.42), channel_id=1, source_target_pairs={{1,2},{3,4},{5,6},{7,8},{9,10},{11,12},{13,14},{2,1},{4,3},{6,5},{... | collective-permute-start | bytes 294920 | tf_op jit(solution)/shard_map/ppermute | solution.py:669
  13.7 0.7 %pad_maximum_fusion.table = f32[16]{0:T(128)S(1)} fusion(f32[8]{0:T(128)} %param.7, f32[8]{0:T(128)} %param.6), kind=kLoop, calls=%fused_computation.1 | loop fusion | flops 16 | bytes 128 | tf_op jit(solution)/shard_map/concatenate | solution.py:680
  14.5 1.4 %middle.1 = (f32[4,24,8,256]{3,2,1,0:T(8,128)S(1)}, f32[4,24,8,256]{3,2,1,0:T(8,128)S(1)}) custom-call(f32[3,256,256]{2,1,0:T(8,128)S(1)} %get-tuple-element.32.own, f32[3,64,256]{2,1,0:T(8,128)S(1)} %collective-permute-done.row_a, f32[3,64,256]{2,1,0:T(8,128)S(1)} %collective-permute-done.1.row_b, f32[16]{0:T(128)S(1)} %pad_maximum_fusion.table), custom_call_target="tpu_custom_call" | custom-call | tf_op jit(solution)/shard_map/middle/pallas_call | solution.py:612
  15.9 0.0 collective-permute-done.2.col_a
  15.9 0.0 collective-permute-done.3.col_b
  15.9 0.6 collective-permute-done.4.corner_a
  16.5 0.0 collective-permute-done.5.corner_b
  16.5 4.6 %down.1 = (f32[13,26,8,384]{3,2,1,0:T(8,128)S(1)}, f32[13,14,8,256]{3,2,1,0:T(8,128)S(1)}, f32[13,8,8,128]{3,2,1,0:T(8,128)S(1)}, f32[13,5,8,128]{3,2,1,0:T(8,12...) custom-call(f32[4,24,8,256]{3,2,1,0:T(8,128)S(1)} %get-tuple-element.37.rhs0, ...), custom_call_target="tpu_custom_call" | custom-call | tf_op jit(solution)/shard_map/down/pallas_call | solution.py:624
  21.1 37.3 %all_to_all.5 = f32[256,1,384]{2,1,0:T(1,128)S(1)} all-to-all(f32[256,1,384]{2,1,0:T(1,128)S(1)} %bitcast.3), channel_id=1, replica_groups=mesh['row'=16,'col'=16] {'row','col'}, dimensions={0} | all-to-all | bytes 786432 | tf_op jit(solution)/shard_map/all_to_all | solution.py:684
  58.4 7.0 %up.1 = f32[2,256,256]{2,1,0:T(8,128)} custom-call(f32[768,128]{1,0:T(8,128)S(1)} %bitcast.2, f32[4,24,128]{2,1,0:T(8,128)S(1)} %get-tuple-element.44.saved4, f32[13,26,8,384]{3,2,1,0:T(8,128)S(1)} %get-tuple-element.45.rest_0_, f32[13,14,8,256]{3,2,1,0:T(8,128)S(1)} %get-tuple-element.46.rest_1_, f32[13,8,8,128]{3,2,1,0:T(8,128)S(1)} %get-tuple-element.47.rest_2_, ...), custom_call_target="tpu_custom_call" | custom-call | tf_op jit(solution)/shard_map/up/pallas_call | solution.py:643
Async XLA Ops:
  1.0 1.0 %copy-start = (f32[2,256,256]{2,1,0:T(8,128)S(1)}, f32[2,256,256]{2,1,0:T(8,128)}, u32[]{:S(2)}) copy-start(f32[2,256,256]{2,1,0:T(8,128)} %observed.1) | copy-start | bytes 1572868
  2.2 7.1 %collective-permute-start = (f32[3,64,256]{2,1,0:T(8,128)S(1)}, f32[3,64,256]{2,1,0:T(8,128)S(1)}, u32[]{:S(2)}, u32[]{:S(2)}) collective-permute-start(f32[3,64,256]{2,1,0:T(8,128)S(1)} %get-tuple-element.27), channel_id=1, source_target_pairs={{0,16},{32,48},{64,80},{96,112},{128,144},{160,176},{192,208},{224... | collective-permute-start | bytes 589832 | tf_op jit(solution)/shard_map/ppermute | solution.py:669
  5.5 7.3 %collective-permute-start.1 = (f32[3,64,256]{2,1,0:T(8,128)S(1)}, f32[3,64,256]{2,1,0:T(8,128)S(1)}, u32[]{:S(2)}, u32[]{:S(2)}) collective-permute-start(f32[3,64,256]{2,1,0:T(8,128)S(1)} %get-tuple-element.28), channel_id=1, source_target_pairs={{16,32},{48,64},{80,96},{112,128},{144,160},{176,192},{208,224},{3... | collective-permute-start | bytes 589832 | tf_op jit(solution)/shard_map/ppermute | solution.py:669
  7.4 8.4 %collective-permute-start.2 = (f32[3,128,128]{2,1,0:T(8,128)S(1)}, f32[3,128,128]{2,1,0:T(8,128)S(1)}, u32[]{:S(2)}, u32[]{:S(2)}) collective-permute-start(f32[3,128,128]{2,1,0:T(8,128)S(1)} %get-tuple-element.39), channel_id=1, source_target_pairs={{0,1},{2,3},{4,5},{6,7},{8,9},{10,11},{12,13},{14,15},{1,0},{3,2},... | collective-permute-start | bytes 589832 | tf_op jit(solution)/shard_map/ppermute | solution.py:669
  8.6 7.2 %collective-permute-start.3 = (f32[3,128,128]{2,1,0:T(8,128)S(1)}, f32[3,128,128]{2,1,0:T(8,128)S(1)}, u32[]{:S(2)}, u32[]{:S(2)}) collective-permute-start(f32[3,128,128]{2,1,0:T(8,128)S(1)} %get-tuple-element.40), channel_id=1, source_target_pairs={{1,2},{3,4},{5,6},{7,8},{9,10},{11,12},{13,14},{2,1},{4,3},{6,5},{... | collective-permute-start | bytes 589832 | tf_op jit(solution)/shard_map/ppermute | solution.py:669
  12.9 3.6 %collective-permute-start.4 = (f32[3,64,128]{2,1,0:T(8,128)S(1)}, f32[3,64,128]{2,1,0:T(8,128)S(1)}, u32[]{:S(2)}, u32[]{:S(2)}) collective-permute-start(f32[3,64,128]{2,1,0:T(8,128)S(1)} %get-tuple-element.41), channel_id=1, source_target_pairs={{0,1},{2,3},{4,5},{6,7},{8,9},{10,11},{12,13},{14,15},{1,0},{3,2},... | collective-permute-start | bytes 294920 | tf_op jit(solution)/shard_map/ppermute | solution.py:669
  13.1 3.4 %collective-permute-start.5 = (f32[3,64,128]{2,1,0:T(8,128)S(1)}, f32[3,64,128]{2,1,0:T(8,128)S(1)}, u32[]{:S(2)}, u32[]{:S(2)}) collective-permute-start(f32[3,64,128]{2,1,0:T(8,128)S(1)} %get-tuple-element.42), channel_id=1, source_target_pairs={{1,2},{3,4},{5,6},{7,8},{9,10},{11,12},{13,14},{2,1},{4,3},{6,5},{... | collective-permute-start | bytes 294920 | tf_op jit(solution)/shard_map/ppermute | solution.py:669

commit v5 on v4

--- a/solution.py
+++ b/solution.py
@@ -3,6 +3,7 @@
 from jax import lax
 from jax.experimental import pallas as pl
 from jax.experimental.pallas import tpu as pltpu
+from jax.sharding import Mesh
 from jax.sharding import PartitionSpec as P
 
 CG_ITERS = 12
@@ -10,6 +11,7 @@
 TILES = (48, 24, 12, 6, 3)
 LANES = (384, 256, 128, 128, 128)
 F32 = jnp.float32
+ROW = ("z", "core")
 BF16 = jnp.bfloat16
 BLACK, EDGE, INV, STATE = 4, 6, 11, 13
 
@@ -117,7 +119,7 @@
 
 
 def place():
-    return lax.axis_index("row"), lax.axis_index("col")
+    return 2 * lax.axis_index("z") + lax.axis_index("core"), lax.axis_index("col")
 
 
 def fold(x, low, swap):
@@ -329,33 +331,42 @@
     pattern = onehot(jnp.logical_and(lane // 64 == l // 64, lane % 64 == l % 4 + 12))
     right = message_row(merged[0:16], pattern, mine)
 
-    block = jnp.concatenate((common + [jnp.zeros((1, 128), F32)]) * 8, axis=0)
+    block = jnp.concatenate((common + [jnp.zeros((2, 128), F32)]) * 8, axis=0)
 
     def send(i, carry):
-        message[pl.ds(pl.multiple_of(i * 24, 8), 24), :] = block
+        message[pl.ds(pl.multiple_of(i * 32, 32), 32), :] = block
         return carry
 
-    lax.fori_loop(0, 32, send, 0)
+    lax.fori_loop(0, 16, send, 0)
     for dr, dc, what in NEIGHBOURS:
         x = {-1: top, 1: bottom}.get(dr, left if dc < 0 else right)
         r, c = row + dr, col + dc
 
         @pl.when(jnp.logical_and(jnp.logical_and(r >= 0, r < 16), jnp.logical_and(c >= 0, c < 16)))
-        def _(r=r, c=c, x=x):
-            message[pl.ds((r * 16 + c) * 3 + 2, 1), :] = x
+        def _(r=r, c=c, x=x, dr=dr):
+            message[pl.ds(((r >> 1) * 16 + c) * 4 + (3 if dr else 2), 1), :] = x
 
 
 NEIGHBOURS = [(dr, dc, None) for dr in (-1, 0, 1) for dc in (-1, 0, 1) if dr or dc]
 
 
-def cg(gathered, kc, e, d, s, w, r):
+def cg(mine, theirs, mix, kc, e, d, s, w, r):
     lane = iota((8, 128), 1)
     sub = iota((8, 128), 0)
     group = lane // 8
+    first_core = place()[0] % 2 == 0
     arrays = [[None] * 16 for _ in range(4)]
     for hi in range(2):
         for pair in range(2):
-            v = [gathered[pl.ds((hi * 128 + c) * 3 + pair, 8, stride=48), :] for c in range(16)]
+            v = []
+            for c in range(16):
+                rows = pl.ds((hi * 64 + c) * 4 + pair, 4, stride=64)
+                x, y = mine[rows, :], theirs[rows, :]
+                start = ((hi * 2 + pair) * 16 + c) * 8
+                mix[pl.ds(start, 4, stride=2), :] = jnp.where(first_core, x, y)
+                mix[pl.ds(start + 1, 4, stride=2), :] = jnp.where(first_core, y, x)
+            for c in range(16):
+                v.append(mix[pl.ds(((hi * 2 + pair) * 16 + c) * 8, 8), :])
             for k in (1, 2, 4, 8):
                 low = (group // k) % 2 == 0
                 for c in range(16):
@@ -447,7 +458,7 @@
             e[f, t] = e[f, t] + alpha * (r[f, t] + beta * d[f, t])
 
 
-def merged_frame(gathered, merged):
+def merged_frame(mine, theirs, merged):
     row, col = place()
     at = iota((24, 128), 0)
     l = iota((24, 128), 1)
@@ -455,14 +466,14 @@
     for dr, dc, _ in NEIGHBOURS:
         r, c = row + dr, col + dc
         there = jnp.logical_and(jnp.logical_and(r >= 0, r < 16), jnp.logical_and(c >= 0, c < 16))
-        index = jnp.where(there, (r * 16 + c) * 3 + 2, 0)
-        x = gathered[pl.ds(index, 1), :] * jnp.where(there, 1.0, 0.0)
+        index = jnp.where(there, ((r >> 1) * 16 + c) * 4 + (3 if dr else 2), 0)
+        x = (theirs if dr else mine)[pl.ds(index, 1), :] * jnp.where(there, 1.0, 0.0)
         if dr:
-            mine = at == (20 if dr < 0 else 16) + (l // 16) % 4
+            ours = at == (20 if dr < 0 else 16) + (l // 16) % 4
         else:
-            mine = at == (l // 4) % 16
+            ours = at == (l // 4) % 16
         key = dc if dr else 2 * dc
-        total[key] = total.get(key, 0.0) + jnp.where(mine, jnp.broadcast_to(x, (24, 128)), 0.0)
+        total[key] = total.get(key, 0.0) + jnp.where(ours, jnp.broadcast_to(x, (24, 128)), 0.0)
     l = iota((128, 128), 0)
     lane = iota((128, 128), 1)
     base = (l // 64) * 64
@@ -481,10 +492,10 @@
     return result
 
 
-def up_kernel(gathered, saved4, *rest):
+def up_kernel(mine, theirs, saved4, *rest):
     states, out = rest[:4], rest[4]
-    full, red, blk, kc, e, d, s, w, r, result, nat, sent = rest[5:]
-    cg(gathered, kc, e, d, s, w, r)
+    full, red, blk, mix, kc, e, d, s, w, r, result, nat, sent = rest[5:]
+    cg(mine, theirs, mix, kc, e, d, s, w, r)
 
     row, col = place()
     n = iota((24, 128), 1)
@@ -501,7 +512,7 @@
         correction += times(pick(rows, whole), cols)
 
     is_red = red4()
-    merged = merged_frame(gathered, saved4[0])
+    merged = merged_frame(mine, theirs, saved4[0])
     k, inv = edges4(saved4[2], saved4[3])
     x = jnp.where(is_red, 0.0, merged + correction)
     x = jnp.where(is_red, (merged + pull4(k, x)) * inv, 0.0)
@@ -623,7 +634,7 @@
 def down(*args):
     return pl.pallas_call(
         down_kernel,
-        out_shape=[shaped(*s) for s in state_shapes()] + [shaped(4, 24, 128), shaped(768, 128)],
+        out_shape=[shaped(*s) for s in state_shapes()] + [shaped(4, 24, 128), shaped(512, 128)],
         in_specs=[VMEM] * 6 + [SMEM],
         out_specs=[VMEM] * 6,
         scratch_shapes=[
@@ -639,16 +650,17 @@
     )(*args)
 
 
-def up(gathered, saved4, saved):
+def up(mine, theirs, saved4, saved):
     return pl.pallas_call(
         up_kernel,
         out_shape=shaped(2, 256, 256),
-        in_specs=[VMEM] * 6,
+        in_specs=[VMEM] * 7,
         out_specs=ANY,
         scratch_shapes=[
             scratch(2, 24, 8, 256),
             scratch(2, 26, 8, 384),
             scratch(2, 26, 8, 384),
+            scratch(512, 128),
             scratch(5, 16, 8, 128),
             scratch(2, 16, 8, 128),
             scratch(2, 16, 8, 128),
@@ -661,17 +673,17 @@
         ],
         compiler_params=PARAMS,
         name="up",
-    )(gathered, saved4, *saved)
+    )(mine, theirs, saved4, *saved)
 
 
 def swap(x, axis, first):
-    pairs = [(i, i + 1) for i in range(first, lax.axis_size(axis) - 1, 2)]
+    pairs = [(i, i + 1) for i in range(first, 15, 2)]
     return lax.ppermute(x, axis, pairs + [(j, i) for i, j in pairs])
 
 
 def local(observed, coherence_class, class_weight, class_stiffness):
     own, row_a, row_b, col_a, col_b = side_strips(observed, (coherence_class + 1).astype(F32))
-    row_a, row_b = swap(row_a, "row", 0), swap(row_b, "row", 1)
+    row_a, row_b = swap(row_a, ROW, 0), swap(row_b, ROW, 1)
     col_a, col_b = swap(col_a, "col", 0), swap(col_b, "col", 1)
     corner_a, corner_b = corner_strips(row_a, row_b)
     held = lax.optimization_barrier((corner_a, corner_b, own, row_a, row_b, class_weight, class_stiffness))
@@ -681,11 +693,13 @@
     rhs, gw = middle(own, row_a, row_b, table)
     results = down(rhs, gw, col_a, col_b, corner_a, corner_b, table)
     *saved, saved4, message = results
-    gathered = lax.all_to_all(message.reshape(256, 1, 384), ("row", "col"), 0, 0).reshape(768, 128)
-    return up(gathered, saved4, saved)
+    mine = lax.all_to_all(message.reshape(128, 4, 128), ("z", "col"), 0, 0)
+    theirs = lax.ppermute(mine, "core", [(0, 1), (1, 0)])
+    return up(mine.reshape(512, 128), theirs.reshape(512, 128), saved4, saved)
 
 
 def solution(mesh):
-    in_specs = (P(None, "row", "col"), P("row", "col"), P(), P())
-    out_specs = P(None, "row", "col")
-    return jax.shard_map(local, mesh=mesh, in_specs=in_specs, out_specs=out_specs, check_vma=False)
+    chips = Mesh(mesh.devices.reshape(8, 2, 16), ("z", "core", "col"))
+    in_specs = (P(None, ROW, "col"), P(ROW, "col"), P(), P())
+    out_specs = P(None, ROW, "col")
+    return jax.shard_map(local, mesh=chips, in_specs=in_specs, out_specs=out_specs, check_vma=False)

time: 65.7 us -> 64 us (0.974)
  blocking collectives: 37.3 us -> 30.9 us
  starting transfers between devices: 7.88 us -> 11.5 us
  waiting for transfers between devices: 4.11 us -> 5.28 us
    all_to_all x1, blocking collectives: 37.3 us -> 30.9 us  [local(): mine = lax.all_to_all(message.reshape(128, 4, 128), ('z', 'col'), 0, 0)]
    ppermute x0 -> x1, starting transfers between devices: none -> 3.61 us  [local(): theirs = lax.ppermute(mine, 'core', [(0, 1), (1, 0)])]
    ppermute x0 -> x1, waiting for transfers between devices: none -> 1.16 us  [local(): theirs = lax.ppermute(mine, 'core', [(0, 1), (1, 0)])]
  transfers between devices with their start and end apart: 6 -> 7, of which waited for: 2 -> 3; matrix products, arithmetic and copies ran while one was open for 1% -> 1% of each run, Pallas kernels for 2% -> 2%
where the time goes in v5:
time: 64 us; the launch traced here: 63.7 us
  blocking collectives  30.9 us (48%)
  Pallas kernels  13.3 us (21%)
  starting transfers between devices  11.5 us (18%)
  waiting for transfers between devices  5.28 us (8%)
  other arithmetic  1.72 us (3%)
  local copies, waits for them, and re-layouts  1.04 us (2%)
    all_to_all x1, blocking collectives, local(): mine = lax.all_to_all(message.reshape(128, 4, 128), ('z', 'col'), 0, 0)  30.9 us
    ppermute x6, starting transfers between devices, swap(): return lax.ppermute(x, axis, pairs + [(j, i) for i, j in pairs])  7.88 us
    pallas_call x1, Pallas kernels, up(): pl.pallas_call(up_kernel, out_shape=shaped(2, 256, 256), in_specs=[VMEM]...  7.06 us
    pallas_call x1, Pallas kernels, down(): pl.pallas_call(down_kernel, out_shape=[shaped(*s) for s in state_shapes()...  4.52 us
    ppermute x6, waiting for transfers between devices, swap(): return lax.ppermute(x, axis, pairs + [(j, i) for i, j in pairs])  4.12 us
    ppermute x1, starting transfers between devices, local(): theirs = lax.ppermute(mine, 'core', [(0, 1), (1, 0)])  3.61 us
    pallas_call x1, Pallas kernels, middle(): pl.pallas_call(middle_kernel, out_shape=[shaped(4, 24, 8, 256)] * 2, in_s...  1.37 us
  transfers between devices with their start and end apart: 7, of which 3 were waited for; matrix products, arithmetic and copies ran while one was open for 1% of the time, Pallas kernels for 2%

profile of v5, /device:TPU:1, one launch (start us, length us, event | category | flops | bytes accessed | tf_op | source)
XLA Modules:
  0.0 63.7 jit_solution(17035611927630761254)
XLA Ops:
  0.0 1.0 %add_convert_fusion.classes = f32[256,256]{1,0:T(8,128)S(1)} fusion(s32[256,256]{1,0:T(8,128)} %param.5), kind=kLoop, calls=%fused_computation | loop fusion | flops 131072 | bytes 524288 | tf_op jit(solution)/shard_map/convert_element_type | solution.py:685
  1.0 0.0 copy-start
  1.0 1.0 %copy-done = f32[2,256,256]{2,1,0:T(8,128)S(1)} copy-done((f32[2,256,256]{2,1,0:T(8,128)S(1)}, f32[2,256,256]{2,1,0:T(8,128)}, u32[]{:S(2)}) %copy-start) | copy-done | bytes 524312
  2.0 0.2 sides.1
  2.2 3.3 %collective-permute-start = (f32[3,64,256]{2,1,0:T(8,128)S(1)}, f32[3,64,256]{2,1,0:T(8,128)S(1)}, u32[]{:S(2)}, u32[]{:S(2)}) collective-permute-start(f32[3,64,256]{2,1,0:T(8,128)S(1)} %get-tuple-element.27), channel_id=1, source_target_pairs={{0,16},{32,48},{64,80},{96,112},{128,144},{160,176},{192,208},{224... | collective-permute-start | bytes 589832 | tf_op jit(solution)/shard_map/ppermute | solution.py:681
  5.5 1.9 %collective-permute-start.1 = (f32[3,64,256]{2,1,0:T(8,128)S(1)}, f32[3,64,256]{2,1,0:T(8,128)S(1)}, u32[]{:S(2)}, u32[]{:S(2)}) collective-permute-start(f32[3,64,256]{2,1,0:T(8,128)S(1)} %get-tuple-element.28), channel_id=1, source_target_pairs={{16,32},{48,64},{80,96},{112,128},{144,160},{176,192},{208,224},{3... | collective-permute-start | bytes 589832 | tf_op jit(solution)/shard_map/ppermute | solution.py:681
  7.4 1.2 %collective-permute-start.2 = (f32[3,128,128]{2,1,0:T(8,128)S(1)}, f32[3,128,128]{2,1,0:T(8,128)S(1)}, u32[]{:S(2)}, u32[]{:S(2)}) collective-permute-start(f32[3,128,128]{2,1,0:T(8,128)S(1)} %get-tuple-element.39), channel_id=1, source_target_pairs={{0,1},{2,3},{4,5},{6,7},{8,9},{10,11},{12,13},{14,15},{1,0},{3,2},... | collective-permute-start | bytes 589832 | tf_op jit(solution)/shard_map/ppermute | solution.py:681
  8.6 0.7 %collective-permute-start.3 = (f32[3,128,128]{2,1,0:T(8,128)S(1)}, f32[3,128,128]{2,1,0:T(8,128)S(1)}, u32[]{:S(2)}, u32[]{:S(2)}) collective-permute-start(f32[3,128,128]{2,1,0:T(8,128)S(1)} %get-tuple-element.40), channel_id=1, source_target_pairs={{1,2},{3,4},{5,6},{7,8},{9,10},{11,12},{13,14},{2,1},{4,3},{6,5},{... | collective-permute-start | bytes 589832 | tf_op jit(solution)/shard_map/ppermute | solution.py:681
  9.3 0.0 collective-permute-done.row_a
  9.3 3.5 %collective-permute-done.1.row_b = f32[3,64,256]{2,1,0:T(8,128)S(1)} collective-permute-done((f32[3,64,256]{2,1,0:T(8,128)S(1)}, f32[3,64,256]{2,1,0:T(8,128)S(1)}, u32[]{:S(2)}, u32[]{:S(2)}) %collective-permute-start.1) | collective-permute-done | bytes 196640 | tf_op jit(solution)/shard_map/ppermute | solution.py:681
  12.8 0.1 corners.1
  12.9 0.1 collective-permute-start.4
  13.1 0.7 %collective-permute-start.5 = (f32[3,64,128]{2,1,0:T(8,128)S(1)}, f32[3,64,128]{2,1,0:T(8,128)S(1)}, u32[]{:S(2)}, u32[]{:S(2)}) collective-permute-start(f32[3,64,128]{2,1,0:T(8,128)S(1)} %get-tuple-element.42), channel_id=1, source_target_pairs={{1,2},{3,4},{5,6},{7,8},{9,10},{11,12},{13,14},{2,1},{4,3},{6,5},{... | collective-permute-start | bytes 294920 | tf_op jit(solution)/shard_map/ppermute | solution.py:681
  13.7 0.7 %pad_maximum_fusion.table = f32[16]{0:T(128)S(1)} fusion(f32[8]{0:T(128)} %param.7, f32[8]{0:T(128)} %param.6), kind=kLoop, calls=%fused_computation.1 | loop fusion | flops 16 | bytes 128 | tf_op jit(solution)/shard_map/concatenate | solution.py:692
  14.5 1.4 %middle.1 = (f32[4,24,8,256]{3,2,1,0:T(8,128)S(1)}, f32[4,24,8,256]{3,2,1,0:T(8,128)S(1)}) custom-call(f32[3,256,256]{2,1,0:T(8,128)S(1)} %get-tuple-element.32.own, f32[3,64,256]{2,1,0:T(8,128)S(1)} %collective-permute-done.row_a, f32[3,64,256]{2,1,0:T(8,128)S(1)} %collective-permute-done.1.row_b, f32[16]{0:T(128)S(1)} %pad_maximum_fusion.table), custom_call_target="tpu_custom_call" | custom-call | tf_op jit(solution)/shard_map/middle/pallas_call | solution.py:623
  15.9 0.0 collective-permute-done.2.col_a
  15.9 0.0 collective-permute-done.3.col_b
  15.9 0.6 collective-permute-done.4.corner_a
  16.5 0.0 collective-permute-done.5.corner_b
  16.5 4.5 %down.1 = (f32[13,26,8,384]{3,2,1,0:T(8,128)S(1)}, f32[13,14,8,256]{3,2,1,0:T(8,128)S(1)}, f32[13,8,8,128]{3,2,1,0:T(8,128)S(1)}, f32[13,5,8,128]{3,2,1,0:T(8,12...) custom-call(f32[4,24,8,256]{3,2,1,0:T(8,128)S(1)} %get-tuple-element.37.rhs0, ...), custom_call_target="tpu_custom_call" | custom-call | tf_op jit(solution)/shard_map/down/pallas_call | solution.py:635
  21.0 30.9 %all_to_all.5 = f32[128,4,128]{2,1,0:T(4,128)S(1)} all-to-all(f32[128,4,128]{2,1,0:T(4,128)S(1)} %bitcast.5), channel_id=1, replica_groups=mesh['z'=8,'core'=2,'col'=16] {'z','col'}, dimensions={0} | all-to-all | bytes 524288 | tf_op jit(solution)/shard_map/all_to_all | solution.py:696
  51.9 3.6 %collective-permute-start.6 = (f32[128,4,128]{2,1,0:T(4,128)S(1)}, f32[128,4,128]{2,1,0:T(4,128)S(1)}, u32[]{:S(2)}, u32[]{:S(2)}) collective-permute-start(f32[128,4,128]{2,1,0:T(4,128)S(1)} %all_to_all.5), channel_id=1, source_target_pairs={{0,16},{16,0},{1,17},{17,1},{2,18},{18,2},{3,19},{19,3},{4,20},{20... | collective-permute-start | bytes 786440 | tf_op jit(solution)/shard_map/ppermute | solution.py:697
  55.5 1.2 %collective-permute-done.6 = f32[128,4,128]{2,1,0:T(4,128)S(1)} collective-permute-done((f32[128,4,128]{2,1,0:T(4,128)S(1)}, f32[128,4,128]{2,1,0:T(4,128)S(1)}, u32[]{:S(2)}, u32[]{:S(2)}) %collective-permute-start.6) | collective-permute-done | bytes 262176 | tf_op jit(solution)/shard_map/ppermute | solution.py:697
  56.6 7.1 %up.1 = f32[2,256,256]{2,1,0:T(8,128)} custom-call(f32[512,128]{1,0:T(8,128)S(1)} %bitcast.3, f32[512,128]{1,0:T(8,128)S(1)} %bitcast.4, f32[4,24,128]{2,1,0:T(8,128)S(1)} %get-tuple-element.44.saved4, f32[13,26,8,384]{3,2,1,0:T(8,128)S(1)} %get-tuple-element.45.rest_0_, f32[13,14,8,256]{3,2,1,0:T(8,128)S(1)} %get-tuple-element.46.rest_1_, ...), custom_call_target="tpu_custom_call" | custom-call | tf_op jit(solution)/shard_map/up/pallas_call | solution.py:654
Async XLA Ops:
  1.0 1.0 %copy-start = (f32[2,256,256]{2,1,0:T(8,128)S(1)}, f32[2,256,256]{2,1,0:T(8,128)}, u32[]{:S(2)}) copy-start(f32[2,256,256]{2,1,0:T(8,128)} %observed.1) | copy-start | bytes 1572868
  2.2 7.1 %collective-permute-start = (f32[3,64,256]{2,1,0:T(8,128)S(1)}, f32[3,64,256]{2,1,0:T(8,128)S(1)}, u32[]{:S(2)}, u32[]{:S(2)}) collective-permute-start(f32[3,64,256]{2,1,0:T(8,128)S(1)} %get-tuple-element.27), channel_id=1, source_target_pairs={{0,16},{32,48},{64,80},{96,112},{128,144},{160,176},{192,208},{224... | collective-permute-start | bytes 589832 | tf_op jit(solution)/shard_map/ppermute | solution.py:681
  5.5 7.3 %collective-permute-start.1 = (f32[3,64,256]{2,1,0:T(8,128)S(1)}, f32[3,64,256]{2,1,0:T(8,128)S(1)}, u32[]{:S(2)}, u32[]{:S(2)}) collective-permute-start(f32[3,64,256]{2,1,0:T(8,128)S(1)} %get-tuple-element.28), channel_id=1, source_target_pairs={{16,32},{48,64},{80,96},{112,128},{144,160},{176,192},{208,224},{3... | collective-permute-start | bytes 589832 | tf_op jit(solution)/shard_map/ppermute | solution.py:681
  7.4 8.4 %collective-permute-start.2 = (f32[3,128,128]{2,1,0:T(8,128)S(1)}, f32[3,128,128]{2,1,0:T(8,128)S(1)}, u32[]{:S(2)}, u32[]{:S(2)}) collective-permute-start(f32[3,128,128]{2,1,0:T(8,128)S(1)} %get-tuple-element.39), channel_id=1, source_target_pairs={{0,1},{2,3},{4,5},{6,7},{8,9},{10,11},{12,13},{14,15},{1,0},{3,2},... | collective-permute-start | bytes 589832 | tf_op jit(solution)/shard_map/ppermute | solution.py:681
  8.6 7.2 %collective-permute-start.3 = (f32[3,128,128]{2,1,0:T(8,128)S(1)}, f32[3,128,128]{2,1,0:T(8,128)S(1)}, u32[]{:S(2)}, u32[]{:S(2)}) collective-permute-start(f32[3,128,128]{2,1,0:T(8,128)S(1)} %get-tuple-element.40), channel_id=1, source_target_pairs={{1,2},{3,4},{5,6},{7,8},{9,10},{11,12},{13,14},{2,1},{4,3},{6,5},{... | collective-permute-start | bytes 589832 | tf_op jit(solution)/shard_map/ppermute | solution.py:681
  12.9 3.6 %collective-permute-start.4 = (f32[3,64,128]{2,1,0:T(8,128)S(1)}, f32[3,64,128]{2,1,0:T(8,128)S(1)}, u32[]{:S(2)}, u32[]{:S(2)}) collective-permute-start(f32[3,64,128]{2,1,0:T(8,128)S(1)} %get-tuple-element.41), channel_id=1, source_target_pairs={{0,1},{2,3},{4,5},{6,7},{8,9},{10,11},{12,13},{14,15},{1,0},{3,2},... | collective-permute-start | bytes 294920 | tf_op jit(solution)/shard_map/ppermute | solution.py:681
  13.1 3.4 %collective-permute-start.5 = (f32[3,64,128]{2,1,0:T(8,128)S(1)}, f32[3,64,128]{2,1,0:T(8,128)S(1)}, u32[]{:S(2)}, u32[]{:S(2)}) collective-permute-start(f32[3,64,128]{2,1,0:T(8,128)S(1)} %get-tuple-element.42), channel_id=1, source_target_pairs={{1,2},{3,4},{5,6},{7,8},{9,10},{11,12},{13,14},{2,1},{4,3},{6,5},{... | collective-permute-start | bytes 294920 | tf_op jit(solution)/shard_map/ppermute | solution.py:681
  51.9 4.8 %collective-permute-start.6 = (f32[128,4,128]{2,1,0:T(4,128)S(1)}, f32[128,4,128]{2,1,0:T(4,128)S(1)}, u32[]{:S(2)}, u32[]{:S(2)}) collective-permute-start(f32[128,4,128]{2,1,0:T(4,128)S(1)} %all_to_all.5), channel_id=1, source_target_pairs={{0,16},{16,0},{1,17},{17,1},{2,18},{18,2},{3,19},{19,3},{4,20},{20... | collective-permute-start | bytes 786440 | tf_op jit(solution)/shard_map/ppermute | solution.py:697

commit v6 on v5

--- a/solution.py
+++ b/solution.py
@@ -145,16 +145,19 @@
         col_b[f] = jnp.where(col % 2 == 0, left, right)
 
 
-def corners_kernel(row_a, row_b, out_a, out_b):
+def unfold(east, west, low):
+    return jnp.where(low, east, west), roll(jnp.where(low, west, east), 64, 1)
+
+
+def corners_kernel(col_a, col_b, out_a, out_b):
     row, col = place()
-    low = iota((64, 128), 1) < 64
+    low = iota((128, 128), 1) < 64
     for f in range(3):
-        a, b = row_a[f], row_b[f]
-        south, north = jnp.where(row % 2 == 0, a, b), jnp.where(row % 2 == 0, b, a)
-        x = jnp.concatenate([south, north], axis=0)
-        left, right = fold(x[:, 0:128], low, False), fold(x[:, 128:256], low, True)
-        out_a[f] = jnp.where(col % 2 == 0, right, left)
-        out_b[f] = jnp.where(col % 2 == 0, left, right)
+        a, b = col_a[f], col_b[f]
+        first, second = unfold(jnp.where(col % 2 == 0, a, b), jnp.where(col % 2 == 0, b, a), low)
+        top, bottom = first[0:64], second[64:128]
+        out_a[f] = jnp.where(row % 2 == 0, bottom, top)
+        out_b[f] = jnp.where(row % 2 == 0, top, bottom)
 
 
 def message_row(x, pattern, mine):
@@ -204,15 +207,17 @@
     saved4, message = rest[4:6]
     gw, red, full, sums, frame, nat = rest[6:]
     row, col = place()
-    even_col = col % 2 == 0
-
-    for a, b, start, size in ((col_a, col_b, 0, 128), (corner_a, corner_b, 256, 64)):
-        low = iota((size, 128), 1) < 64
-        for f in range(3):
-            x, y = a[f], b[f]
-            e, w = jnp.where(even_col, x, y), jnp.where(even_col, y, x)
-            frame[f, start : start + size, :] = jnp.where(low, e, w)
-            frame[f, start + size : start + 2 * size, :] = roll(jnp.where(low, w, e), 64, 1)
+    even_row, even_col = row % 2 == 0, col % 2 == 0
+
+    low = iota((128, 128), 1) < 64
+    for f in range(3):
+        a, b = col_a[f], col_b[f]
+        first, second = unfold(jnp.where(even_col, a, b), jnp.where(even_col, b, a), low)
+        frame[f, 0:128, :] = first
+        frame[f, 128:256, :] = second
+        a, b = corner_a[f], corner_b[f]
+        frame[f, 256:320, :] = jnp.where(even_row, a, b)
+        frame[f, 320:384, :] = jnp.where(even_row, b, a)
     tables = class_tables(table)
     narrow = even_lanes((8, 128))
 
@@ -608,7 +613,7 @@
     )(observed, classes)
 
 
-def corner_strips(row_a, row_b):
+def corner_strips(col_a, col_b):
     return pl.pallas_call(
         corners_kernel,
         out_shape=[shaped(3, 64, 128)] * 2,
@@ -616,7 +621,7 @@
         out_specs=[VMEM] * 2,
         compiler_params=PARAMS,
         name="corners",
-    )(row_a, row_b)
+    )(col_a, col_b)
 
 
 def middle(own, row_a, row_b, table):
@@ -683,12 +688,12 @@
 
 def local(observed, coherence_class, class_weight, class_stiffness):
     own, row_a, row_b, col_a, col_b = side_strips(observed, (coherence_class + 1).astype(F32))
+    col_a, col_b = swap(col_a, "col", 0), swap(col_b, "col", 1)
     row_a, row_b = swap(row_a, ROW, 0), swap(row_b, ROW, 1)
-    col_a, col_b = swap(col_a, "col", 0), swap(col_b, "col", 1)
-    corner_a, corner_b = corner_strips(row_a, row_b)
-    held = lax.optimization_barrier((corner_a, corner_b, own, row_a, row_b, class_weight, class_stiffness))
-    corner_a, corner_b, own, row_a, row_b, class_weight, class_stiffness = held
-    corner_a, corner_b = swap(corner_a, "col", 0), swap(corner_b, "col", 1)
+    corner_a, corner_b = corner_strips(col_a, col_b)
+    held = lax.optimization_barrier((corner_a, corner_b, own, class_weight, class_stiffness))
+    corner_a, corner_b, own, class_weight, class_stiffness = held
+    corner_a, corner_b = swap(corner_a, ROW, 0), swap(corner_b, ROW, 1)
     table = jnp.concatenate([class_weight, class_stiffness])
     rhs, gw = middle(own, row_a, row_b, table)
     results = down(rhs, gw, col_a, col_b, corner_a, corner_b, table)

time: 64 us -> 65.6 us (1.025)
  starting transfers between devices: 11.5 us -> 14.9 us
  waiting for transfers between devices: 5.28 us -> 2.28 us
  blocking collectives: 30.9 us -> 32 us
    ppermute x6, starting transfers between devices: 7.88 us -> 11.7 us  [swap(): return lax.ppermute(x, axis, pairs + [(j, i) for i, j in pairs])]
    ppermute x6, waiting for transfers between devices: 4.12 us -> 1.12 us  [swap(): return lax.ppermute(x, axis, pairs + [(j, i) for i, j in pairs])]
    all_to_all x1, blocking collectives: 30.9 us -> 32 us  [local(): mine = lax.all_to_all(message.reshape(128, 4, 128), ('z', 'col'), 0, 0)]
  transfers between devices with their start and end apart: 7 -> 7, of which waited for: 3 -> 2; matrix products, arithmetic and copies ran while one was open for 1% -> 1% of each run, Pallas kernels for 2% -> 2%
where the time goes in v6:
time: 65.6 us; the launch traced here: 65.3 us
  blocking collectives  32 us (49%)
  starting transfers between devices  14.9 us (23%)
  Pallas kernels  13.3 us (20%)
  waiting for transfers between devices  2.28 us (3%)
  other arithmetic  1.72 us (3%)
  local copies, waits for them, and re-layouts  1.04 us (2%)
    all_to_all x1, blocking collectives, local(): mine = lax.all_to_all(message.reshape(128, 4, 128), ('z', 'col'), 0, 0)  32 us
    ppermute x6, starting transfers between devices, swap(): return lax.ppermute(x, axis, pairs + [(j, i) for i, j in pairs])  11.7 us
    pallas_call x1, Pallas kernels, up(): pl.pallas_call(up_kernel, out_shape=shaped(2, 256, 256), in_specs=[VMEM]...  7.06 us
    pallas_call x1, Pallas kernels, down(): pl.pallas_call(down_kernel, out_shape=[shaped(*s) for s in state_shapes()...  4.54 us
    ppermute x1, starting transfers between devices, local(): theirs = lax.ppermute(mine, 'core', [(0, 1), (1, 0)])  3.2 us
    pallas_call x1, Pallas kernels, middle(): pl.pallas_call(middle_kernel, out_shape=[shaped(4, 24, 8, 256)] * 2, in_s...  1.37 us
  transfers between devices with their start and end apart: 7, of which 2 were waited for; matrix products, arithmetic and copies ran while one was open for 1% of the time, Pallas kernels for 2%

profile of v6, /device:TPU:1, one launch (start us, length us, event | category | flops | bytes accessed | tf_op | source)
XLA Modules:
  0.0 65.3 jit_solution(9932749628401653097)
XLA Ops:
  0.0 1.0 %add_convert_fusion.classes = f32[256,256]{1,0:T(8,128)S(1)} fusion(s32[256,256]{1,0:T(8,128)} %param.5), kind=kLoop, calls=%fused_computation | loop fusion | flops 131072 | bytes 524288 | tf_op jit(solution)/shard_map/convert_element_type | solution.py:690
  1.0 0.0 copy-start
  1.0 1.0 %copy-done = f32[2,256,256]{2,1,0:T(8,128)S(1)} copy-done((f32[2,256,256]{2,1,0:T(8,128)S(1)}, f32[2,256,256]{2,1,0:T(8,128)}, u32[]{:S(2)}) %copy-start) | copy-done | bytes 524312
  2.0 0.2 sides.1
  2.2 2.2 %collective-permute-start = (f32[3,128,128]{2,1,0:T(8,128)S(1)}, f32[3,128,128]{2,1,0:T(8,128)S(1)}, u32[]{:S(2)}, u32[]{:S(2)}) collective-permute-start(f32[3,128,128]{2,1,0:T(8,128)S(1)} %get-tuple-element.25), channel_id=1, source_target_pairs={{0,1},{2,3},{4,5},{6,7},{8,9},{10,11},{12,13},{14,15},{1,0},{3,2},... | collective-permute-start | bytes 589832 | tf_op jit(solution)/shard_map/ppermute | solution.py:686
  4.4 0.7 %collective-permute-start.1 = (f32[3,128,128]{2,1,0:T(8,128)S(1)}, f32[3,128,128]{2,1,0:T(8,128)S(1)}, u32[]{:S(2)}, u32[]{:S(2)}) collective-permute-start(f32[3,128,128]{2,1,0:T(8,128)S(1)} %get-tuple-element.26), channel_id=1, source_target_pairs={{1,2},{3,4},{5,6},{7,8},{9,10},{11,12},{13,14},{2,1},{4,3},{6,5},{... | collective-permute-start | bytes 589832 | tf_op jit(solution)/shard_map/ppermute | solution.py:686
  5.1 1.2 %collective-permute-start.2 = (f32[3,64,256]{2,1,0:T(8,128)S(1)}, f32[3,64,256]{2,1,0:T(8,128)S(1)}, u32[]{:S(2)}, u32[]{:S(2)}) collective-permute-start(f32[3,64,256]{2,1,0:T(8,128)S(1)} %get-tuple-element.31), channel_id=1, source_target_pairs={{0,16},{32,48},{64,80},{96,112},{128,144},{160,176},{192,208},{224... | collective-permute-start | bytes 589832 | tf_op jit(solution)/shard_map/ppermute | solution.py:686
  6.3 3.3 %collective-permute-start.3 = (f32[3,64,256]{2,1,0:T(8,128)S(1)}, f32[3,64,256]{2,1,0:T(8,128)S(1)}, u32[]{:S(2)}, u32[]{:S(2)}) collective-permute-start(f32[3,64,256]{2,1,0:T(8,128)S(1)} %get-tuple-element.32), channel_id=1, source_target_pairs={{16,32},{48,64},{80,96},{112,128},{144,160},{176,192},{208,224},{3... | collective-permute-start | bytes 589832 | tf_op jit(solution)/shard_map/ppermute | solution.py:686
  9.6 0.0 collective-permute-done.col_a
  9.6 0.0 collective-permute-done.1.col_b
  9.6 0.1 corners.1
  9.7 1.7 %collective-permute-start.4 = (f32[3,64,128]{2,1,0:T(8,128)S(1)}, f32[3,64,128]{2,1,0:T(8,128)S(1)}, u32[]{:S(2)}, u32[]{:S(2)}) collective-permute-start(f32[3,64,128]{2,1,0:T(8,128)S(1)} %get-tuple-element.37), channel_id=1, source_target_pairs={{0,16},{32,48},{64,80},{96,112},{128,144},{160,176},{192,208},{224... | collective-permute-start | bytes 294920 | tf_op jit(solution)/shard_map/ppermute | solution.py:686
  11.4 2.7 %collective-permute-start.5 = (f32[3,64,128]{2,1,0:T(8,128)S(1)}, f32[3,64,128]{2,1,0:T(8,128)S(1)}, u32[]{:S(2)}, u32[]{:S(2)}) collective-permute-start(f32[3,64,128]{2,1,0:T(8,128)S(1)} %get-tuple-element.38), channel_id=1, source_target_pairs={{16,32},{48,64},{80,96},{112,128},{144,160},{176,192},{208,224},{3... | collective-permute-start | bytes 294920 | tf_op jit(solution)/shard_map/ppermute | solution.py:686
  14.1 0.7 %pad_maximum_fusion.table = f32[16]{0:T(128)S(1)} fusion(f32[8]{0:T(128)} %param.7, f32[8]{0:T(128)} %param.6), kind=kLoop, calls=%fused_computation.1 | loop fusion | flops 16 | bytes 128 | tf_op jit(solution)/shard_map/concatenate | solution.py:697
  14.8 0.0 collective-permute-done.2.row_a
  14.8 0.0 collective-permute-done.3.row_b
  14.8 1.4 %middle.1 = (f32[4,24,8,256]{3,2,1,0:T(8,128)S(1)}, f32[4,24,8,256]{3,2,1,0:T(8,128)S(1)}) custom-call(f32[3,256,256]{2,1,0:T(8,128)S(1)} %get-tuple-element.30.own, f32[3,64,256]{2,1,0:T(8,128)S(1)} %collective-permute-done.2.row_a, f32[3,64,256]{2,1,0:T(8,128)S(1)} %collective-permute-done.3.row_b, f32[16]{0:T(128)S(1)} %pad_maximum_fusion.table), custom_call_target="tpu_custom_call" | custom-call | tf_op jit(solution)/shard_map/middle/pallas_call | solution.py:628
  16.2 0.0 collective-permute-done.4.corner_a
  16.2 1.1 %collective-permute-done.5.corner_b = f32[3,64,128]{2,1,0:T(8,128)S(1)} collective-permute-done((f32[3,64,128]{2,1,0:T(8,128)S(1)}, f32[3,64,128]{2,1,0:T(8,128)S(1)}, u32[]{:S(2)}, u32[]{:S(2)}) %collective-permute-start.5) | collective-permute-done | bytes 98336 | tf_op jit(solution)/shard_map/ppermute | solution.py:686
  17.3 4.5 %down.1 = (f32[13,26,8,384]{3,2,1,0:T(8,128)S(1)}, f32[13,14,8,256]{3,2,1,0:T(8,128)S(1)}, f32[13,8,8,128]{3,2,1,0:T(8,128)S(1)}, f32[13,5,8,128]{3,2,1,0:T(8,12...) custom-call(f32[4,24,8,256]{3,2,1,0:T(8,128)S(1)} %get-tuple-element.35.rhs0, ...), custom_call_target="tpu_custom_call" | custom-call | tf_op jit(solution)/shard_map/down/pallas_call | solution.py:640
  21.9 32.0 %all_to_all.5 = f32[128,4,128]{2,1,0:T(4,128)S(1)} all-to-all(f32[128,4,128]{2,1,0:T(4,128)S(1)} %bitcast.5), channel_id=1, replica_groups=mesh['z'=8,'core'=2,'col'=16] {'z','col'}, dimensions={0} | all-to-all | bytes 524288 | tf_op jit(solution)/shard_map/all_to_all | solution.py:701
  53.9 3.2 %collective-permute-start.6 = (f32[128,4,128]{2,1,0:T(4,128)S(1)}, f32[128,4,128]{2,1,0:T(4,128)S(1)}, u32[]{:S(2)}, u32[]{:S(2)}) collective-permute-start(f32[128,4,128]{2,1,0:T(4,128)S(1)} %all_to_all.5), channel_id=1, source_target_pairs={{0,16},{16,0},{1,17},{17,1},{2,18},{18,2},{3,19},{19,3},{4,20},{20... | collective-permute-start | bytes 786440 | tf_op jit(solution)/shard_map/ppermute | solution.py:702
  57.1 1.2 %collective-permute-done.6 = f32[128,4,128]{2,1,0:T(4,128)S(1)} collective-permute-done((f32[128,4,128]{2,1,0:T(4,128)S(1)}, f32[128,4,128]{2,1,0:T(4,128)S(1)}, u32[]{:S(2)}, u32[]{:S(2)}) %collective-permute-start.6) | collective-permute-done | bytes 262176 | tf_op jit(solution)/shard_map/ppermute | solution.py:702
  58.2 7.1 %up.1 = f32[2,256,256]{2,1,0:T(8,128)} custom-call(f32[512,128]{1,0:T(8,128)S(1)} %bitcast.3, f32[512,128]{1,0:T(8,128)S(1)} %bitcast.4, f32[4,24,128]{2,1,0:T(8,128)S(1)} %get-tuple-element.40.saved4, f32[13,26,8,384]{3,2,1,0:T(8,128)S(1)} %get-tuple-element.41.rest_0_, f32[13,14,8,256]{3,2,1,0:T(8,128)S(1)} %get-tuple-element.42.rest_1_, ...), custom_call_target="tpu_custom_call" | custom-call | tf_op jit(solution)/shard_map/up/pallas_call | solution.py:659
Async XLA Ops:
  1.0 1.0 %copy-start = (f32[2,256,256]{2,1,0:T(8,128)S(1)}, f32[2,256,256]{2,1,0:T(8,128)}, u32[]{:S(2)}) copy-start(f32[2,256,256]{2,1,0:T(8,128)} %observed.1) | copy-start | bytes 1572868
  2.2 7.4 %collective-permute-start = (f32[3,128,128]{2,1,0:T(8,128)S(1)}, f32[3,128,128]{2,1,0:T(8,128)S(1)}, u32[]{:S(2)}, u32[]{:S(2)}) collective-permute-start(f32[3,128,128]{2,1,0:T(8,128)S(1)} %get-tuple-element.25), channel_id=1, source_target_pairs={{0,1},{2,3},{4,5},{6,7},{8,9},{10,11},{12,13},{14,15},{1,0},{3,2},... | collective-permute-start | bytes 589832 | tf_op jit(solution)/shard_map/ppermute | solution.py:686
  4.4 5.2 %collective-permute-start.1 = (f32[3,128,128]{2,1,0:T(8,128)S(1)}, f32[3,128,128]{2,1,0:T(8,128)S(1)}, u32[]{:S(2)}, u32[]{:S(2)}) collective-permute-start(f32[3,128,128]{2,1,0:T(8,128)S(1)} %get-tuple-element.26), channel_id=1, source_target_pairs={{1,2},{3,4},{5,6},{7,8},{9,10},{11,12},{13,14},{2,1},{4,3},{6,5},{... | collective-permute-start | bytes 589832 | tf_op jit(solution)/shard_map/ppermute | solution.py:686
  5.1 9.8 %collective-permute-start.2 = (f32[3,64,256]{2,1,0:T(8,128)S(1)}, f32[3,64,256]{2,1,0:T(8,128)S(1)}, u32[]{:S(2)}, u32[]{:S(2)}) collective-permute-start(f32[3,64,256]{2,1,0:T(8,128)S(1)} %get-tuple-element.31), channel_id=1, source_target_pairs={{0,16},{32,48},{64,80},{96,112},{128,144},{160,176},{192,208},{224... | collective-permute-start | bytes 589832 | tf_op jit(solution)/shard_map/ppermute | solution.py:686
  6.3 8.5 %collective-permute-start.3 = (f32[3,64,256]{2,1,0:T(8,128)S(1)}, f32[3,64,256]{2,1,0:T(8,128)S(1)}, u32[]{:S(2)}, u32[]{:S(2)}) collective-permute-start(f32[3,64,256]{2,1,0:T(8,128)S(1)} %get-tuple-element.32), channel_id=1, source_target_pairs={{16,32},{48,64},{80,96},{112,128},{144,160},{176,192},{208,224},{3... | collective-permute-start | bytes 589832 | tf_op jit(solution)/shard_map/ppermute | solution.py:686
  9.7 6.5 %collective-permute-start.4 = (f32[3,64,128]{2,1,0:T(8,128)S(1)}, f32[3,64,128]{2,1,0:T(8,128)S(1)}, u32[]{:S(2)}, u32[]{:S(2)}) collective-permute-start(f32[3,64,128]{2,1,0:T(8,128)S(1)} %get-tuple-element.37), channel_id=1, source_target_pairs={{0,16},{32,48},{64,80},{96,112},{128,144},{160,176},{192,208},{224... | collective-permute-start | bytes 294920 | tf_op jit(solution)/shard_map/ppermute | solution.py:686
  11.4 5.9 %collective-permute-start.5 = (f32[3,64,128]{2,1,0:T(8,128)S(1)}, f32[3,64,128]{2,1,0:T(8,128)S(1)}, u32[]{:S(2)}, u32[]{:S(2)}) collective-permute-start(f32[3,64,128]{2,1,0:T(8,128)S(1)} %get-tuple-element.38), channel_id=1, source_target_pairs={{16,32},{48,64},{80,96},{112,128},{144,160},{176,192},{208,224},{3... | collective-permute-start | bytes 294920 | tf_op jit(solution)/shard_map/ppermute | solution.py:686
  53.9 4.4 %collective-permute-start.6 = (f32[128,4,128]{2,1,0:T(4,128)S(1)}, f32[128,4,128]{2,1,0:T(4,128)S(1)}, u32[]{:S(2)}, u32[]{:S(2)}) collective-permute-start(f32[128,4,128]{2,1,0:T(4,128)S(1)} %all_to_all.5), channel_id=1, source_target_pairs={{0,16},{16,0},{1,17},{17,1},{2,18},{18,2},{3,19},{19,3},{4,20},{20... | collective-permute-start | bytes 786440 | tf_op jit(solution)/shard_map/ppermute | solution.py:702

commit v7 on v5

--- a/solution.py
+++ b/solution.py
@@ -174,8 +174,38 @@
     return jnp.where(even, x, y), jnp.where(even, y, x)
 
 
-def middle_kernel(own, row_a, row_b, table, rhs, gw, frame):
-    row, _ = place()
+def small_patterns(col):
+    x, y = iota((128, 128), 0), iota((128, 128), 1)
+    same = x // 64 == y // 64
+    result = [coarse_lane(2, x) == y, side_lane(0, x) == y, side_lane(1, x) == y]
+    result.append(jnp.logical_and(same, (x % 64) // 2 == y % 8))
+    result.append(jnp.logical_and(same, x % 64 == y % 16))
+    result.append(jnp.logical_and(same, x % 64 == y % 4))
+    result.append(jnp.logical_and(same, x % 64 == y % 4 + 12))
+    result += [side_lane(0, y) == x, side_lane(1, y) == x, coarse_lane(2, y) == x]
+    for f in range(2):
+        c = (y + 32) % 128 - 32 - 64 * f
+        result.append(jnp.logical_and(jnp.logical_and(c >= -32, c < 32), x == col * 8 + (c >> 1)))
+    base = (x // 64) * 64
+    j, c = x % 16, x % 4
+    result.append(y == base + j)
+    result.append(jnp.logical_and(j >= 12, y == (base + j - 16) % 128))
+    result.append(jnp.logical_and(j < 4, y == base + 16 + j))
+    result.append(y == (base + c - 4) % 128)
+    result.append(y == base + 16 + c)
+    return result
+
+
+(TO_4, TO_5, COMMON, ROWS, LEFT, RIGHT, FROM_4, FROM_3, COLS, AROUND) = (0, 1, 3, 4, 5, 6, 7, 9, 10, 12)
+BIG = ((384, 256), (256, 128), (128, 256), (256, 384))
+
+
+def middle_kernel(own, row_a, row_b, table, rhs, gw, small, down0, down1, up1, up0, frame):
+    row, col = place()
+    for i, pattern in enumerate(small_patterns(col)):
+        small[i] = onehot(pattern)
+    for level, fine, ref in ((0, 0, down0), (1, 0, down1), (1, 1, up1), (0, 1, up0)):
+        ref[...] = onehot(coarse_lane(level, iota(ref.shape, fine)) == iota(ref.shape, 1 - fine))
     for f in range(3):
         for half in range(2):
             lanes = slice(half * 128, half * 128 + 128)
@@ -199,7 +229,7 @@
     loop(24, pack, 12)
 
 
-def down_kernel(rhs0, gw0, col_a, col_b, corner_a, corner_b, table, *rest):
+def down_kernel(rhs0, gw0, small, down0, down1, col_a, col_b, corner_a, corner_b, table, *rest):
     states = rest[:4]
     saved4, message = rest[4:6]
     gw, red, full, sums, frame, nat = rest[6:]
@@ -285,15 +315,13 @@
                 sums[f, a, :, here] = pull_red(a, state.at[BLACK : BLACK + 2], f, state, even)
 
         loop(count, restrict, unroll)
-        fine = iota((width, LANES[level + 1]), 0)
-        lane = iota((width, LANES[level + 1]), 1)
         if level < 3:
-            pattern = onehot(coarse_lane(level, fine) == lane)
+            pattern = (down0[...], down1[...], small[TO_4])[level]
             for q in range(4):
                 x = sums[q, 0:count, :, here].reshape(count * 8, width)
                 full[q, 0:count, :, pl.ds(0, LANES[level + 1])] = times(x, pattern).reshape(count, 8, LANES[level + 1])
         else:
-            first, second = (onehot(side_lane(f, fine) == lane) for f in range(2))
+            first, second = small[TO_5], small[TO_5 + 1]
             x = [sums[q, 0:3, :, here].reshape(24, 128) for q in range(4)]
             results = [times(x[0], first) + times(x[1], second)] + [times(x[q], first + second) for q in (2, 3)]
             for q in range(3):
@@ -313,23 +341,17 @@
     nat[3] = jnp.where(is_red, pull4(k, v), 0.0)
     nat[4] = jnp.where(iota((24, 128), 1) < 64, 0.5 * g, w)
 
-    lane = iota((128, 128), 0)
-    l = iota((128, 128), 1)
     sub, at = iota((8, 128), 0), iota((8, 128), 1)
-    pattern = onehot(jnp.logical_and(lane // 64 == l // 64, (lane % 64) // 2 == l % 8))
     mine = sub == (at // 8) % 8
     common = []
     for q in (3, 4):
         x = nat[q, pl.ds(0, 8, stride=2), :] + nat[q, pl.ds(1, 8, stride=2), :]
-        common.append(message_row(x, pattern, mine))
-    pattern = onehot(jnp.logical_and(lane // 64 == l // 64, lane % 64 == l % 16))
-    top = message_row(merged[0:8], pattern, sub == (at // 16) % 4)
-    bottom = message_row(merged[8:16], pattern, sub == (at // 16) % 4 + 4)
+        common.append(message_row(x, small[COMMON], mine))
+    top = message_row(merged[0:8], small[ROWS], sub == (at // 16) % 4)
+    bottom = message_row(merged[8:16], small[ROWS], sub == (at // 16) % 4 + 4)
     mine = iota((16, 128), 0) == (iota((16, 128), 1) // 4) % 16
-    pattern = onehot(jnp.logical_and(lane // 64 == l // 64, lane % 64 == l % 4))
-    left = message_row(merged[0:16], pattern, mine)
-    pattern = onehot(jnp.logical_and(lane // 64 == l // 64, lane % 64 == l % 4 + 12))
-    right = message_row(merged[0:16], pattern, mine)
+    left = message_row(merged[0:16], small[LEFT], mine)
+    right = message_row(merged[0:16], small[RIGHT], mine)
 
     block = jnp.concatenate((common + [jnp.zeros((2, 128), F32)]) * 8, axis=0)
 
@@ -458,7 +480,7 @@
             e[f, t] = e[f, t] + alpha * (r[f, t] + beta * d[f, t])
 
 
-def merged_frame(mine, theirs, merged):
+def merged_frame(mine, theirs, small, merged):
     row, col = place()
     at = iota((24, 128), 0)
     l = iota((24, 128), 1)
@@ -474,25 +496,14 @@
             ours = at == (l // 4) % 16
         key = dc if dr else 2 * dc
         total[key] = total.get(key, 0.0) + jnp.where(ours, jnp.broadcast_to(x, (24, 128)), 0.0)
-    l = iota((128, 128), 0)
-    lane = iota((128, 128), 1)
-    base = (l // 64) * 64
-    j, c = l % 16, l % 4
-    patterns = {
-        0: lane == base + j,
-        -1: jnp.logical_and(j >= 12, lane == (base + j - 16) % 128),
-        1: jnp.logical_and(j < 4, lane == base + 16 + j),
-        -2: lane == (base + c - 4) % 128,
-        2: lane == base + 16 + c,
-    }
     own = jnp.logical_and(at < 16, iota((24, 128), 1) % 64 < 16)
     result = jnp.where(own, merged, 0.0)
     for key, x in total.items():
-        result += times(x, onehot(patterns[key]))
+        result += times(x, small[AROUND + (0, -1, 1, -2, 2).index(key)])
     return result
 
 
-def up_kernel(mine, theirs, saved4, *rest):
+def up_kernel(mine, theirs, small, up1, up0, saved4, *rest):
     states, out = rest[:4], rest[4]
     full, red, blk, mix, kc, e, d, s, w, r, result, nat, sent = rest[5:]
     cg(mine, theirs, mix, kc, e, d, s, w, r)
@@ -502,17 +513,13 @@
     at = iota((24, 128), 0)
     grid_row = (n // 64) * 64 + (n % 8) * 8 + (n // 8) % 8
     rows = onehot(grid_row == row * 8 + (jnp.where(at < 20, at, at - 24) >> 1))
-    j = iota((128, 128), 0)
-    lane = iota((128, 128), 1)
     correction = 0.0
     for f in range(2):
-        c = (lane + 32) % 128 - 32 - 64 * f
-        cols = onehot(jnp.logical_and(jnp.logical_and(c >= -32, c < 32), j == col * 8 + (c >> 1)))
         whole = jnp.concatenate([e[f, t] for t in range(16)], axis=0)
-        correction += times(pick(rows, whole), cols)
+        correction += times(pick(rows, whole), small[COLS + f])
 
     is_red = red4()
-    merged = merged_frame(mine, theirs, saved4[0])
+    merged = merged_frame(mine, theirs, small, saved4[0])
     k, inv = edges4(saved4[2], saved4[3])
     x = jnp.where(is_red, 0.0, merged + correction)
     x = jnp.where(is_red, (merged + pull4(k, x)) * inv, 0.0)
@@ -526,12 +533,10 @@
         unroll = (24, 12, 6, 3)[level]
         here = pl.ds(0, width)
         if level == 3:
-            lane, wide = iota((128, 128), 0), iota((128, 128), 1)
-            corrections = [times(ordered, onehot(side_lane(f, wide) == lane)) for f in range(2)]
+            corrections = [times(ordered, small[FROM_4 + f]) for f in range(2)]
         else:
             coarse = LANES[level + 1]
-            lane, wide = iota((coarse, width), 0), iota((coarse, width), 1)
-            pattern = onehot(coarse_lane(level, wide) == lane)
+            pattern = (up0[...], up1[...], small[FROM_3])[level]
             corrections = [
                 times(full[f, 0:count, :, pl.ds(0, coarse)].reshape(count * 8, coarse), pattern) for f in range(2)
             ]
@@ -622,9 +627,9 @@
 def middle(own, row_a, row_b, table):
     return pl.pallas_call(
         middle_kernel,
-        out_shape=[shaped(4, 24, 8, 256)] * 2,
+        out_shape=[shaped(4, 24, 8, 256)] * 2 + [jax.ShapeDtypeStruct(x, BF16) for x in ((17, 128, 128), *BIG)],
         in_specs=[VMEM] * 3 + [SMEM],
-        out_specs=[VMEM] * 2,
+        out_specs=[VMEM] * 7,
         scratch_shapes=[scratch(3, 2, 384, 128)],
         compiler_params=PARAMS,
         name="middle",
@@ -635,7 +640,7 @@
     return pl.pallas_call(
         down_kernel,
         out_shape=[shaped(*s) for s in state_shapes()] + [shaped(4, 24, 128), shaped(512, 128)],
-        in_specs=[VMEM] * 6 + [SMEM],
+        in_specs=[VMEM] * 9 + [SMEM],
         out_specs=[VMEM] * 6,
         scratch_shapes=[
             scratch(4, 26, 8, 384),
@@ -650,11 +655,11 @@
     )(*args)
 
 
-def up(mine, theirs, saved4, saved):
+def up(mine, theirs, small, up1, up0, saved4, saved):
     return pl.pallas_call(
         up_kernel,
         out_shape=shaped(2, 256, 256),
-        in_specs=[VMEM] * 7,
+        in_specs=[VMEM] * 10,
         out_specs=ANY,
         scratch_shapes=[
             scratch(2, 24, 8, 256),
@@ -673,7 +678,7 @@
         ],
         compiler_params=PARAMS,
         name="up",
-    )(mine, theirs, saved4, *saved)
+    )(mine, theirs, small, up1, up0, saved4, *saved)
 
 
 def swap(x, axis, first):
@@ -690,12 +695,12 @@
     corner_a, corner_b, own, row_a, row_b, class_weight, class_stiffness = held
     corner_a, corner_b = swap(corner_a, "col", 0), swap(corner_b, "col", 1)
     table = jnp.concatenate([class_weight, class_stiffness])
-    rhs, gw = middle(own, row_a, row_b, table)
-    results = down(rhs, gw, col_a, col_b, corner_a, corner_b, table)
+    rhs, gw, small, down0, down1, up1, up0 = middle(own, row_a, row_b, table)
+    results = down(rhs, gw, small, down0, down1, col_a, col_b, corner_a, corner_b, table)
     *saved, saved4, message = results
     mine = lax.all_to_all(message.reshape(128, 4, 128), ("z", "col"), 0, 0)
     theirs = lax.ppermute(mine, "core", [(0, 1), (1, 0)])
-    return up(mine.reshape(512, 128), theirs.reshape(512, 128), saved4, saved)
+    return up(mine.reshape(512, 128), theirs.reshape(512, 128), small, up1, up0, saved4, saved)
 
 
 def solution(mesh):

time: 64 us -> 63.9 us (level)
  transfers between devices with their start and end apart: 7 -> 7, of which waited for: 3 -> 3; matrix products, arithmetic and copies ran while one was open for 1% -> 1% of each run, Pallas kernels for 2% -> 3%
where the time goes in v7:
time: 63.9 us; the launch traced here: 63.6 us
  blocking collectives  30.9 us (48%)
  Pallas kernels  13.4 us (21%)
  starting transfers between devices  11.5 us (18%)
  waiting for transfers between devices  5.01 us (8%)
  other arithmetic  1.72 us (3%)
  local copies, waits for them, and re-layouts  1.04 us (2%)
    all_to_all x1, blocking collectives, local(): mine = lax.all_to_all(message.reshape(128, 4, 128), ('z', 'col'), 0, 0)  30.9 us
    ppermute x6, starting transfers between devices, swap(): return lax.ppermute(x, axis, pairs + [(j, i) for i, j in pairs])  7.88 us
    pallas_call x1, Pallas kernels, up(): pl.pallas_call(up_kernel, out_shape=shaped(2, 256, 256), in_specs=[VMEM]...  6.96 us
    pallas_call x1, Pallas kernels, down(): pl.pallas_call(down_kernel, out_shape=[shaped(*s) for s in state_shapes()...  4.53 us
    ppermute x6, waiting for transfers between devices, swap(): return lax.ppermute(x, axis, pairs + [(j, i) for i, j in pairs])  3.85 us
    ppermute x1, starting transfers between devices, local(): theirs = lax.ppermute(mine, 'core', [(0, 1), (1, 0)])  3.61 us
    pallas_call x1, Pallas kernels, middle(): pl.pallas_call(middle_kernel, out_shape=[shaped(4, 24, 8, 256)] * 2 + [ja...  1.64 us
  transfers between devices with their start and end apart: 7, of which 3 were waited for; matrix products, arithmetic and copies ran while one was open for 1% of the time, Pallas kernels for 3%

profile of v7, /device:TPU:1, one launch (start us, length us, event | category | flops | bytes accessed | tf_op | source)
XLA Modules:
  0.0 63.6 jit_solution(16880343417805897897)
XLA Ops:
  0.0 1.0 %add_convert_fusion.classes = f32[256,256]{1,0:T(8,128)S(1)} fusion(s32[256,256]{1,0:T(8,128)} %param.5), kind=kLoop, calls=%fused_computation | loop fusion | flops 131072 | bytes 524288 | tf_op jit(solution)/shard_map/convert_element_type | solution.py:690
  1.0 0.0 copy-start
  1.0 1.0 %copy-done = f32[2,256,256]{2,1,0:T(8,128)S(1)} copy-done((f32[2,256,256]{2,1,0:T(8,128)S(1)}, f32[2,256,256]{2,1,0:T(8,128)}, u32[]{:S(2)}) %copy-start) | copy-done | bytes 524312
  2.0 0.2 sides.1
  2.2 3.3 %collective-permute-start = (f32[3,64,256]{2,1,0:T(8,128)S(1)}, f32[3,64,256]{2,1,0:T(8,128)S(1)}, u32[]{:S(2)}, u32[]{:S(2)}) collective-permute-start(f32[3,64,256]{2,1,0:T(8,128)S(1)} %get-tuple-element.32), channel_id=1, source_target_pairs={{0,16},{32,48},{64,80},{96,112},{128,144},{160,176},{192,208},{224... | collective-permute-start | bytes 589832 | tf_op jit(solution)/shard_map/ppermute | solution.py:686
  5.5 1.9 %collective-permute-start.1 = (f32[3,64,256]{2,1,0:T(8,128)S(1)}, f32[3,64,256]{2,1,0:T(8,128)S(1)}, u32[]{:S(2)}, u32[]{:S(2)}) collective-permute-start(f32[3,64,256]{2,1,0:T(8,128)S(1)} %get-tuple-element.33), channel_id=1, source_target_pairs={{16,32},{48,64},{80,96},{112,128},{144,160},{176,192},{208,224},{3... | collective-permute-start | bytes 589832 | tf_op jit(solution)/shard_map/ppermute | solution.py:686
  7.4 1.2 %collective-permute-start.2 = (f32[3,128,128]{2,1,0:T(8,128)S(1)}, f32[3,128,128]{2,1,0:T(8,128)S(1)}, u32[]{:S(2)}, u32[]{:S(2)}) collective-permute-start(f32[3,128,128]{2,1,0:T(8,128)S(1)} %get-tuple-element.47), channel_id=1, source_target_pairs={{0,1},{2,3},{4,5},{6,7},{8,9},{10,11},{12,13},{14,15},{1,0},{3,2},... | collective-permute-start | bytes 589832 | tf_op jit(solution)/shard_map/ppermute | solution.py:686
  8.6 0.7 %collective-permute-start.3 = (f32[3,128,128]{2,1,0:T(8,128)S(1)}, f32[3,128,128]{2,1,0:T(8,128)S(1)}, u32[]{:S(2)}, u32[]{:S(2)}) collective-permute-start(f32[3,128,128]{2,1,0:T(8,128)S(1)} %get-tuple-element.48), channel_id=1, source_target_pairs={{1,2},{3,4},{5,6},{7,8},{9,10},{11,12},{13,14},{2,1},{4,3},{6,5},{... | collective-permute-start | bytes 589832 | tf_op jit(solution)/shard_map/ppermute | solution.py:686
  9.3 0.0 collective-permute-done.row_a
  9.3 3.5 %collective-permute-done.1.row_b = f32[3,64,256]{2,1,0:T(8,128)S(1)} collective-permute-done((f32[3,64,256]{2,1,0:T(8,128)S(1)}, f32[3,64,256]{2,1,0:T(8,128)S(1)}, u32[]{:S(2)}, u32[]{:S(2)}) %collective-permute-start.1) | collective-permute-done | bytes 196640 | tf_op jit(solution)/shard_map/ppermute | solution.py:686
  12.8 0.1 corners.1
  12.9 0.1 collective-permute-start.4
  13.1 0.7 %collective-permute-start.5 = (f32[3,64,128]{2,1,0:T(8,128)S(1)}, f32[3,64,128]{2,1,0:T(8,128)S(1)}, u32[]{:S(2)}, u32[]{:S(2)}) collective-permute-start(f32[3,64,128]{2,1,0:T(8,128)S(1)} %get-tuple-element.50), channel_id=1, source_target_pairs={{1,2},{3,4},{5,6},{7,8},{9,10},{11,12},{13,14},{2,1},{4,3},{6,5},{... | collective-permute-start | bytes 294920 | tf_op jit(solution)/shard_map/ppermute | solution.py:686
  13.7 0.7 %pad_maximum_fusion.table = f32[16]{0:T(128)S(1)} fusion(f32[8]{0:T(128)} %param.7, f32[8]{0:T(128)} %param.6), kind=kLoop, calls=%fused_computation.1 | loop fusion | flops 16 | bytes 128 | tf_op jit(solution)/shard_map/concatenate | solution.py:697
  14.5 1.6 %middle.1 = (f32[4,24,8,256]{3,2,1,0:T(8,128)S(1)}, f32[4,24,8,256]{3,2,1,0:T(8,128)S(1)}, bf16[17,128,128]{2,1,0:T(8,128)(2,1)S(1)}, bf16[384,256]{1,0:T(8,128)...) custom-call(f32[3,256,256]{2,1,0:T(8,128)S(1)} %get-tuple-element.37.own, ...), custom_call_target="tpu_custom_call" | custom-call | tf_op jit(solution)/shard_map/middle/pallas_call | solution.py:628
  16.1 0.0 collective-permute-done.2.col_a
  16.1 0.0 collective-permute-done.3.col_b
  16.1 0.3 collective-permute-done.4.corner_a
  16.5 0.0 collective-permute-done.5.corner_b
  16.5 4.5 %down.1 = (f32[13,26,8,384]{3,2,1,0:T(8,128)S(1)}, f32[13,14,8,256]{3,2,1,0:T(8,128)S(1)}, f32[13,8,8,128]{3,2,1,0:T(8,128)S(1)}, f32[13,5,8,128]{3,2,1,0:T(8,12...) custom-call(f32[4,24,8,256]{3,2,1,0:T(8,128)S(1)} %get-tuple-element.42.rhs0, ...), custom_call_target="tpu_custom_call" | custom-call | tf_op jit(solution)/shard_map/down/pallas_call | solution.py:640
  21.0 30.9 %all_to_all.5 = f32[128,4,128]{2,1,0:T(4,128)S(1)} all-to-all(f32[128,4,128]{2,1,0:T(4,128)S(1)} %bitcast.5), channel_id=1, replica_groups=mesh['z'=8,'core'=2,'col'=16] {'z','col'}, dimensions={0} | all-to-all | bytes 524288 | tf_op jit(solution)/shard_map/all_to_all | solution.py:701
  51.9 3.6 %collective-permute-start.6 = (f32[128,4,128]{2,1,0:T(4,128)S(1)}, f32[128,4,128]{2,1,0:T(4,128)S(1)}, u32[]{:S(2)}, u32[]{:S(2)}) collective-permute-start(f32[128,4,128]{2,1,0:T(4,128)S(1)} %all_to_all.5), channel_id=1, source_target_pairs={{0,16},{16,0},{1,17},{17,1},{2,18},{18,2},{3,19},{19,3},{4,20},{20... | collective-permute-start | bytes 786440 | tf_op jit(solution)/shard_map/ppermute | solution.py:702
  55.5 1.2 %collective-permute-done.6 = f32[128,4,128]{2,1,0:T(4,128)S(1)} collective-permute-done((f32[128,4,128]{2,1,0:T(4,128)S(1)}, f32[128,4,128]{2,1,0:T(4,128)S(1)}, u32[]{:S(2)}, u32[]{:S(2)}) %collective-permute-start.6) | collective-permute-done | bytes 262176 | tf_op jit(solution)/shard_map/ppermute | solution.py:702
  56.7 7.0 %up.1 = f32[2,256,256]{2,1,0:T(8,128)} custom-call(f32[512,128]{1,0:T(8,128)S(1)} %bitcast.3, f32[512,128]{1,0:T(8,128)S(1)} %bitcast.4, bf16[17,128,128]{2,1,0:T(8,128)(2,1)S(1)} %get-tuple-element.44.small, bf16[128,256]{1,0:T(8,128)(2,1)S(1)} %get-tuple-element.52.up1, bf16[256,384]{1,0:T(8,128)(2,1)S(1)} %get-tuple-element.53.up0, ...), custom_call_target="tpu_custom_call" | custom-call | tf_op jit(solution)/shard_map/up/pallas_call | solution.py:659
Async XLA Ops:
  1.0 1.0 %copy-start = (f32[2,256,256]{2,1,0:T(8,128)S(1)}, f32[2,256,256]{2,1,0:T(8,128)}, u32[]{:S(2)}) copy-start(f32[2,256,256]{2,1,0:T(8,128)} %observed.1) | copy-start | bytes 1572868
  2.2 7.1 %collective-permute-start = (f32[3,64,256]{2,1,0:T(8,128)S(1)}, f32[3,64,256]{2,1,0:T(8,128)S(1)}, u32[]{:S(2)}, u32[]{:S(2)}) collective-permute-start(f32[3,64,256]{2,1,0:T(8,128)S(1)} %get-tuple-element.32), channel_id=1, source_target_pairs={{0,16},{32,48},{64,80},{96,112},{128,144},{160,176},{192,208},{224... | collective-permute-start | bytes 589832 | tf_op jit(solution)/shard_map/ppermute | solution.py:686
  5.5 7.3 %collective-permute-start.1 = (f32[3,64,256]{2,1,0:T(8,128)S(1)}, f32[3,64,256]{2,1,0:T(8,128)S(1)}, u32[]{:S(2)}, u32[]{:S(2)}) collective-permute-start(f32[3,64,256]{2,1,0:T(8,128)S(1)} %get-tuple-element.33), channel_id=1, source_target_pairs={{16,32},{48,64},{80,96},{112,128},{144,160},{176,192},{208,224},{3... | collective-permute-start | bytes 589832 | tf_op jit(solution)/shard_map/ppermute | solution.py:686
  7.4 8.7 %collective-permute-start.2 = (f32[3,128,128]{2,1,0:T(8,128)S(1)}, f32[3,128,128]{2,1,0:T(8,128)S(1)}, u32[]{:S(2)}, u32[]{:S(2)}) collective-permute-start(f32[3,128,128]{2,1,0:T(8,128)S(1)} %get-tuple-element.47), channel_id=1, source_target_pairs={{0,1},{2,3},{4,5},{6,7},{8,9},{10,11},{12,13},{14,15},{1,0},{3,2},... | collective-permute-start | bytes 589832 | tf_op jit(solution)/shard_map/ppermute | solution.py:686
  8.6 7.5 %collective-permute-start.3 = (f32[3,128,128]{2,1,0:T(8,128)S(1)}, f32[3,128,128]{2,1,0:T(8,128)S(1)}, u32[]{:S(2)}, u32[]{:S(2)}) collective-permute-start(f32[3,128,128]{2,1,0:T(8,128)S(1)} %get-tuple-element.48), channel_id=1, source_target_pairs={{1,2},{3,4},{5,6},{7,8},{9,10},{11,12},{13,14},{2,1},{4,3},{6,5},{... | collective-permute-start | bytes 589832 | tf_op jit(solution)/shard_map/ppermute | solution.py:686
  12.9 3.6 %collective-permute-start.4 = (f32[3,64,128]{2,1,0:T(8,128)S(1)}, f32[3,64,128]{2,1,0:T(8,128)S(1)}, u32[]{:S(2)}, u32[]{:S(2)}) collective-permute-start(f32[3,64,128]{2,1,0:T(8,128)S(1)} %get-tuple-element.49), channel_id=1, source_target_pairs={{0,1},{2,3},{4,5},{6,7},{8,9},{10,11},{12,13},{14,15},{1,0},{3,2},... | collective-permute-start | bytes 294920 | tf_op jit(solution)/shard_map/ppermute | solution.py:686
  13.1 3.4 %collective-permute-start.5 = (f32[3,64,128]{2,1,0:T(8,128)S(1)}, f32[3,64,128]{2,1,0:T(8,128)S(1)}, u32[]{:S(2)}, u32[]{:S(2)}) collective-permute-start(f32[3,64,128]{2,1,0:T(8,128)S(1)} %get-tuple-element.50), channel_id=1, source_target_pairs={{1,2},{3,4},{5,6},{7,8},{9,10},{11,12},{13,14},{2,1},{4,3},{6,5},{... | collective-permute-start | bytes 294920 | tf_op jit(solution)/shard_map/ppermute | solution.py:686
  51.9 4.8 %collective-permute-start.6 = (f32[128,4,128]{2,1,0:T(4,128)S(1)}, f32[128,4,128]{2,1,0:T(4,128)S(1)}, u32[]{:S(2)}, u32[]{:S(2)}) collective-permute-start(f32[128,4,128]{2,1,0:T(4,128)S(1)} %all_to_all.5), channel_id=1, source_target_pairs={{0,16},{16,0},{1,17},{17,1},{2,18},{18,2},{3,19},{19,3},{4,20},{20... | collective-permute-start | bytes 786440 | tf_op jit(solution)/shard_map/ppermute | solution.py:702

commit v8 on v7

--- a/solution.py
+++ b/solution.py
@@ -473,7 +473,9 @@
             result.append((fresh[f][0], fresh[f][0] / (fresh[f][1] - beta * fresh[f][0] / alpha), beta))
         return tuple(result)
 
-    state = lax.fori_loop(0, CG_ITERS - 1, iterate, tuple(state))
+    state = tuple(state)
+    for i in range(CG_ITERS - 1):
+        state = iterate(i, state)
     for f in range(2):
         _, alpha, beta = state[f]
         for t in range(16):

time: 63.9 us -> 63.7 us (level)
  no operation moved by 1% of the time
where the time goes in v8:
time: 63.7 us; the launch traced here: 63.4 us
  blocking collectives  30.9 us (49%)
  Pallas kernels  13 us (20%)
  starting transfers between devices  11.5 us (18%)
  waiting for transfers between devices  5.01 us (8%)
  other arithmetic  1.72 us (3%)
  local copies, waits for them, and re-layouts  1.04 us (2%)
    all_to_all x1, blocking collectives, local(): mine = lax.all_to_all(message.reshape(128, 4, 128), ('z', 'col'), 0, 0)  30.9 us
    ppermute x6, starting transfers between devices, swap(): return lax.ppermute(x, axis, pairs + [(j, i) for i, j in pairs])  7.88 us
    pallas_call x1, Pallas kernels, up(): pl.pallas_call(up_kernel, out_shape=shaped(2, 256, 256), in_specs=[VMEM]...  6.57 us
    pallas_call x1, Pallas kernels, down(): pl.pallas_call(down_kernel, out_shape=[shaped(*s) for s in state_shapes()...  4.53 us
    ppermute x6, waiting for transfers between devices, swap(): return lax.ppermute(x, axis, pairs + [(j, i) for i, j in pairs])  3.85 us
    ppermute x1, starting transfers between devices, local(): theirs = lax.ppermute(mine, 'core', [(0, 1), (1, 0)])  3.61 us
    pallas_call x1, Pallas kernels, middle(): pl.pallas_call(middle_kernel, out_shape=[shaped(4, 24, 8, 256)] * 2 + [ja...  1.64 us
  transfers between devices with their start and end apart: 7, of which 3 were waited for; matrix products, arithmetic and copies ran while one was open for 1% of the time, Pallas kernels for 3%

profile of v8, /device:TPU:1, one launch (start us, length us, event | category | flops | bytes accessed | tf_op | source)
XLA Modules:
  0.0 63.4 jit_solution(159266238469375261)
XLA Ops:
  0.0 1.0 %add_convert_fusion.classes = f32[256,256]{1,0:T(8,128)S(1)} fusion(s32[256,256]{1,0:T(8,128)} %param.5), kind=kLoop, calls=%fused_computation | loop fusion | flops 131072 | bytes 524288 | tf_op jit(solution)/shard_map/convert_element_type | solution.py:692
  1.0 0.0 copy-start
  1.0 1.0 %copy-done = f32[2,256,256]{2,1,0:T(8,128)S(1)} copy-done((f32[2,256,256]{2,1,0:T(8,128)S(1)}, f32[2,256,256]{2,1,0:T(8,128)}, u32[]{:S(2)}) %copy-start) | copy-done | bytes 524312
  2.0 0.2 sides.1
  2.2 3.3 %collective-permute-start = (f32[3,64,256]{2,1,0:T(8,128)S(1)}, f32[3,64,256]{2,1,0:T(8,128)S(1)}, u32[]{:S(2)}, u32[]{:S(2)}) collective-permute-start(f32[3,64,256]{2,1,0:T(8,128)S(1)} %get-tuple-element.32), channel_id=1, source_target_pairs={{0,16},{32,48},{64,80},{96,112},{128,144},{160,176},{192,208},{224... | collective-permute-start | bytes 589832 | tf_op jit(solution)/shard_map/ppermute | solution.py:688
  5.5 1.9 %collective-permute-start.1 = (f32[3,64,256]{2,1,0:T(8,128)S(1)}, f32[3,64,256]{2,1,0:T(8,128)S(1)}, u32[]{:S(2)}, u32[]{:S(2)}) collective-permute-start(f32[3,64,256]{2,1,0:T(8,128)S(1)} %get-tuple-element.33), channel_id=1, source_target_pairs={{16,32},{48,64},{80,96},{112,128},{144,160},{176,192},{208,224},{3... | collective-permute-start | bytes 589832 | tf_op jit(solution)/shard_map/ppermute | solution.py:688
  7.4 1.2 %collective-permute-start.2 = (f32[3,128,128]{2,1,0:T(8,128)S(1)}, f32[3,128,128]{2,1,0:T(8,128)S(1)}, u32[]{:S(2)}, u32[]{:S(2)}) collective-permute-start(f32[3,128,128]{2,1,0:T(8,128)S(1)} %get-tuple-element.47), channel_id=1, source_target_pairs={{0,1},{2,3},{4,5},{6,7},{8,9},{10,11},{12,13},{14,15},{1,0},{3,2},... | collective-permute-start | bytes 589832 | tf_op jit(solution)/shard_map/ppermute | solution.py:688
  8.6 0.7 %collective-permute-start.3 = (f32[3,128,128]{2,1,0:T(8,128)S(1)}, f32[3,128,128]{2,1,0:T(8,128)S(1)}, u32[]{:S(2)}, u32[]{:S(2)}) collective-permute-start(f32[3,128,128]{2,1,0:T(8,128)S(1)} %get-tuple-element.48), channel_id=1, source_target_pairs={{1,2},{3,4},{5,6},{7,8},{9,10},{11,12},{13,14},{2,1},{4,3},{6,5},{... | collective-permute-start | bytes 589832 | tf_op jit(solution)/shard_map/ppermute | solution.py:688
  9.3 0.0 collective-permute-done.row_a
  9.3 3.5 %collective-permute-done.1.row_b = f32[3,64,256]{2,1,0:T(8,128)S(1)} collective-permute-done((f32[3,64,256]{2,1,0:T(8,128)S(1)}, f32[3,64,256]{2,1,0:T(8,128)S(1)}, u32[]{:S(2)}, u32[]{:S(2)}) %collective-permute-start.1) | collective-permute-done | bytes 196640 | tf_op jit(solution)/shard_map/ppermute | solution.py:688
  12.8 0.1 corners.1
  12.9 0.1 collective-permute-start.4
  13.1 0.7 %collective-permute-start.5 = (f32[3,64,128]{2,1,0:T(8,128)S(1)}, f32[3,64,128]{2,1,0:T(8,128)S(1)}, u32[]{:S(2)}, u32[]{:S(2)}) collective-permute-start(f32[3,64,128]{2,1,0:T(8,128)S(1)} %get-tuple-element.50), channel_id=1, source_target_pairs={{1,2},{3,4},{5,6},{7,8},{9,10},{11,12},{13,14},{2,1},{4,3},{6,5},{... | collective-permute-start | bytes 294920 | tf_op jit(solution)/shard_map/ppermute | solution.py:688
  13.7 0.7 %pad_maximum_fusion.table = f32[16]{0:T(128)S(1)} fusion(f32[8]{0:T(128)} %param.7, f32[8]{0:T(128)} %param.6), kind=kLoop, calls=%fused_computation.1 | loop fusion | flops 16 | bytes 128 | tf_op jit(solution)/shard_map/concatenate | solution.py:699
  14.5 1.6 %middle.1 = (f32[4,24,8,256]{3,2,1,0:T(8,128)S(1)}, f32[4,24,8,256]{3,2,1,0:T(8,128)S(1)}, bf16[17,128,128]{2,1,0:T(8,128)(2,1)S(1)}, bf16[384,256]{1,0:T(8,128)...) custom-call(f32[3,256,256]{2,1,0:T(8,128)S(1)} %get-tuple-element.37.own, ...), custom_call_target="tpu_custom_call" | custom-call | tf_op jit(solution)/shard_map/middle/pallas_call | solution.py:630
  16.1 0.0 collective-permute-done.2.col_a
  16.1 0.0 collective-permute-done.3.col_b
  16.1 0.3 collective-permute-done.4.corner_a
  16.5 0.0 collective-permute-done.5.corner_b
  16.5 4.5 %down.1 = (f32[13,26,8,384]{3,2,1,0:T(8,128)S(1)}, f32[13,14,8,256]{3,2,1,0:T(8,128)S(1)}, f32[13,8,8,128]{3,2,1,0:T(8,128)S(1)}, f32[13,5,8,128]{3,2,1,0:T(8,12...) custom-call(f32[4,24,8,256]{3,2,1,0:T(8,128)S(1)} %get-tuple-element.42.rhs0, ...), custom_call_target="tpu_custom_call" | custom-call | tf_op jit(solution)/shard_map/down/pallas_call | solution.py:642
  21.0 30.9 %all_to_all.5 = f32[128,4,128]{2,1,0:T(4,128)S(1)} all-to-all(f32[128,4,128]{2,1,0:T(4,128)S(1)} %bitcast.5), channel_id=1, replica_groups=mesh['z'=8,'core'=2,'col'=16] {'z','col'}, dimensions={0} | all-to-all | bytes 524288 | tf_op jit(solution)/shard_map/all_to_all | solution.py:703
  51.9 3.6 %collective-permute-start.6 = (f32[128,4,128]{2,1,0:T(4,128)S(1)}, f32[128,4,128]{2,1,0:T(4,128)S(1)}, u32[]{:S(2)}, u32[]{:S(2)}) collective-permute-start(f32[128,4,128]{2,1,0:T(4,128)S(1)} %all_to_all.5), channel_id=1, source_target_pairs={{0,16},{16,0},{1,17},{17,1},{2,18},{18,2},{3,19},{19,3},{4,20},{20... | collective-permute-start | bytes 786440 | tf_op jit(solution)/shard_map/ppermute | solution.py:704
  55.5 1.2 %collective-permute-done.6 = f32[128,4,128]{2,1,0:T(4,128)S(1)} collective-permute-done((f32[128,4,128]{2,1,0:T(4,128)S(1)}, f32[128,4,128]{2,1,0:T(4,128)S(1)}, u32[]{:S(2)}, u32[]{:S(2)}) %collective-permute-start.6) | collective-permute-done | bytes 262176 | tf_op jit(solution)/shard_map/ppermute | solution.py:704
  56.7 6.6 %up.1 = f32[2,256,256]{2,1,0:T(8,128)} custom-call(f32[512,128]{1,0:T(8,128)S(1)} %bitcast.3, f32[512,128]{1,0:T(8,128)S(1)} %bitcast.4, bf16[17,128,128]{2,1,0:T(8,128)(2,1)S(1)} %get-tuple-element.44.small, bf16[128,256]{1,0:T(8,128)(2,1)S(1)} %get-tuple-element.52.up1, bf16[256,384]{1,0:T(8,128)(2,1)S(1)} %get-tuple-element.53.up0, ...), custom_call_target="tpu_custom_call" | custom-call | tf_op jit(solution)/shard_map/up/pallas_call | solution.py:661
Async XLA Ops:
  1.0 1.0 %copy-start = (f32[2,256,256]{2,1,0:T(8,128)S(1)}, f32[2,256,256]{2,1,0:T(8,128)}, u32[]{:S(2)}) copy-start(f32[2,256,256]{2,1,0:T(8,128)} %observed.1) | copy-start | bytes 1572868
  2.2 7.1 %collective-permute-start = (f32[3,64,256]{2,1,0:T(8,128)S(1)}, f32[3,64,256]{2,1,0:T(8,128)S(1)}, u32[]{:S(2)}, u32[]{:S(2)}) collective-permute-start(f32[3,64,256]{2,1,0:T(8,128)S(1)} %get-tuple-element.32), channel_id=1, source_target_pairs={{0,16},{32,48},{64,80},{96,112},{128,144},{160,176},{192,208},{224... | collective-permute-start | bytes 589832 | tf_op jit(solution)/shard_map/ppermute | solution.py:688
  5.5 7.3 %collective-permute-start.1 = (f32[3,64,256]{2,1,0:T(8,128)S(1)}, f32[3,64,256]{2,1,0:T(8,128)S(1)}, u32[]{:S(2)}, u32[]{:S(2)}) collective-permute-start(f32[3,64,256]{2,1,0:T(8,128)S(1)} %get-tuple-element.33), channel_id=1, source_target_pairs={{16,32},{48,64},{80,96},{112,128},{144,160},{176,192},{208,224},{3... | collective-permute-start | bytes 589832 | tf_op jit(solution)/shard_map/ppermute | solution.py:688
  7.4 8.7 %collective-permute-start.2 = (f32[3,128,128]{2,1,0:T(8,128)S(1)}, f32[3,128,128]{2,1,0:T(8,128)S(1)}, u32[]{:S(2)}, u32[]{:S(2)}) collective-permute-start(f32[3,128,128]{2,1,0:T(8,128)S(1)} %get-tuple-element.47), channel_id=1, source_target_pairs={{0,1},{2,3},{4,5},{6,7},{8,9},{10,11},{12,13},{14,15},{1,0},{3,2},... | collective-permute-start | bytes 589832 | tf_op jit(solution)/shard_map/ppermute | solution.py:688
  8.6 7.5 %collective-permute-start.3 = (f32[3,128,128]{2,1,0:T(8,128)S(1)}, f32[3,128,128]{2,1,0:T(8,128)S(1)}, u32[]{:S(2)}, u32[]{:S(2)}) collective-permute-start(f32[3,128,128]{2,1,0:T(8,128)S(1)} %get-tuple-element.48), channel_id=1, source_target_pairs={{1,2},{3,4},{5,6},{7,8},{9,10},{11,12},{13,14},{2,1},{4,3},{6,5},{... | collective-permute-start | bytes 589832 | tf_op jit(solution)/shard_map/ppermute | solution.py:688
  12.9 3.6 %collective-permute-start.4 = (f32[3,64,128]{2,1,0:T(8,128)S(1)}, f32[3,64,128]{2,1,0:T(8,128)S(1)}, u32[]{:S(2)}, u32[]{:S(2)}) collective-permute-start(f32[3,64,128]{2,1,0:T(8,128)S(1)} %get-tuple-element.49), channel_id=1, source_target_pairs={{0,1},{2,3},{4,5},{6,7},{8,9},{10,11},{12,13},{14,15},{1,0},{3,2},... | collective-permute-start | bytes 294920 | tf_op jit(solution)/shard_map/ppermute | solution.py:688
  13.1 3.4 %collective-permute-start.5 = (f32[3,64,128]{2,1,0:T(8,128)S(1)}, f32[3,64,128]{2,1,0:T(8,128)S(1)}, u32[]{:S(2)}, u32[]{:S(2)}) collective-permute-start(f32[3,64,128]{2,1,0:T(8,128)S(1)} %get-tuple-element.50), channel_id=1, source_target_pairs={{1,2},{3,4},{5,6},{7,8},{9,10},{11,12},{13,14},{2,1},{4,3},{6,5},{... | collective-permute-start | bytes 294920 | tf_op jit(solution)/shard_map/ppermute | solution.py:688
  51.9 4.8 %collective-permute-start.6 = (f32[128,4,128]{2,1,0:T(4,128)S(1)}, f32[128,4,128]{2,1,0:T(4,128)S(1)}, u32[]{:S(2)}, u32[]{:S(2)}) collective-permute-start(f32[128,4,128]{2,1,0:T(4,128)S(1)} %all_to_all.5), channel_id=1, source_target_pairs={{0,16},{16,0},{1,17},{17,1},{2,18},{18,2},{3,19},{19,3},{4,20},{20... | collective-permute-start | bytes 786440 | tf_op jit(solution)/shard_map/ppermute | solution.py:704

commit v9 on v8

--- a/solution.py
+++ b/solution.py
@@ -35,7 +35,11 @@
 
 def times(x, pattern):
     high, low = split(x)
-    return dot(high, pattern) + dot(low, pattern)
+    count = x.shape[0]
+    if count % 16:
+        return dot(high, pattern) + dot(low, pattern)
+    both = dot(jnp.concatenate([high, low], axis=0), pattern)
+    return both[:count] + both[count:]
 
 
 def pick(pattern, x):

time: 63.7 us -> 63.5 us (level)
  no operation moved by 1% of the time
where the time goes in v9:
time: 63.5 us; the launch traced here: 63.3 us
  blocking collectives  30.9 us (49%)
  Pallas kernels  12.9 us (20%)
  starting transfers between devices  11.5 us (18%)
  waiting for transfers between devices  5.01 us (8%)
  other arithmetic  1.72 us (3%)
  local copies, waits for them, and re-layouts  1.04 us (2%)
    all_to_all x1, blocking collectives, local(): mine = lax.all_to_all(message.reshape(128, 4, 128), ('z', 'col'), 0, 0)  30.9 us
    ppermute x6, starting transfers between devices, swap(): return lax.ppermute(x, axis, pairs + [(j, i) for i, j in pairs])  7.88 us
    pallas_call x1, Pallas kernels, up(): pl.pallas_call(up_kernel, out_shape=shaped(2, 256, 256), in_specs=[VMEM]...  6.56 us
    pallas_call x1, Pallas kernels, down(): pl.pallas_call(down_kernel, out_shape=[shaped(*s) for s in state_shapes()...  4.41 us
    ppermute x6, waiting for transfers between devices, swap(): return lax.ppermute(x, axis, pairs + [(j, i) for i, j in pairs])  3.85 us
    ppermute x1, starting transfers between devices, local(): theirs = lax.ppermute(mine, 'core', [(0, 1), (1, 0)])  3.61 us
    pallas_call x1, Pallas kernels, middle(): pl.pallas_call(middle_kernel, out_shape=[shaped(4, 24, 8, 256)] * 2 + [ja...  1.64 us
  transfers between devices with their start and end apart: 7, of which 3 were waited for; matrix products, arithmetic and copies ran while one was open for 1% of the time, Pallas kernels for 3%

profile of v9, /device:TPU:1, one launch (start us, length us, event | category | flops | bytes accessed | tf_op | source)
XLA Modules:
  0.0 63.3 jit_solution(17092517541968647593)
XLA Ops:
  0.0 1.0 %add_convert_fusion.classes = f32[256,256]{1,0:T(8,128)S(1)} fusion(s32[256,256]{1,0:T(8,128)} %param.5), kind=kLoop, calls=%fused_computation | loop fusion | flops 131072 | bytes 524288 | tf_op jit(solution)/shard_map/convert_element_type | solution.py:696
  1.0 0.0 copy-start
  1.0 1.0 %copy-done = f32[2,256,256]{2,1,0:T(8,128)S(1)} copy-done((f32[2,256,256]{2,1,0:T(8,128)S(1)}, f32[2,256,256]{2,1,0:T(8,128)}, u32[]{:S(2)}) %copy-start) | copy-done | bytes 524312
  2.0 0.2 sides.1
  2.2 3.3 %collective-permute-start = (f32[3,64,256]{2,1,0:T(8,128)S(1)}, f32[3,64,256]{2,1,0:T(8,128)S(1)}, u32[]{:S(2)}, u32[]{:S(2)}) collective-permute-start(f32[3,64,256]{2,1,0:T(8,128)S(1)} %get-tuple-element.32), channel_id=1, source_target_pairs={{0,16},{32,48},{64,80},{96,112},{128,144},{160,176},{192,208},{224... | collective-permute-start | bytes 589832 | tf_op jit(solution)/shard_map/ppermute | solution.py:692
  5.5 1.9 %collective-permute-start.1 = (f32[3,64,256]{2,1,0:T(8,128)S(1)}, f32[3,64,256]{2,1,0:T(8,128)S(1)}, u32[]{:S(2)}, u32[]{:S(2)}) collective-permute-start(f32[3,64,256]{2,1,0:T(8,128)S(1)} %get-tuple-element.33), channel_id=1, source_target_pairs={{16,32},{48,64},{80,96},{112,128},{144,160},{176,192},{208,224},{3... | collective-permute-start | bytes 589832 | tf_op jit(solution)/shard_map/ppermute | solution.py:692
  7.4 1.2 %collective-permute-start.2 = (f32[3,128,128]{2,1,0:T(8,128)S(1)}, f32[3,128,128]{2,1,0:T(8,128)S(1)}, u32[]{:S(2)}, u32[]{:S(2)}) collective-permute-start(f32[3,128,128]{2,1,0:T(8,128)S(1)} %get-tuple-element.47), channel_id=1, source_target_pairs={{0,1},{2,3},{4,5},{6,7},{8,9},{10,11},{12,13},{14,15},{1,0},{3,2},... | collective-permute-start | bytes 589832 | tf_op jit(solution)/shard_map/ppermute | solution.py:692
  8.6 0.7 %collective-permute-start.3 = (f32[3,128,128]{2,1,0:T(8,128)S(1)}, f32[3,128,128]{2,1,0:T(8,128)S(1)}, u32[]{:S(2)}, u32[]{:S(2)}) collective-permute-start(f32[3,128,128]{2,1,0:T(8,128)S(1)} %get-tuple-element.48), channel_id=1, source_target_pairs={{1,2},{3,4},{5,6},{7,8},{9,10},{11,12},{13,14},{2,1},{4,3},{6,5},{... | collective-permute-start | bytes 589832 | tf_op jit(solution)/shard_map/ppermute | solution.py:692
  9.3 0.0 collective-permute-done.row_a
  9.3 3.5 %collective-permute-done.1.row_b = f32[3,64,256]{2,1,0:T(8,128)S(1)} collective-permute-done((f32[3,64,256]{2,1,0:T(8,128)S(1)}, f32[3,64,256]{2,1,0:T(8,128)S(1)}, u32[]{:S(2)}, u32[]{:S(2)}) %collective-permute-start.1) | collective-permute-done | bytes 196640 | tf_op jit(solution)/shard_map/ppermute | solution.py:692
  12.8 0.1 corners.1
  12.9 0.1 collective-permute-start.4
  13.1 0.7 %collective-permute-start.5 = (f32[3,64,128]{2,1,0:T(8,128)S(1)}, f32[3,64,128]{2,1,0:T(8,128)S(1)}, u32[]{:S(2)}, u32[]{:S(2)}) collective-permute-start(f32[3,64,128]{2,1,0:T(8,128)S(1)} %get-tuple-element.50), channel_id=1, source_target_pairs={{1,2},{3,4},{5,6},{7,8},{9,10},{11,12},{13,14},{2,1},{4,3},{6,5},{... | collective-permute-start | bytes 294920 | tf_op jit(solution)/shard_map/ppermute | solution.py:692
  13.7 0.7 %pad_maximum_fusion.table = f32[16]{0:T(128)S(1)} fusion(f32[8]{0:T(128)} %param.7, f32[8]{0:T(128)} %param.6), kind=kLoop, calls=%fused_computation.1 | loop fusion | flops 16 | bytes 128 | tf_op jit(solution)/shard_map/concatenate | solution.py:703
  14.5 1.6 %middle.1 = (f32[4,24,8,256]{3,2,1,0:T(8,128)S(1)}, f32[4,24,8,256]{3,2,1,0:T(8,128)S(1)}, bf16[17,128,128]{2,1,0:T(8,128)(2,1)S(1)}, bf16[384,256]{1,0:T(8,128)...) custom-call(f32[3,256,256]{2,1,0:T(8,128)S(1)} %get-tuple-element.37.own, ...), custom_call_target="tpu_custom_call" | custom-call | tf_op jit(solution)/shard_map/middle/pallas_call | solution.py:634
  16.1 0.0 collective-permute-done.2.col_a
  16.1 0.0 collective-permute-done.3.col_b
  16.1 0.3 collective-permute-done.4.corner_a
  16.5 0.0 collective-permute-done.5.corner_b
  16.5 4.4 %down.1 = (f32[13,26,8,384]{3,2,1,0:T(8,128)S(1)}, f32[13,14,8,256]{3,2,1,0:T(8,128)S(1)}, f32[13,8,8,128]{3,2,1,0:T(8,128)S(1)}, f32[13,5,8,128]{3,2,1,0:T(8,12...) custom-call(f32[4,24,8,256]{3,2,1,0:T(8,128)S(1)} %get-tuple-element.42.rhs0, ...), custom_call_target="tpu_custom_call" | custom-call | tf_op jit(solution)/shard_map/down/pallas_call | solution.py:646
  20.9 30.9 %all_to_all.5 = f32[128,4,128]{2,1,0:T(4,128)S(1)} all-to-all(f32[128,4,128]{2,1,0:T(4,128)S(1)} %bitcast.5), channel_id=1, replica_groups=mesh['z'=8,'core'=2,'col'=16] {'z','col'}, dimensions={0} | all-to-all | bytes 524288 | tf_op jit(solution)/shard_map/all_to_all | solution.py:707
  51.8 3.6 %collective-permute-start.6 = (f32[128,4,128]{2,1,0:T(4,128)S(1)}, f32[128,4,128]{2,1,0:T(4,128)S(1)}, u32[]{:S(2)}, u32[]{:S(2)}) collective-permute-start(f32[128,4,128]{2,1,0:T(4,128)S(1)} %all_to_all.5), channel_id=1, source_target_pairs={{0,16},{16,0},{1,17},{17,1},{2,18},{18,2},{3,19},{19,3},{4,20},{20... | collective-permute-start | bytes 786440 | tf_op jit(solution)/shard_map/ppermute | solution.py:708
  55.4 1.2 %collective-permute-done.6 = f32[128,4,128]{2,1,0:T(4,128)S(1)} collective-permute-done((f32[128,4,128]{2,1,0:T(4,128)S(1)}, f32[128,4,128]{2,1,0:T(4,128)S(1)}, u32[]{:S(2)}, u32[]{:S(2)}) %collective-permute-start.6) | collective-permute-done | bytes 262176 | tf_op jit(solution)/shard_map/ppermute | solution.py:708
  56.5 6.6 %up.1 = f32[2,256,256]{2,1,0:T(8,128)} custom-call(f32[512,128]{1,0:T(8,128)S(1)} %bitcast.3, f32[512,128]{1,0:T(8,128)S(1)} %bitcast.4, bf16[17,128,128]{2,1,0:T(8,128)(2,1)S(1)} %get-tuple-element.44.small, bf16[128,256]{1,0:T(8,128)(2,1)S(1)} %get-tuple-element.52.up1, bf16[256,384]{1,0:T(8,128)(2,1)S(1)} %get-tuple-element.53.up0, ...), custom_call_target="tpu_custom_call" | custom-call | tf_op jit(solution)/shard_map/up/pallas_call | solution.py:665
Async XLA Ops:
  1.0 1.0 %copy-start = (f32[2,256,256]{2,1,0:T(8,128)S(1)}, f32[2,256,256]{2,1,0:T(8,128)}, u32[]{:S(2)}) copy-start(f32[2,256,256]{2,1,0:T(8,128)} %observed.1) | copy-start | bytes 1572868
  2.2 7.1 %collective-permute-start = (f32[3,64,256]{2,1,0:T(8,128)S(1)}, f32[3,64,256]{2,1,0:T(8,128)S(1)}, u32[]{:S(2)}, u32[]{:S(2)}) collective-permute-start(f32[3,64,256]{2,1,0:T(8,128)S(1)} %get-tuple-element.32), channel_id=1, source_target_pairs={{0,16},{32,48},{64,80},{96,112},{128,144},{160,176},{192,208},{224... | collective-permute-start | bytes 589832 | tf_op jit(solution)/shard_map/ppermute | solution.py:692
  5.5 7.3 %collective-permute-start.1 = (f32[3,64,256]{2,1,0:T(8,128)S(1)}, f32[3,64,256]{2,1,0:T(8,128)S(1)}, u32[]{:S(2)}, u32[]{:S(2)}) collective-permute-start(f32[3,64,256]{2,1,0:T(8,128)S(1)} %get-tuple-element.33), channel_id=1, source_target_pairs={{16,32},{48,64},{80,96},{112,128},{144,160},{176,192},{208,224},{3... | collective-permute-start | bytes 589832 | tf_op jit(solution)/shard_map/ppermute | solution.py:692
  7.4 8.7 %collective-permute-start.2 = (f32[3,128,128]{2,1,0:T(8,128)S(1)}, f32[3,128,128]{2,1,0:T(8,128)S(1)}, u32[]{:S(2)}, u32[]{:S(2)}) collective-permute-start(f32[3,128,128]{2,1,0:T(8,128)S(1)} %get-tuple-element.47), channel_id=1, source_target_pairs={{0,1},{2,3},{4,5},{6,7},{8,9},{10,11},{12,13},{14,15},{1,0},{3,2},... | collective-permute-start | bytes 589832 | tf_op jit(solution)/shard_map/ppermute | solution.py:692
  8.6 7.5 %collective-permute-start.3 = (f32[3,128,128]{2,1,0:T(8,128)S(1)}, f32[3,128,128]{2,1,0:T(8,128)S(1)}, u32[]{:S(2)}, u32[]{:S(2)}) collective-permute-start(f32[3,128,128]{2,1,0:T(8,128)S(1)} %get-tuple-element.48), channel_id=1, source_target_pairs={{1,2},{3,4},{5,6},{7,8},{9,10},{11,12},{13,14},{2,1},{4,3},{6,5},{... | collective-permute-start | bytes 589832 | tf_op jit(solution)/shard_map/ppermute | solution.py:692
  12.9 3.6 %collective-permute-start.4 = (f32[3,64,128]{2,1,0:T(8,128)S(1)}, f32[3,64,128]{2,1,0:T(8,128)S(1)}, u32[]{:S(2)}, u32[]{:S(2)}) collective-permute-start(f32[3,64,128]{2,1,0:T(8,128)S(1)} %get-tuple-element.49), channel_id=1, source_target_pairs={{0,1},{2,3},{4,5},{6,7},{8,9},{10,11},{12,13},{14,15},{1,0},{3,2},... | collective-permute-start | bytes 294920 | tf_op jit(solution)/shard_map/ppermute | solution.py:692
  13.1 3.4 %collective-permute-start.5 = (f32[3,64,128]{2,1,0:T(8,128)S(1)}, f32[3,64,128]{2,1,0:T(8,128)S(1)}, u32[]{:S(2)}, u32[]{:S(2)}) collective-permute-start(f32[3,64,128]{2,1,0:T(8,128)S(1)} %get-tuple-element.50), channel_id=1, source_target_pairs={{1,2},{3,4},{5,6},{7,8},{9,10},{11,12},{13,14},{2,1},{4,3},{6,5},{... | collective-permute-start | bytes 294920 | tf_op jit(solution)/shard_map/ppermute | solution.py:692
  51.8 4.8 %collective-permute-start.6 = (f32[128,4,128]{2,1,0:T(4,128)S(1)}, f32[128,4,128]{2,1,0:T(4,128)S(1)}, u32[]{:S(2)}, u32[]{:S(2)}) collective-permute-start(f32[128,4,128]{2,1,0:T(4,128)S(1)} %all_to_all.5), channel_id=1, source_target_pairs={{0,16},{16,0},{1,17},{17,1},{2,18},{18,2},{3,19},{19,3},{4,20},{20... | collective-permute-start | bytes 786440 | tf_op jit(solution)/shard_map/ppermute | solution.py:708
